TPU v7x, 512 devices: a whole 4x4x16 slice. The times are simulated.
512 devices in a mesh: occ: 32 (over z_lo, x, core), vir: 16 (over y, z_hi).
Axes of the slice: x: 4, y: 4, z: 16 (z_hi: 4, z_lo: 4; z = z_hi * 4 + z_lo), core: 2. Of those that a mesh axis runs over, the one named last changes fastest.
Arguments:
- amplitudes: float32 [4864, 2560], P('occ', 'vir'), may hold values from -6 to 6
- integrals: float32 [2560, 16384], P('occ', 'vir'), may hold values from -0.125 to 0.125
- pair_list: int32 [4864, 2], P('occ'), may hold values from 0 to 99, as said below
- partner: int32 [2560], replicated, may hold values from 0 to 2559, as said below
Outputs:
- ladder: float32 [4864, 16384], P('occ', 'vir')
Inputs may be any that keep to these rules, and one draw needn't show every extreme that they name: `pair_list`: the rows are distinct pairs with i <= j, a subset of all pairs of 100 occupied orbitals; some rows have i == j. partner[partner[k]] == k and partner[k] != k for every slot k.
All inputs are finite; a program needn't handle non-finite values.
Results may differ from a plain program's by a relative error of at most 0.00007.
Values sent between devices are 32-bit elements; how exact they have to be, the bound alone decides.
No kernel may reach another device: no remote copies, remote signals or barrier semaphores. Data moves between devices by JAX's collectives and lax.ppermute only.
A program may use at most 64 MiB of HBM per device.

v0:
```python
import jax
import jax.numpy as jnp
from jax import lax
from jax.sharding import PartitionSpec as P

NA = 128


def body(amplitudes, integrals, pair_list, partner):
    pair_rows = amplitudes.shape[0]
    columns_here = integrals.shape[1]
    rows_here = columns_here // NA
    gathered = lax.all_gather(amplitudes, "vir", axis=1, tiled=True)
    antisym = gathered - jnp.take(gathered, partner, axis=1)
    direct = jnp.dot(
        antisym,
        lax.all_gather(integrals, "occ", axis=0, tiled=True),
        precision=lax.Precision.HIGHEST,
        preferred_element_type=jnp.float32,
    )
    blocks = direct.reshape(pair_rows, rows_here, NA)
    swapped = lax.all_to_all(blocks, "vir", split_axis=2, concat_axis=1, tiled=True)
    direct = direct + jnp.swapaxes(swapped, 1, 2).reshape(direct.shape)
    weight = jnp.where(pair_list[:, 0] == pair_list[:, 1], 0.5, 1.0).astype(jnp.float32)
    return weight[:, None] * direct


def solution(mesh):
    placed = (P("occ", "vir"), P("occ", "vir"), P("occ", None), P())
    return jax.shard_map(
        body, mesh=mesh, in_specs=placed, out_specs=P("occ", "vir"), check_vma=False
    )
```

profile of v0, /device:TPU:1, one launch (start us, length us, event | category | flops | bytes accessed | tf_op | source)
XLA Modules:
  0.0 280.9 jit_solution(8765773242449853521)
XLA Ops:
  6.5 0.0 all-gather.6.cloned.1.call-start
  6.5 0.7 all-gather.6.cloned.1.call-update
  7.3 0.0 all-gather.4.cloned.1.call-start
  7.3 0.7 all-gather.4.cloned.1.call-update
  8.0 0.7 compare_select_fusion
  8.7 0.7 compare_and_fusion
  9.4 110.6 %all-gather.6.cloned.1.call-done = f32[16,160,152]{1,2,0:T(8,128)} async-done(((f32[1,160,152]{1,2,0:T(8,128)}), f32[16,160,152]{1,2,0:T(8,128)}) %all-gather.6.cloned.1.call-update) | async-done | bytes 1556496 | tf_op jit(solution)/shard_map/all_gather | solution.py:13
  120.1 2.5 copy.11
  122.6 7.0 %gather_fusion = f32[2560,152]{1,0:T(8,128)} fusion(f32[152,2560]{0,1:T(8,128)S(1)} %bitcast.24, s32[3072]{0:T(1024)S(1)} %pad_clamp_fusion), kind=kCustom, calls=%fused_computation | custom fusion | bytes 3123200 | tf_op jit(solution)/shard_map/jit(_take)/gather | solution.py:14
  129.6 66.6 %all-gather.4.cloned.1.call-done = f32[2560,1024]{1,0:T(8,128)} async-done(((f32[80,1024]{1,0:T(8,128)}), f32[2560,1024]{1,0:T(8,128)}) %all-gather.4.cloned.1.call-update) | async-done | bytes 10485776 | tf_op jit(solution)/shard_map/all_gather | solution.py:17
  196.2 11.7 %fusion = f32[152,1024]{1,0:T(8,128)S(1)} fusion(f32[2560,1024]{1,0:T(8,128)} %all-gather.4.cloned.1.call-done, f32[152,2560]{0,1:T(8,128)S(1)} %bitcast.25, f32[2560,152]{1,0:T(8,128)} %gather_fusion, pred[2560]{0:T(1024)(128)(4,1)S(1)} %compare_and_fusion), kind=kOutput, calls=%fused_computation.2 | convolution fusion | flops 4782284800 | bytes 14223872 | tf_op jit(solution)/shard_map/dot_general | solution.py:15
  207.9 0.0 copy-start
  207.9 0.1 copy.17
  208.1 1.4 copy.12
  209.5 13.1 %all-to-all-start = ((f32[152,8,128]{0,1,2:T(8,128)}), f32[152,8,128]{0,1,2:T(8,128)S(1)}, u32[]{:S(2)}, u32[]{:S(2)}) async-start(f32[152,8,128]{0,1,2:T(8,128)} %copy.12), calls=%async_computation | async-start | bytes 2097152 | tf_op jit(solution)/shard_map/all_to_all | solution.py:22
  222.6 0.0 copy-done
  222.6 49.6 %all-to-all-done = f32[152,8,128]{0,1,2:T(8,128)S(1)} async-done(((f32[152,8,128]{0,1,2:T(8,128)}), f32[152,8,128]{0,1,2:T(8,128)S(1)}, u32[]{:S(2)}, u32[]{:S(2)}) %all-to-all-start) | async-done | bytes 622624 | tf_op jit(solution)/shard_map/all_to_all | solution.py:22
  272.2 0.3 copy.14
  272.6 0.5 copy.15
  273.1 1.0 fusion.4
  (2 shorter events, 0.0 us)
Async XLA Ops:
  6.5 113.6 %all-gather.6.cloned.1.call-start = ((), (), s32[]{:S(2)}) async-start(), calls=%async_computation.2 | async-start | bytes 2646016 | tf_op jit(solution)/shard_map/all_gather | solution.py:13
  7.3 189.0 %all-gather.4.cloned.1.call-start = ((), (), s32[]{:S(2)}) async-start(), calls=%async_computation.1 | async-start | bytes 10813440 | tf_op jit(solution)/shard_map/all_gather | solution.py:17
  207.9 14.7 %copy-start = (s32[152,2]{0,1:T(2,128)S(1)}, s32[152,2]{0,1:T(2,128)}, u32[]{:S(2)}) copy-start(s32[152,2]{0,1:T(2,128)} %param.6) | copy-start | bytes 3652
  209.5 62.7 %all-to-all-start = ((f32[152,8,128]{0,1,2:T(8,128)}), f32[152,8,128]{0,1,2:T(8,128)S(1)}, u32[]{:S(2)}, u32[]{:S(2)}) async-start(f32[152,8,128]{0,1,2:T(8,128)} %copy.12), calls=%async_computation | async-start | bytes 2097152 | tf_op jit(solution)/shard_map/all_to_all | solution.py:22
Sparse Core Ops, SparseCore 0:
  10.4 109.6 all-gather.5
  122.2 73.9 all-gather.3
where the time goes:
time: 286 us; the launch traced here: 281 us
  waiting for transfers between devices  228 us (80%)
  between operations  13.5 us (5%)
  starting transfers between devices  13.1 us (5%)
  local copies, waits for them, and re-layouts  11.9 us (4%)
  matrix products  11.7 us (4%)
    all_gather x1, waiting for transfers between devices, body(): gathered = lax.all_gather(amplitudes, 'vir', axis=1, tiled=True)  111 us
    all_gather x1, waiting for transfers between devices, body(): lax.all_gather(integrals, 'occ', axis=0, tiled=True)  66.6 us
    all_to_all x1, waiting for transfers between devices, body(): lax.all_to_all(blocks, 'vir', split_axis=2, concat_axis=1, tiled=True)  49.6 us
    all_to_all x1, starting transfers between devices, body(): lax.all_to_all(blocks, 'vir', split_axis=2, concat_axis=1, tiled=True)  13.1 us
    dot_general x1, matrix products, body(): jnp.dot(antisym, lax.all_gather(integrals, 'occ', axis=0, tiled=True), pr...  11.7 us
    gather x1, local copies, waits for them, and re-layouts, body(): antisym = gathered - jnp.take(gathered, partner, axis=1)  7.05 us
  transfers between devices with their start and end apart: 3, of which 3 were waited for; matrix products, arithmetic and copies ran while one was open for 4% of the time, Pallas kernels for 0%

commit v1 on v0

v1 whole, which is shorter than its diff:
```python
import jax
import jax.numpy as jnp
from jax import lax
from jax.sharding import Mesh, PartitionSpec as P

NA = 128
VIR = ("y", "zh")
OCC = ("zl", "x", "c")
RING = (0, 1, 3, 2)
SLOT = (0, 2, 3, 1)


def shift(n, by):
    return [(i, (i + by) % n) for i in range(n)]


def both_ways(block, axis):
    half = block.shape[0] // 2
    left = lax.ppermute(block, axis, shift(4, 1))
    right = lax.ppermute(block, axis, shift(4, -1))
    far_top = lax.ppermute(left[:half], axis, shift(4, 1))
    far_low = lax.ppermute(right[half:], axis, shift(4, -1))
    return [block, left, right, far_top, far_low]


def symmetrized(integrals):
    rows = integrals.shape[0]
    here = integrals.shape[1] // NA
    ranks = NA // here
    sent = integrals.reshape(rows, here, ranks, here).transpose(2, 1, 3, 0).reshape(ranks, here, here * rows)
    got = lax.all_to_all(sent, VIR, split_axis=0, concat_axis=0, tiled=True)
    swapped = got.reshape(NA, here * rows).T.reshape(here, rows, NA)
    return integrals + swapped.transpose(1, 0, 2).reshape(integrals.shape)


def body(amplitudes, integrals, pair_list, partner):
    rows_k = integrals.shape[0]
    x, core = lax.axis_index("x"), lax.axis_index("c")
    y, zh = lax.axis_index("y"), lax.axis_index("zh")
    ring_place = jnp.array([0, 1, 3, 2], jnp.int32)[lax.axis_index("zl")]

    blocks = [symmetrized(integrals)]
    for _ in range(3):
        blocks.append(lax.ppermute(blocks[-1], "zl", [(RING[i], RING[(i + 1) % 4]) for i in range(4)]))
    slabs = [jnp.concatenate(both_ways(b, "x"), axis=0) for b in blocks]

    columns_k = amplitudes.shape[1]
    by_zh = jnp.concatenate(both_ways(amplitudes.T, "zh"), axis=0)
    tau = jnp.concatenate(both_ways(by_zh, "y"), axis=0)

    ring = jnp.array(RING, jnp.int32)
    zs = ring[(ring_place - jnp.arange(4)) % 4]
    xs = (x + jnp.array([0, -1, 1, 2])) % 4
    chunk = (zs[:, None] * 4 + xs[None, :]).reshape(16) * 2
    chunk = jnp.concatenate([chunk + core, chunk + 1 - core])
    slot = jnp.array(SLOT, jnp.int32)

    def place(k):
        rank = k // columns_k
        return (slot[(rank // 4 - y) % 4] * 4 + slot[(rank % 4 - zh) % 4]) * columns_k + k % columns_k

    own = (chunk[:, None] * rows_k + jnp.arange(rows_k)[None, :]).reshape(-1)
    other = partner.reshape(-1, rows_k).at[chunk].get(mode="promise_in_bounds").reshape(-1)
    antisym = tau.at[place(own)].get(mode="promise_in_bounds") - tau.at[place(other)].get(mode="promise_in_bounds")
    half = antisym.shape[0] // 2
    mine = antisym[:half]
    theirs = lax.ppermute(antisym[half:], "c", shift(2, 1))

    def product(lhs):
        return lax.dot_general(
            lhs, jnp.concatenate(slabs, axis=0), (((0,), (0,)), ((), ())),
            precision=lax.Precision.HIGH, preferred_element_type=jnp.float32,
        )

    back = lax.ppermute(product(theirs), "c", shift(2, 1))
    weight = jnp.where(pair_list[:, 0] == pair_list[:, 1], 0.5, 1.0).astype(jnp.float32)
    return weight[:, None] * (product(mine) + back)


def solution(mesh):
    fine = Mesh(mesh.devices.reshape(4, 4, 2, 4, 4), OCC + VIR)
    placed = (P(OCC, VIR), P(OCC, VIR), P(OCC, None), P())
    return jax.shard_map(
        body, mesh=fine, in_specs=placed, out_specs=P(OCC, VIR), check_vma=False
    )
```

time: 286 us -> 215 us (0.75)
  the two profiles are of different devices: /device:TPU:1 before, /device:TPU:39 now
where the time goes in v1:
time: 215 us; the launch traced here: 213 us
  starting transfers between devices  121 us (56%)
  local copies, waits for them, and re-layouts  57.3 us (27%)
  waiting for transfers between devices  19.9 us (9%)
  matrix products  7.2 us (3%)
  other arithmetic  7.17 us (3%)
    ppermute x6, starting transfers between devices, both_ways(): left = lax.ppermute(block, axis, shift(4, 1))  27.3 us
    ppermute x6, starting transfers between devices, both_ways(): far_top = lax.ppermute(left[:half], axis, shift(4, 1))  26.1 us
    unnamed x33, local copies, waits for them, and re-layouts  22.3 us
    ppermute x6, starting transfers between devices, both_ways(): right = lax.ppermute(block, axis, shift(4, -1))  17.2 us
    ppermute x6, starting transfers between devices, both_ways(): far_low = lax.ppermute(right[half:], axis, shift(4, -1))  14.3 us
    ppermute x6, waiting for transfers between devices, both_ways(): far_low = lax.ppermute(right[half:], axis, shift(4, -1))  12.8 us
    all_to_all x1, starting transfers between devices, symmetrized(): got = lax.all_to_all(sent, VIR, split_axis=0, concat_axis=0, tiled=True)  12.4 us
    ppermute x3, starting transfers between devices, body(): lax.ppermute(blocks[-1], 'zl', [(RING[i], RING[(i + 1) % 4]) for i in ran...  10.8 us
  transfers between devices with their start and end apart: 30, of which 5 were waited for; matrix products, arithmetic and copies ran while one was open for 30% of the time, Pallas kernels for 0%

profile of v1, /device:TPU:39, one launch (start us, length us, event | category | flops | bytes accessed | tf_op | source)
XLA Modules:
  0.0 213.3 jit_solution(17244894347769887543)
XLA Ops:
  1.0 8.8 %collective-permute-start = (f32[160,152]{1,0:T(8,128)S(1)}, f32[160,152]{1,0:T(8,128)}, u32[]{:S(2)}, u32[]{:S(2)}) collective-permute-start(f32[160,152]{1,0:T(8,128)S(1)} %bitcast.31), channel_id=1, source_target_pairs={{0,1},{1,2},{2,3},{3,0},{4,5},{5,6},{6,7},{7,4},{8,9},{9,10},{10,1... | collective-permute-start | bytes 291848 | tf_op jit(solution)/shard_map/ppermute | solution.py:19
  9.8 4.7 %collective-permute-start.1 = (f32[160,152]{1,0:T(8,128)S(1)}, f32[160,152]{1,0:T(8,128)}, u32[]{:S(2)}, u32[]{:S(2)}) collective-permute-start(f32[160,152]{1,0:T(8,128)S(1)} %bitcast.32), channel_id=1, source_target_pairs={{0,3},{1,0},{2,1},{3,2},{4,7},{5,4},{6,5},{7,6},{8,11},{9,8},{10,9... | collective-permute-start | bytes 291848 | tf_op jit(solution)/shard_map/ppermute | solution.py:20
  16.7 12.4 %all-to-all-start = ((f32[16,8,640]{2,1,0:T(8,128)}), f32[16,8,640]{2,1,0:T(8,128)}, u32[]{:S(2)}, u32[]{:S(2)}) async-start(f32[16,8,640]{2,1,0:T(8,128)} %copy.31), calls=%async_computation | async-start | bytes 655360 | tf_op jit(solution)/shard_map/all_to_all | solution.py:31
  36.7 7.1 %collective-permute-start.2 = (f32[80,152]{1,0:T(8,128)S(1)}, f32[80,152]{1,0:T(8,128)S(1)}, u32[]{:S(2)}, u32[]{:S(2)}) collective-permute-start(f32[80,152]{1,0:T(8,128)S(1)} %slice.92), channel_id=1, source_target_pairs={{0,1},{1,2},{2,3},{3,0},{4,5},{5,6},{6,7},{7,4},{8,9},{9,10},{10,1... | collective-permute-start | bytes 145928 | tf_op jit(solution)/shard_map/ppermute | solution.py:21
  48.7 9.7 %collective-permute-done.3 = f32[80,152]{1,0:T(8,128)S(1)} collective-permute-done((f32[80,152]{1,0:T(8,128)S(1)}, f32[80,152]{1,0:T(8,128)S(1)}, u32[]{:S(2)}, u32[]{:S(2)}) %collective-permute-start.3) | collective-permute-done | bytes 48672 | tf_op jit(solution)/shard_map/ppermute | solution.py:22
  59.4 2.9 %collective-permute-start.4 = (f32[640,152]{0,1:T(8,128)}, f32[640,152]{0,1:T(8,128)}, u32[]{:S(2)}, u32[]{:S(2)}) collective-permute-start(f32[640,152]{0,1:T(8,128)} %copy.20), channel_id=1, source_target_pairs={{0,4},{4,8},{8,12},{12,0},{1,5},{5,9},{9,13},{13,1},{2,6},{6,10},{... | collective-permute-start | bytes 1167368 | tf_op jit(solution)/shard_map/ppermute | solution.py:19
  62.3 3.6 %collective-permute-start.5 = (f32[640,152]{0,1:T(8,128)}, f32[640,152]{0,1:T(8,128)}, u32[]{:S(2)}, u32[]{:S(2)}) collective-permute-start(f32[640,152]{0,1:T(8,128)} %copy.20), channel_id=1, source_target_pairs={{0,12},{4,0},{8,4},{12,8},{1,13},{5,1},{9,5},{13,9},{2,14},{6,2},{... | collective-permute-start | bytes 1167368 | tf_op jit(solution)/shard_map/ppermute | solution.py:20
  66.4 5.1 %collective-permute-done.4 = f32[640,152]{0,1:T(8,128)} collective-permute-done((f32[640,152]{0,1:T(8,128)}, f32[640,152]{0,1:T(8,128)}, u32[]{:S(2)}, u32[]{:S(2)}) %collective-permute-start.4) | collective-permute-done | bytes 389152 | tf_op jit(solution)/shard_map/ppermute | solution.py:19
  77.5 4.6 %collective-permute-start.7 = (f32[320,152]{1,0:T(8,128)}, f32[320,152]{1,0:T(8,128)}, u32[]{:S(2)}, u32[]{:S(2)}) collective-permute-start(f32[320,152]{1,0:T(8,128)} %slice.95), channel_id=1, source_target_pairs={{0,12},{4,0},{8,4},{12,8},{1,13},{5,1},{9,5},{13,9},{2,14},{6,2},{... | collective-permute-start | bytes 583688 | tf_op jit(solution)/shard_map/ppermute | solution.py:22
  89.2 3.2 %collective-permute-start.9 = (f32[80,1024]{1,0:T(8,128)}, f32[80,1024]{1,0:T(8,128)}, u32[]{:S(2)}, u32[]{:S(2)}) collective-permute-start(f32[80,1024]{1,0:T(8,128)} %get-tuple-element.6), channel_id=1, source_target_pairs={{0,96},{32,0},{64,32},{96,64},{1,97},{33,1},{65,33},{97,65},{2,98}... | collective-permute-start | bytes 983048 | tf_op jit(solution)/shard_map/ppermute | solution.py:20
  96.4 7.1 %gather_fusion.3 = f32[2560,152]{1,0:T(8,128)} fusion(f32[2560,152]{1,0:T(8,128)S(1)} %constant_dynamic-update-slice_fusion.5, s32[3072]{0:T(1024)S(1)} %get-tuple-element.23), kind=kCustom, calls=%fused_computation.3 | custom fusion | bytes 3123200 | tf_op jit(solution)/shard_map/gather | solution.py:64
  103.4 7.1 %gather_fusion.1 = f32[2560,152]{1,0:T(8,128)} fusion(f32[2560,152]{1,0:T(8,128)S(1)} %constant_dynamic-update-slice_fusion.5, s32[3072]{0:T(1024)S(1)} %get-tuple-element.24), kind=kCustom, calls=%fused_computation.1 | custom fusion | bytes 3123200 | tf_op jit(solution)/shard_map/gather | solution.py:64
  116.2 5.7 %collective-permute-start.27 = (f32[1280,152]{0,1:T(8,128)S(1)}, f32[1280,152]{0,1:T(8,128)S(1)}, u32[]{:S(2)}, u32[]{:S(2)}) collective-permute-start(f32[1280,152]{0,1:T(8,128)S(1)} %copy.30), channel_id=1, source_target_pairs={{0,16},{16,0},{1,17},{17,1},{2,18},{18,2},{3,19},{19,3},{4,20},{20... | collective-permute-start | bytes 2334728 | tf_op jit(solution)/shard_map/ppermute | solution.py:67
  122.9 3.3 %collective-permute-start.10 = (f32[40,1024]{1,0:T(8,128)S(1)}, f32[40,1024]{1,0:T(8,128)S(1)}, u32[]{:S(2)}, u32[]{:S(2)}) collective-permute-start(f32[40,1024]{1,0:T(8,128)S(1)} %slice.97), channel_id=1, source_target_pairs={{0,32},{32,64},{64,96},{96,0},{1,33},{33,65},{65,97},{97,1},{2,34}... | collective-permute-start | bytes 491528 | tf_op jit(solution)/shard_map/ppermute | solution.py:21
  129.2 4.5 %collective-permute-start.13 = (f32[80,1024]{1,0:T(8,128)}, f32[80,1024]{1,0:T(8,128)S(1)}, u32[]{:S(2)}, u32[]{:S(2)}) collective-permute-start(f32[80,1024]{1,0:T(8,128)} %collective-permute-done.12), channel_id=1, source_target_pairs={{0,32},{32,64},{64,96},{96,0},{1,33},{33,65},{65,97},{97,1},{2,34}... | collective-permute-start | bytes 983048 | tf_op jit(solution)/shard_map/ppermute | solution.py:19
  144.1 4.6 %collective-permute-start.15 = (f32[40,1024]{1,0:T(8,128)S(1)}, f32[40,1024]{1,0:T(8,128)S(1)}, u32[]{:S(2)}, u32[]{:S(2)}) collective-permute-start(f32[40,1024]{1,0:T(8,128)S(1)} %slice.99), channel_id=1, source_target_pairs={{0,32},{32,64},{64,96},{96,0},{1,33},{33,65},{65,97},{97,1},{2,34}... | collective-permute-start | bytes 491528 | tf_op jit(solution)/shard_map/ppermute | solution.py:21
  150.9 4.3 %collective-permute-start.18 = (f32[80,1024]{1,0:T(8,128)S(1)}, f32[80,1024]{1,0:T(8,128)S(1)}, u32[]{:S(2)}, u32[]{:S(2)}) collective-permute-start(f32[80,1024]{1,0:T(8,128)S(1)} %collective-permute-done.17), channel_id=1, source_target_pairs={{0,32},{32,64},{64,96},{96,0},{1,33},{33,65},{65,97},{97,1},{2,34}... | collective-permute-start | bytes 983048 | tf_op jit(solution)/shard_map/ppermute | solution.py:19
  158.7 7.0 %collective-permute-start.22 = (f32[80,1024]{1,0:T(8,128)S(1)}, f32[80,1024]{1,0:T(8,128)S(1)}, u32[]{:S(2)}, u32[]{:S(2)}) collective-permute-start(f32[80,1024]{1,0:T(8,128)S(1)} %collective-permute-done.17), channel_id=1, source_target_pairs={{0,128},{128,384},{384,256},{256,0},{1,129},{129,385},{385,257},{2... | collective-permute-start | bytes 983048 | tf_op jit(solution)/shard_map/ppermute | solution.py:44
  167.8 4.6 %collective-permute-start.20 = (f32[40,1024]{1,0:T(8,128)S(1)}, f32[40,1024]{1,0:T(8,128)S(1)}, u32[]{:S(2)}, u32[]{:S(2)}) collective-permute-start(f32[40,1024]{1,0:T(8,128)S(1)} %slice.101), channel_id=1, source_target_pairs={{0,32},{32,64},{64,96},{96,0},{1,33},{33,65},{65,97},{97,1},{2,34}... | collective-permute-start | bytes 491528 | tf_op jit(solution)/shard_map/ppermute | solution.py:21
  174.4 4.6 %collective-permute-start.23 = (f32[80,1024]{1,0:T(8,128)S(1)}, f32[80,1024]{1,0:T(8,128)S(1)}, u32[]{:S(2)}, u32[]{:S(2)}) collective-permute-start(f32[80,1024]{1,0:T(8,128)S(1)} %collective-permute-done.22), channel_id=1, source_target_pairs={{0,32},{32,64},{64,96},{96,0},{1,33},{33,65},{65,97},{97,1},{2,34}... | collective-permute-start | bytes 983048 | tf_op jit(solution)/shard_map/ppermute | solution.py:19
  184.5 4.6 %collective-permute-start.25 = (f32[40,1024]{1,0:T(8,128)S(1)}, f32[40,1024]{1,0:T(8,128)S(1)}, u32[]{:S(2)}, u32[]{:S(2)}) collective-permute-start(f32[40,1024]{1,0:T(8,128)S(1)} %slice.103), channel_id=1, source_target_pairs={{0,32},{32,64},{64,96},{96,0},{1,33},{33,65},{65,97},{97,1},{2,34}... | collective-permute-start | bytes 491528 | tf_op jit(solution)/shard_map/ppermute | solution.py:21
  193.3 3.1 %collective-permute-done.26 = f32[40,1024]{1,0:T(8,128)S(1)} collective-permute-done((f32[40,1024]{1,0:T(8,128)S(1)}, f32[40,1024]{1,0:T(8,128)S(1)}, u32[]{:S(2)}, u32[]{:S(2)}) %collective-permute-start.26) | collective-permute-done | bytes 163872 | tf_op jit(solution)/shard_map/ppermute | solution.py:22
  197.1 4.4 %fusion.29 = f32[152,1024]{1,0:T(8,128)S(1)} fusion(f32[1280,152]{0,1:T(8,128)S(1)} %collective-permute-done.27, f32[1280,1024]{1,0:T(8,128)} %constant_dynamic-update-slice_fusion.14), kind=kOutput, calls=%fused_computation.130 | convolution fusion | flops 1195376640 | bytes 6643712 | tf_op jit(solution)/shard_map/dot_general | solution.py:70
  201.5 7.3 %collective-permute-start.28 = (f32[152,1024]{1,0:T(8,128)S(1)}, f32[152,1024]{1,0:T(8,128)S(1)}, u32[]{:S(2)}, u32[]{:S(2)}) collective-permute-start(f32[152,1024]{1,0:T(8,128)S(1)} %fusion.29), channel_id=1, source_target_pairs={{0,16},{16,0},{1,17},{17,1},{2,18},{18,2},{3,19},{19,3},{4,20},{20... | collective-permute-start | bytes 1867784 | tf_op jit(solution)/shard_map/ppermute | solution.py:75
  (128 shorter events, 78.5 us)
Async XLA Ops:
  1.0 34.7 %collective-permute-start = (f32[160,152]{1,0:T(8,128)S(1)}, f32[160,152]{1,0:T(8,128)}, u32[]{:S(2)}, u32[]{:S(2)}) collective-permute-start(f32[160,152]{1,0:T(8,128)S(1)} %bitcast.31), channel_id=1, source_target_pairs={{0,1},{1,2},{2,3},{3,0},{4,5},{5,6},{6,7},{7,4},{8,9},{9,10},{10,1... | collective-permute-start | bytes 291848 | tf_op jit(solution)/shard_map/ppermute | solution.py:19
  9.8 33.9 %collective-permute-start.1 = (f32[160,152]{1,0:T(8,128)S(1)}, f32[160,152]{1,0:T(8,128)}, u32[]{:S(2)}, u32[]{:S(2)}) collective-permute-start(f32[160,152]{1,0:T(8,128)S(1)} %bitcast.32), channel_id=1, source_target_pairs={{0,3},{1,0},{2,1},{3,2},{4,7},{5,4},{6,5},{7,6},{8,11},{9,8},{10,9... | collective-permute-start | bytes 291848 | tf_op jit(solution)/shard_map/ppermute | solution.py:20
  16.7 66.5 %all-to-all-start = ((f32[16,8,640]{2,1,0:T(8,128)}), f32[16,8,640]{2,1,0:T(8,128)}, u32[]{:S(2)}, u32[]{:S(2)}) async-start(f32[16,8,640]{2,1,0:T(8,128)} %copy.31), calls=%async_computation | async-start | bytes 655360 | tf_op jit(solution)/shard_map/all_to_all | solution.py:31
  36.7 12.0 %collective-permute-start.2 = (f32[80,152]{1,0:T(8,128)S(1)}, f32[80,152]{1,0:T(8,128)S(1)}, u32[]{:S(2)}, u32[]{:S(2)}) collective-permute-start(f32[80,152]{1,0:T(8,128)S(1)} %slice.92), channel_id=1, source_target_pairs={{0,1},{1,2},{2,3},{3,0},{4,5},{5,6},{6,7},{7,4},{8,9},{9,10},{10,1... | collective-permute-start | bytes 145928 | tf_op jit(solution)/shard_map/ppermute | solution.py:21
  44.7 13.7 %collective-permute-start.3 = (f32[80,152]{1,0:T(8,128)S(1)}, f32[80,152]{1,0:T(8,128)S(1)}, u32[]{:S(2)}, u32[]{:S(2)}) collective-permute-start(f32[80,152]{1,0:T(8,128)S(1)} %slice.93), channel_id=1, source_target_pairs={{0,3},{1,0},{2,1},{3,2},{4,7},{5,4},{6,5},{7,6},{8,11},{9,8},{10,9... | collective-permute-start | bytes 145928 | tf_op jit(solution)/shard_map/ppermute | solution.py:22
  59.4 12.1 %collective-permute-start.4 = (f32[640,152]{0,1:T(8,128)}, f32[640,152]{0,1:T(8,128)}, u32[]{:S(2)}, u32[]{:S(2)}) collective-permute-start(f32[640,152]{0,1:T(8,128)} %copy.20), channel_id=1, source_target_pairs={{0,4},{4,8},{8,12},{12,0},{1,5},{5,9},{9,13},{13,1},{2,6},{6,10},{... | collective-permute-start | bytes 1167368 | tf_op jit(solution)/shard_map/ppermute | solution.py:19
  62.3 13.2 %collective-permute-start.5 = (f32[640,152]{0,1:T(8,128)}, f32[640,152]{0,1:T(8,128)}, u32[]{:S(2)}, u32[]{:S(2)}) collective-permute-start(f32[640,152]{0,1:T(8,128)} %copy.20), channel_id=1, source_target_pairs={{0,12},{4,0},{8,4},{12,8},{1,13},{5,1},{9,5},{13,9},{2,14},{6,2},{... | collective-permute-start | bytes 1167368 | tf_op jit(solution)/shard_map/ppermute | solution.py:20
  73.6 20.8 %collective-permute-start.6 = (f32[320,152]{1,0:T(8,128)}, f32[320,152]{1,0:T(8,128)}, u32[]{:S(2)}, u32[]{:S(2)}) collective-permute-start(f32[320,152]{1,0:T(8,128)} %slice.94), channel_id=1, source_target_pairs={{0,4},{4,8},{8,12},{12,0},{1,5},{5,9},{9,13},{13,1},{2,6},{6,10},{... | collective-permute-start | bytes 583688 | tf_op jit(solution)/shard_map/ppermute | solution.py:21
  77.5 17.9 %collective-permute-start.7 = (f32[320,152]{1,0:T(8,128)}, f32[320,152]{1,0:T(8,128)}, u32[]{:S(2)}, u32[]{:S(2)}) collective-permute-start(f32[320,152]{1,0:T(8,128)} %slice.95), channel_id=1, source_target_pairs={{0,12},{4,0},{8,4},{12,8},{1,13},{5,1},{9,5},{13,9},{2,14},{6,2},{... | collective-permute-start | bytes 583688 | tf_op jit(solution)/shard_map/ppermute | solution.py:22
  87.1 34.9 %collective-permute-start.8 = (f32[80,1024]{1,0:T(8,128)}, f32[80,1024]{1,0:T(8,128)}, u32[]{:S(2)}, u32[]{:S(2)}) collective-permute-start(f32[80,1024]{1,0:T(8,128)} %get-tuple-element.6), channel_id=1, source_target_pairs={{0,32},{32,64},{64,96},{96,0},{1,33},{33,65},{65,97},{97,1},{2,34}... | collective-permute-start | bytes 983048 | tf_op jit(solution)/shard_map/ppermute | solution.py:19
  89.2 37.1 %collective-permute-start.9 = (f32[80,1024]{1,0:T(8,128)}, f32[80,1024]{1,0:T(8,128)}, u32[]{:S(2)}, u32[]{:S(2)}) collective-permute-start(f32[80,1024]{1,0:T(8,128)} %get-tuple-element.6), channel_id=1, source_target_pairs={{0,96},{32,0},{64,32},{96,64},{1,97},{33,1},{65,33},{97,65},{2,98}... | collective-permute-start | bytes 983048 | tf_op jit(solution)/shard_map/ppermute | solution.py:20
  92.4 36.8 %collective-permute-start.12 = (f32[80,1024]{1,0:T(8,128)}, f32[80,1024]{1,0:T(8,128)}, u32[]{:S(2)}, u32[]{:S(2)}) collective-permute-start(f32[80,1024]{1,0:T(8,128)} %get-tuple-element.6), channel_id=1, source_target_pairs={{0,128},{128,384},{384,256},{256,0},{1,129},{129,385},{385,257},{2... | collective-permute-start | bytes 983048 | tf_op jit(solution)/shard_map/ppermute | solution.py:44
  116.2 80.9 %collective-permute-start.27 = (f32[1280,152]{0,1:T(8,128)S(1)}, f32[1280,152]{0,1:T(8,128)S(1)}, u32[]{:S(2)}, u32[]{:S(2)}) collective-permute-start(f32[1280,152]{0,1:T(8,128)S(1)} %copy.30), channel_id=1, source_target_pairs={{0,16},{16,0},{1,17},{17,1},{2,18},{18,2},{3,19},{19,3},{4,20},{20... | collective-permute-start | bytes 2334728 | tf_op jit(solution)/shard_map/ppermute | solution.py:67
  122.9 16.2 %collective-permute-start.10 = (f32[40,1024]{1,0:T(8,128)S(1)}, f32[40,1024]{1,0:T(8,128)S(1)}, u32[]{:S(2)}, u32[]{:S(2)}) collective-permute-start(f32[40,1024]{1,0:T(8,128)S(1)} %slice.97), channel_id=1, source_target_pairs={{0,32},{32,64},{64,96},{96,0},{1,33},{33,65},{65,97},{97,1},{2,34}... | collective-permute-start | bytes 491528 | tf_op jit(solution)/shard_map/ppermute | solution.py:21
  127.2 14.5 %collective-permute-start.11 = (f32[40,1024]{1,0:T(8,128)S(1)}, f32[40,1024]{1,0:T(8,128)S(1)}, u32[]{:S(2)}, u32[]{:S(2)}) collective-permute-start(f32[40,1024]{1,0:T(8,128)S(1)} %slice.98), channel_id=1, source_target_pairs={{0,96},{32,0},{64,32},{96,64},{1,97},{33,1},{65,33},{97,65},{2,98}... | collective-permute-start | bytes 491528 | tf_op jit(solution)/shard_map/ppermute | solution.py:22
  129.2 15.0 %collective-permute-start.13 = (f32[80,1024]{1,0:T(8,128)}, f32[80,1024]{1,0:T(8,128)S(1)}, u32[]{:S(2)}, u32[]{:S(2)}) collective-permute-start(f32[80,1024]{1,0:T(8,128)} %collective-permute-done.12), channel_id=1, source_target_pairs={{0,32},{32,64},{64,96},{96,0},{1,33},{33,65},{65,97},{97,1},{2,34}... | collective-permute-start | bytes 983048 | tf_op jit(solution)/shard_map/ppermute | solution.py:19
  133.7 15.0 %collective-permute-start.14 = (f32[80,1024]{1,0:T(8,128)}, f32[80,1024]{1,0:T(8,128)S(1)}, u32[]{:S(2)}, u32[]{:S(2)}) collective-permute-start(f32[80,1024]{1,0:T(8,128)} %collective-permute-done.12), channel_id=1, source_target_pairs={{0,96},{32,0},{64,32},{96,64},{1,97},{33,1},{65,33},{97,65},{2,98}... | collective-permute-start | bytes 983048 | tf_op jit(solution)/shard_map/ppermute | solution.py:20
  139.1 11.8 %collective-permute-start.17 = (f32[80,1024]{1,0:T(8,128)}, f32[80,1024]{1,0:T(8,128)S(1)}, u32[]{:S(2)}, u32[]{:S(2)}) collective-permute-start(f32[80,1024]{1,0:T(8,128)} %collective-permute-done.12), channel_id=1, source_target_pairs={{0,128},{128,384},{384,256},{256,0},{1,129},{129,385},{385,257},{2... | collective-permute-start | bytes 983048 | tf_op jit(solution)/shard_map/ppermute | solution.py:44
  144.1 14.6 %collective-permute-start.15 = (f32[40,1024]{1,0:T(8,128)S(1)}, f32[40,1024]{1,0:T(8,128)S(1)}, u32[]{:S(2)}, u32[]{:S(2)}) collective-permute-start(f32[40,1024]{1,0:T(8,128)S(1)} %slice.99), channel_id=1, source_target_pairs={{0,32},{32,64},{64,96},{96,0},{1,33},{33,65},{65,97},{97,1},{2,34}... | collective-permute-start | bytes 491528 | tf_op jit(solution)/shard_map/ppermute | solution.py:21
  148.8 17.6 %collective-permute-start.16 = (f32[40,1024]{1,0:T(8,128)S(1)}, f32[40,1024]{1,0:T(8,128)S(1)}, u32[]{:S(2)}, u32[]{:S(2)}) collective-permute-start(f32[40,1024]{1,0:T(8,128)S(1)} %slice.100), channel_id=1, source_target_pairs={{0,96},{32,0},{64,32},{96,64},{1,97},{33,1},{65,33},{97,65},{2,98}... | collective-permute-start | bytes 491528 | tf_op jit(solution)/shard_map/ppermute | solution.py:22
  150.9 16.9 %collective-permute-start.18 = (f32[80,1024]{1,0:T(8,128)S(1)}, f32[80,1024]{1,0:T(8,128)S(1)}, u32[]{:S(2)}, u32[]{:S(2)}) collective-permute-start(f32[80,1024]{1,0:T(8,128)S(1)} %collective-permute-done.17), channel_id=1, source_target_pairs={{0,32},{32,64},{64,96},{96,0},{1,33},{33,65},{65,97},{97,1},{2,34}... | collective-permute-start | bytes 983048 | tf_op jit(solution)/shard_map/ppermute | solution.py:19
  155.3 17.2 %collective-permute-start.19 = (f32[80,1024]{1,0:T(8,128)S(1)}, f32[80,1024]{1,0:T(8,128)S(1)}, u32[]{:S(2)}, u32[]{:S(2)}) collective-permute-start(f32[80,1024]{1,0:T(8,128)S(1)} %collective-permute-done.17), channel_id=1, source_target_pairs={{0,96},{32,0},{64,32},{96,64},{1,97},{33,1},{65,33},{97,65},{2,98}... | collective-permute-start | bytes 983048 | tf_op jit(solution)/shard_map/ppermute | solution.py:20
  158.7 15.7 %collective-permute-start.22 = (f32[80,1024]{1,0:T(8,128)S(1)}, f32[80,1024]{1,0:T(8,128)S(1)}, u32[]{:S(2)}, u32[]{:S(2)}) collective-permute-start(f32[80,1024]{1,0:T(8,128)S(1)} %collective-permute-done.17), channel_id=1, source_target_pairs={{0,128},{128,384},{384,256},{256,0},{1,129},{129,385},{385,257},{2... | collective-permute-start | bytes 983048 | tf_op jit(solution)/shard_map/ppermute | solution.py:44
  167.8 14.6 %collective-permute-start.20 = (f32[40,1024]{1,0:T(8,128)S(1)}, f32[40,1024]{1,0:T(8,128)S(1)}, u32[]{:S(2)}, u32[]{:S(2)}) collective-permute-start(f32[40,1024]{1,0:T(8,128)S(1)} %slice.101), channel_id=1, source_target_pairs={{0,32},{32,64},{64,96},{96,0},{1,33},{33,65},{65,97},{97,1},{2,34}... | collective-permute-start | bytes 491528 | tf_op jit(solution)/shard_map/ppermute | solution.py:21
  (9 other events, 97.6 us)

commit v2 on v1

v2 whole, which is shorter than its diff:
```python
import functools

import jax
import jax.numpy as jnp
from jax import lax
from jax.experimental import pallas as pl
from jax.experimental.pallas import tpu as pltpu
from jax.sharding import Mesh, PartitionSpec as P

NA = 128
VIR = ("y", "zh")
OCC = ("zl", "x", "c")
RING = (0, 1, 3, 2)
SLOT = (0, 2, 3, 1)
VMEM = pl.BlockSpec(memory_space=pltpu.VMEM)
SMEM = pl.BlockSpec(memory_space=pltpu.SMEM)


def shift(n, by):
    return [(i, (i + by) % n) for i in range(n)]


def around(up, down, axis):
    return lax.ppermute(up, axis, shift(4, 1)), lax.ppermute(down, axis, shift(4, -1))


def symmetrized(integrals):
    rows = integrals.shape[0]
    here = integrals.shape[1] // NA
    ranks = NA // here
    sent = integrals.reshape(rows, here, ranks, here).transpose(2, 1, 3, 0).reshape(ranks, here, here * rows)
    got = lax.all_to_all(sent, VIR, split_axis=0, concat_axis=0, tiled=True)
    swapped = got.reshape(NA, here * rows).T.reshape(here, rows, NA)
    return integrals + swapped.transpose(1, 0, 2).reshape(integrals.shape)


def antisym_kernel(block, base_ref, other_ref, tau_ref, mine_ref, theirs_ref, rows_ref):
    total = rows_ref.shape[0]

    def one(b, _):
        at = pl.multiple_of(b * block, 8)
        for r in range(block):
            rows_ref[pl.ds(at + r, 1), :] = tau_ref[pl.ds(other_ref[at + r], 1), :]
        here = tau_ref[pl.ds(pl.multiple_of(base_ref[b], 8), block), :]
        rows_ref[pl.ds(at, block), :] = here - rows_ref[pl.ds(at, block), :]
        return 0

    lax.fori_loop(0, total // block, one, 0)
    half = total // 2
    for j in range(0, half, 128):
        mine_ref[:, j : j + 128] = rows_ref[j : j + 128, :].T
        theirs_ref[:, j : j + 128] = rows_ref[half + j : half + j + 128, :].T


def product_kernel(counts, mine_ref, theirs_ref, *refs):
    pieces = refs[: len(counts)]
    own_ref, other_ref, high_ref, low_ref = refs[len(counts) :]
    at = 0
    for piece, count in zip(pieces, counts):
        for r in range(0, count, 80):
            value = piece[r : r + 80, :]
            high = value.astype(jnp.bfloat16)
            high_ref[at : at + 80, :] = high
            low_ref[at : at + 80, :] = (value - high.astype(jnp.float32)).astype(jnp.bfloat16)
            at += 80
    lhs = jnp.concatenate([mine_ref[...], theirs_ref[...]], axis=0)
    lhs_high = lhs.astype(jnp.bfloat16)
    lhs_low = (lhs - lhs_high.astype(jnp.float32)).astype(jnp.bfloat16)
    dot = functools.partial(jnp.dot, preferred_element_type=jnp.float32)
    pairs = own_ref.shape[0]
    for n in range(0, own_ref.shape[1], 256):
        high, low = high_ref[:, n : n + 256], low_ref[:, n : n + 256]
        total = dot(lhs_high, high) + (dot(lhs_high, low) + dot(lhs_low, high))
        own_ref[:, n : n + 256] = total[:pairs]
        other_ref[:, n : n + 256] = total[pairs:]


def body(amplitudes, integrals, pair_list, partner):
    rows_k, columns = integrals.shape
    pairs, columns_k = amplitudes.shape
    slab = partner.shape[0]
    x, core = lax.axis_index("x"), lax.axis_index("c")
    zh = lax.axis_index("zh")
    ring_place = jnp.array([0, 1, 3, 2], jnp.int32)[lax.axis_index("zl")]

    s = [symmetrized(integrals)]
    for _ in range(3):
        s.append(lax.ppermute(s[-1], "zl", [(RING[i], RING[(i + 1) % 4]) for i in range(4)]))
    first = jnp.concatenate(s[:2], axis=0)
    la, ra = around(first, first, "x")
    lb, rb = around(
        jnp.concatenate([s[2], s[3], la[:rows_k]], axis=0), jnp.concatenate([s[2], s[3], ra[rows_k:]], axis=0), "x"
    )
    lc, rc = around(lb[:rows_k], rb[rows_k : 2 * rows_k], "x")
    pieces = s + [la, ra, lb, rb, lc, rc]
    order = [(0, 0), (1, 0), (2, 0), (3, 0), (0, -1), (1, -1), (0, 1), (1, 1)]
    order += [(2, -1), (3, -1), (0, 2), (2, 1), (3, 1), (1, 2), (2, 2), (3, 2)]

    turned = amplitudes.T
    half = columns_k // 2
    left, right = around(turned, turned, "zh")
    far_top, far_low = around(left[:half], right[half:], "zh")
    by_zh = jnp.concatenate([turned, left, right, far_top, far_low], axis=0)
    tau = lax.all_gather(by_zh, "y", axis=0, tiled=True)

    slot = jnp.array(SLOT, jnp.int32)

    def place(k):
        rank = k // columns_k
        return ((rank // 4) * 4 + slot[(rank % 4 - zh) % 4]) * columns_k + k % columns_k

    steps = jnp.array(order, jnp.int32)
    zs = jnp.array(RING, jnp.int32)[(ring_place - steps[:, 0]) % 4]
    chunk = (zs * 4 + (x + steps[:, 1]) % 4) * 2
    chunk = jnp.concatenate([chunk + core, chunk + 1 - core])
    base = place(chunk * rows_k)
    other = place(partner).reshape(-1, rows_k).at[chunk].get(mode="promise_in_bounds").reshape(-1)
    mine, theirs = pl.pallas_call(
        functools.partial(antisym_kernel, rows_k),
        out_shape=[jax.ShapeDtypeStruct((pairs, slab // 2), jnp.float32)] * 2,
        in_specs=[SMEM, SMEM, VMEM],
        out_specs=[VMEM] * 2,
        scratch_shapes=[pltpu.VMEM((slab, pairs), jnp.float32)],
        compiler_params=pltpu.CompilerParams(vmem_limit_bytes=16 * 2**20),
        cost_estimate=pl.CostEstimate(flops=slab * pairs, bytes_accessed=3 * slab * pairs * 4, transcendentals=0),
        name="antisym",
    )(base, other, tau)
    theirs = lax.ppermute(theirs, "c", shift(2, 1))

    own, back = pl.pallas_call(
        functools.partial(product_kernel, [p.shape[0] for p in pieces]),
        out_shape=[jax.ShapeDtypeStruct((pairs, columns), jnp.float32)] * 2,
        in_specs=[VMEM] * (2 + len(pieces)),
        out_specs=[VMEM] * 2,
        scratch_shapes=[pltpu.VMEM((slab // 2, columns), jnp.bfloat16)] * 2,
        compiler_params=pltpu.CompilerParams(vmem_limit_bytes=32 * 2**20),
        cost_estimate=pl.CostEstimate(flops=6 * pairs * slab * columns, bytes_accessed=8 * 2**20, transcendentals=0),
        name="product",
    )(mine, theirs, *pieces)
    back = lax.ppermute(back, "c", shift(2, 1))
    weight = jnp.where(pair_list[:, 0] == pair_list[:, 1], 0.5, 1.0).astype(jnp.float32)
    return weight[:, None] * (own + back)


def solution(mesh):
    fine = Mesh(mesh.devices.reshape(4, 4, 2, 4, 4), OCC + VIR)
    placed = (P(OCC, VIR), P(OCC, VIR), P(OCC, None), P())
    return jax.shard_map(
        body, mesh=fine, in_specs=placed, out_specs=P(OCC, VIR), check_vma=False
    )
```

time: 215 us -> 171 us (0.80)
  the two profiles are of different devices: /device:TPU:39 before, /device:TPU:1 now
where the time goes in v2:
time: 171 us; the launch traced here: 168 us
  starting transfers between devices  73 us (43%)
  waiting for transfers between devices  54.8 us (32%)
  Pallas kernels  13.9 us (8%)
  between operations  13.8 us (8%)
  local copies, waits for them, and re-layouts  9.24 us (5%)
  other arithmetic  3.59 us (2%)
    ppermute x5, waiting for transfers between devices, around(): lax.ppermute(down, axis, shift(4, -1))  23.1 us
    ppermute x5, starting transfers between devices, around(): lax.ppermute(up, axis, shift(4, 1))  21.4 us
    all_to_all x1, starting transfers between devices, symmetrized(): got = lax.all_to_all(sent, VIR, split_axis=0, concat_axis=0, tiled=True)  18.5 us
    ppermute x5, waiting for transfers between devices, around(): lax.ppermute(up, axis, shift(4, 1))  17.4 us
    ppermute x5, starting transfers between devices, around(): lax.ppermute(down, axis, shift(4, -1))  14.2 us
    ppermute x3, starting transfers between devices, body(): lax.ppermute(s[-1], 'zl', [(RING[i], RING[(i + 1) % 4]) for i in range(4)])  13.3 us
    pallas_call x1, Pallas kernels, body(): pl.pallas_call(functools.partial(antisym_kernel, rows_k), out_shape=[jax....  9.8 us
    all_gather x1, waiting for transfers between devices, body(): tau = lax.all_gather(by_zh, 'y', axis=0, tiled=True)  6.38 us
  transfers between devices with their start and end apart: 17, of which 11 were waited for; matrix products, arithmetic and copies ran while one was open for 4% of the time, Pallas kernels for 6%

profile of v2, /device:TPU:1, one launch (start us, length us, event | category | flops | bytes accessed | tf_op | source)
XLA Modules:
  0.0 168.3 jit_solution(438870118336921812)
XLA Ops:
  8.8 18.5 %all-to-all-start = ((f32[16,8,640]{2,1,0:T(8,128)}), f32[16,8,640]{2,1,0:T(8,128)S(1)}, u32[]{:S(2)}, u32[]{:S(2)}) async-start(f32[16,8,640]{2,1,0:T(8,128)} %copy.15), calls=%async_computation | async-start | bytes 655360 | tf_op jit(solution)/shard_map/all_to_all | solution.py:32
  27.5 7.2 %collective-permute-start = (f32[160,152]{1,0:T(8,128)S(1)}, f32[160,152]{1,0:T(8,128)S(1)}, u32[]{:S(2)}, u32[]{:S(2)}) collective-permute-start(f32[160,152]{1,0:T(8,128)S(1)} %bitcast.51), channel_id=1, source_target_pairs={{0,1},{1,2},{2,3},{3,0},{4,5},{5,6},{6,7},{7,4},{8,9},{9,10},{10,1... | collective-permute-start | bytes 291848 | tf_op jit(solution)/shard_map/ppermute | solution.py:24
  37.4 5.5 %collective-permute-done = f32[160,152]{1,0:T(8,128)S(1)} collective-permute-done((f32[160,152]{1,0:T(8,128)S(1)}, f32[160,152]{1,0:T(8,128)S(1)}, u32[]{:S(2)}, u32[]{:S(2)}) %collective-permute-start) | collective-permute-done | bytes 97312 | tf_op jit(solution)/shard_map/ppermute | solution.py:24
  42.9 4.9 %collective-permute-start.2 = (f32[80,152]{1,0:T(8,128)S(1)}, f32[80,152]{1,0:T(8,128)S(1)}, u32[]{:S(2)}, u32[]{:S(2)}) collective-permute-start(f32[80,152]{1,0:T(8,128)S(1)} %slice.54), channel_id=1, source_target_pairs={{0,1},{1,2},{2,3},{3,0},{4,5},{5,6},{6,7},{7,4},{8,9},{9,10},{10,1... | collective-permute-start | bytes 145928 | tf_op jit(solution)/shard_map/ppermute | solution.py:24
  47.7 13.8 %collective-permute-done.1 = f32[160,152]{1,0:T(8,128)S(1)} collective-permute-done((f32[160,152]{1,0:T(8,128)S(1)}, f32[160,152]{1,0:T(8,128)S(1)}, u32[]{:S(2)}, u32[]{:S(2)}) %collective-permute-start.1) | collective-permute-done | bytes 97312 | tf_op jit(solution)/shard_map/ppermute | solution.py:24
  63.6 3.6 %collective-permute-done.2 = f32[80,152]{1,0:T(8,128)S(1)} collective-permute-done((f32[80,152]{1,0:T(8,128)S(1)}, f32[80,152]{1,0:T(8,128)S(1)}, u32[]{:S(2)}, u32[]{:S(2)}) %collective-permute-start.2) | collective-permute-done | bytes 48672 | tf_op jit(solution)/shard_map/ppermute | solution.py:24
  67.2 4.7 %collective-permute-done.3 = f32[80,152]{1,0:T(8,128)S(1)} collective-permute-done((f32[80,152]{1,0:T(8,128)S(1)}, f32[80,152]{1,0:T(8,128)S(1)}, u32[]{:S(2)}, u32[]{:S(2)}) %collective-permute-start.3) | collective-permute-done | bytes 48672 | tf_op jit(solution)/shard_map/ppermute | solution.py:24
  76.4 6.2 %collective-permute-done.5.refs_1_ = f32[80,1024]{1,0:T(8,128)S(1)} collective-permute-done((f32[80,1024]{1,0:T(8,128)S(1)}, f32[80,1024]{1,0:T(8,128)S(1)}, u32[]{:S(2)}, u32[]{:S(2)}) %collective-permute-start.5) | collective-permute-done | bytes 327712 | tf_op jit(solution)/shard_map/ppermute | solution.py:88
  82.6 6.3 %collective-permute-start.6 = (f32[80,1024]{1,0:T(8,128)S(1)}, f32[80,1024]{1,0:T(8,128)S(1)}, u32[]{:S(2)}, u32[]{:S(2)}) collective-permute-start(f32[80,1024]{1,0:T(8,128)S(1)} %collective-permute-done.5.refs_1_), channel_id=1, source_target_pairs={{0,128},{128,384},{384,256},{256,0},{1,129},{129,385},{385,257},{2... | collective-permute-start | bytes 983048 | tf_op jit(solution)/shard_map/ppermute | solution.py:88
  89.0 3.1 %collective-permute-start.8 = (f32[160,1024]{1,0:T(8,128)S(1)}, f32[160,1024]{1,0:T(8,128)S(1)}, u32[]{:S(2)}, u32[]{:S(2)}) collective-permute-start(f32[160,1024]{1,0:T(8,128)S(1)} %pad_maximum_fusion.3), channel_id=1, source_target_pairs={{0,32},{32,64},{64,96},{96,0},{1,33},{33,65},{65,97},{97,1},{2,34}... | collective-permute-start | bytes 1966088 | tf_op jit(solution)/shard_map/ppermute | solution.py:24
  92.1 3.4 %collective-permute-start.9 = (f32[160,1024]{1,0:T(8,128)S(1)}, f32[160,1024]{1,0:T(8,128)S(1)}, u32[]{:S(2)}, u32[]{:S(2)}) collective-permute-start(f32[160,1024]{1,0:T(8,128)S(1)} %pad_maximum_fusion.3), channel_id=1, source_target_pairs={{0,96},{32,0},{64,32},{96,64},{1,97},{33,1},{65,33},{97,65},{2,98}... | collective-permute-start | bytes 1966088 | tf_op jit(solution)/shard_map/ppermute | solution.py:24
  95.5 5.0 %collective-permute-start.7 = (f32[80,1024]{1,0:T(8,128)S(1)}, f32[80,1024]{1,0:T(8,128)S(1)}, u32[]{:S(2)}, u32[]{:S(2)}) collective-permute-start(f32[80,1024]{1,0:T(8,128)S(1)} %collective-permute-done.6.refs_2_), channel_id=1, source_target_pairs={{0,128},{128,384},{384,256},{256,0},{1,129},{129,385},{385,257},{2... | collective-permute-start | bytes 983048 | tf_op jit(solution)/shard_map/ppermute | solution.py:88
  101.4 3.9 %collective-permute-done.8.refs_4_ = f32[160,1024]{1,0:T(8,128)S(1)} collective-permute-done((f32[160,1024]{1,0:T(8,128)S(1)}, f32[160,1024]{1,0:T(8,128)S(1)}, u32[]{:S(2)}, u32[]{:S(2)}) %collective-permute-start.8) | collective-permute-done | bytes 655392 | tf_op jit(solution)/shard_map/ppermute | solution.py:24
  108.5 3.1 %collective-permute-start.10 = (f32[240,1024]{1,0:T(8,128)}, f32[240,1024]{1,0:T(8,128)}, u32[]{:S(2)}, u32[]{:S(2)}) collective-permute-start(f32[240,1024]{1,0:T(8,128)} %get-tuple-element.18), channel_id=1, source_target_pairs={{0,32},{32,64},{64,96},{96,0},{1,33},{33,65},{65,97},{97,1},{2,34}... | collective-permute-start | bytes 2949128 | tf_op jit(solution)/shard_map/ppermute | solution.py:24
  111.6 3.4 %collective-permute-start.11 = (f32[240,1024]{1,0:T(8,128)}, f32[240,1024]{1,0:T(8,128)}, u32[]{:S(2)}, u32[]{:S(2)}) collective-permute-start(f32[240,1024]{1,0:T(8,128)} %get-tuple-element.17), channel_id=1, source_target_pairs={{0,96},{32,0},{64,32},{96,64},{1,97},{33,1},{65,33},{97,65},{2,98}... | collective-permute-start | bytes 2949128 | tf_op jit(solution)/shard_map/ppermute | solution.py:24
  115.1 6.4 %all-gather.2.cloned.1.call-done.tau_ref = f32[2560,152]{1,0:T(8,128)} async-done(((f32[640,152]{1,0:T(8,128)}), f32[2560,152]{1,0:T(8,128)}) %all-gather.2.cloned.1.call-update) | async-done | bytes 1556496 | tf_op jit(solution)/shard_map/all_gather | solution.py:104
  123.2 9.8 %antisym.1 = (f32[152,1280]{1,0:T(8,128)S(1)}, f32[152,1280]{1,0:T(8,128)S(1)}) custom-call(s32[32]{0:T(128)S(1)} %fusion.11.base_ref, s32[2560]{0:T(1024)S(1)} %reshape.222.other_ref, f32[2560,152]{1,0:T(8,128)S(1)} %copy-done), custom_call_target="tpu_custom_call" | custom-call | flops 389120 | bytes 4669440 | tf_op jit(solution)/shard_map/antisym/pallas_call | solution.py:118
  133.1 2.6 %collective-permute-start.4 = (f32[152,1280]{1,0:T(8,128)S(1)}, f32[152,1280]{1,0:T(8,128)S(1)}, u32[]{:S(2)}, u32[]{:S(2)}) collective-permute-start(f32[152,1280]{1,0:T(8,128)S(1)} %get-tuple-element.10), channel_id=1, source_target_pairs={{0,16},{16,0},{1,17},{17,1},{2,18},{18,2},{3,19},{19,3},{4,20},{20... | collective-permute-start | bytes 2334728 | tf_op jit(solution)/shard_map/ppermute | solution.py:128
  136.7 3.1 %collective-permute-start.12 = (f32[80,1024]{1,0:T(8,128)S(1)}, f32[80,1024]{1,0:T(8,128)S(1)}, u32[]{:S(2)}, u32[]{:S(2)}) collective-permute-start(f32[80,1024]{1,0:T(8,128)S(1)} %slice.58), channel_id=1, source_target_pairs={{0,32},{32,64},{64,96},{96,0},{1,33},{33,65},{65,97},{97,1},{2,34}... | collective-permute-start | bytes 983048 | tf_op jit(solution)/shard_map/ppermute | solution.py:24
  140.8 3.4 %collective-permute-start.13 = (f32[80,1024]{1,0:T(8,128)S(1)}, f32[80,1024]{1,0:T(8,128)S(1)}, u32[]{:S(2)}, u32[]{:S(2)}) collective-permute-start(f32[80,1024]{1,0:T(8,128)S(1)} %slice.59), channel_id=1, source_target_pairs={{0,96},{32,0},{64,32},{96,64},{1,97},{33,1},{65,33},{97,65},{2,98}... | collective-permute-start | bytes 983048 | tf_op jit(solution)/shard_map/ppermute | solution.py:24
  144.2 4.5 %collective-permute-done.12.refs_8_ = f32[80,1024]{1,0:T(8,128)S(1)} collective-permute-done((f32[80,1024]{1,0:T(8,128)S(1)}, f32[80,1024]{1,0:T(8,128)S(1)}, u32[]{:S(2)}, u32[]{:S(2)}) %collective-permute-start.12) | collective-permute-done | bytes 327712 | tf_op jit(solution)/shard_map/ppermute | solution.py:24
  148.6 3.0 %collective-permute-done.13.refs_9_ = f32[80,1024]{1,0:T(8,128)S(1)} collective-permute-done((f32[80,1024]{1,0:T(8,128)S(1)}, f32[80,1024]{1,0:T(8,128)S(1)}, u32[]{:S(2)}, u32[]{:S(2)}) %collective-permute-start.13) | collective-permute-done | bytes 327712 | tf_op jit(solution)/shard_map/ppermute | solution.py:24
  151.7 4.1 %product.1 = (f32[152,1024]{1,0:T(8,128)S(1)}, f32[152,1024]{1,0:T(8,128)S(1)}) custom-call(f32[152,1280]{1,0:T(8,128)S(1)} %get-tuple-element.9.mine_ref, f32[152,1280]{1,0:T(8,128)S(1)} %collective-permute-done.4.theirs_ref, f32[80,1024]{1,0:T(8,128)S(1)} %bitcast_add_fusion.refs_0_, f32[80,1024]{1,0:T(8,128)S(1)} %collective-permute-done.5.refs_1_, ...), custom_call_target="tpu_custom_call" | custom-call | flops 2390753280 | bytes 8388608 | tf_op jit(solution)/shard_map/product/pallas_call | solution.py:130
  155.8 3.0 %collective-permute-start.14 = (f32[152,1024]{1,0:T(8,128)S(1)}, f32[152,1024]{1,0:T(8,128)S(1)}, u32[]{:S(2)}, u32[]{:S(2)}) collective-permute-start(f32[152,1024]{1,0:T(8,128)S(1)} %get-tuple-element.12), channel_id=1, source_target_pairs={{0,16},{16,0},{1,17},{17,1},{2,18},{18,2},{3,19},{19,3},{4,20},{20... | collective-permute-start | bytes 1867784 | tf_op jit(solution)/shard_map/ppermute | solution.py:140
  (67 shorter events, 22.1 us)
Async XLA Ops:
  6.5 30.2 %copy-start.1 = (s32[4]{0:T(128)S(1)}, s32[4]{0:T(128)}, u32[]{:S(2)}) copy-start(s32[4]{0:T(128)} %constant.129.clone) | copy-start | bytes 52
  6.5 66.2 %copy-start.8 = (s32[16,1]{0,1:T(1,128)S(1)}, s32[16,1]{0,1:T(1,128)}, u32[]{:S(2)}) copy-start(s32[16,1]{0,1:T(1,128)} %constant.137) | copy-start | bytes 196
  6.5 20.8 %copy-start.4 = (f32[152,160]{1,0:T(8,128)S(1)}, f32[152,160]{1,0:T(8,128)}, u32[]{:S(2)}) copy-start(f32[152,160]{1,0:T(8,128)} %param.8) | copy-start | bytes 291844
  7.8 65.9 %copy-start.2 = (f32[80,1024]{1,0:T(8,128)S(1)}, f32[80,1024]{1,0:T(8,128)}, u32[]{:S(2)}) copy-start(f32[80,1024]{1,0:T(8,128)} %param.9) | copy-start | bytes 983044
  8.8 67.5 %copy-start.5 = (s32[2560]{0:T(1024)S(1)}, s32[2560]{0:T(1024)}, u32[]{:S(2)}) copy-start(s32[2560]{0:T(1024)} %param.11) | copy-start | bytes 30724
  8.8 64.7 %all-to-all-start = ((f32[16,8,640]{2,1,0:T(8,128)}), f32[16,8,640]{2,1,0:T(8,128)S(1)}, u32[]{:S(2)}, u32[]{:S(2)}) async-start(f32[16,8,640]{2,1,0:T(8,128)} %copy.15), calls=%async_computation | async-start | bytes 655360 | tf_op jit(solution)/shard_map/all_to_all | solution.py:32
  27.3 94.2 %all-gather.2.cloned.1.call-start = ((), (), s32[]{:S(2)}) async-start(), calls=%async_computation.1 | async-start | bytes 3276800 | tf_op jit(solution)/shard_map/all_gather | solution.py:104
  27.5 15.4 %collective-permute-start = (f32[160,152]{1,0:T(8,128)S(1)}, f32[160,152]{1,0:T(8,128)S(1)}, u32[]{:S(2)}, u32[]{:S(2)}) collective-permute-start(f32[160,152]{1,0:T(8,128)S(1)} %bitcast.51), channel_id=1, source_target_pairs={{0,1},{1,2},{2,3},{3,0},{4,5},{5,6},{6,7},{7,4},{8,9},{9,10},{10,1... | collective-permute-start | bytes 291848 | tf_op jit(solution)/shard_map/ppermute | solution.py:24
  34.7 26.8 %collective-permute-start.1 = (f32[160,152]{1,0:T(8,128)S(1)}, f32[160,152]{1,0:T(8,128)S(1)}, u32[]{:S(2)}, u32[]{:S(2)}) collective-permute-start(f32[160,152]{1,0:T(8,128)S(1)} %bitcast.52), channel_id=1, source_target_pairs={{0,3},{1,0},{2,1},{3,2},{4,7},{5,4},{6,5},{7,6},{8,11},{9,8},{10,9... | collective-permute-start | bytes 291848 | tf_op jit(solution)/shard_map/ppermute | solution.py:24
  42.9 24.3 %collective-permute-start.2 = (f32[80,152]{1,0:T(8,128)S(1)}, f32[80,152]{1,0:T(8,128)S(1)}, u32[]{:S(2)}, u32[]{:S(2)}) collective-permute-start(f32[80,152]{1,0:T(8,128)S(1)} %slice.54), channel_id=1, source_target_pairs={{0,1},{1,2},{2,3},{3,0},{4,5},{5,6},{6,7},{7,4},{8,9},{9,10},{10,1... | collective-permute-start | bytes 145928 | tf_op jit(solution)/shard_map/ppermute | solution.py:24
  61.5 34.0 %copy-start.7 = (s32[16,1]{0,1:T(1,128)S(1)}, s32[16,1]{0,1:T(1,128)}, u32[]{:S(2)}) copy-start(s32[16,1]{0,1:T(1,128)} %constant.136) | copy-start | bytes 196
  61.5 10.3 %collective-permute-start.3 = (f32[80,152]{1,0:T(8,128)S(1)}, f32[80,152]{1,0:T(8,128)S(1)}, u32[]{:S(2)}, u32[]{:S(2)}) collective-permute-start(f32[80,152]{1,0:T(8,128)S(1)} %slice.55), channel_id=1, source_target_pairs={{0,3},{1,0},{2,1},{3,2},{4,7},{5,4},{6,5},{7,6},{8,11},{9,8},{10,9... | collective-permute-start | bytes 145928 | tf_op jit(solution)/shard_map/ppermute | solution.py:24
  73.7 8.9 %collective-permute-start.5 = (f32[80,1024]{1,0:T(8,128)S(1)}, f32[80,1024]{1,0:T(8,128)S(1)}, u32[]{:S(2)}, u32[]{:S(2)}) collective-permute-start(f32[80,1024]{1,0:T(8,128)S(1)} %bitcast_add_fusion.refs_0_), channel_id=1, source_target_pairs={{0,128},{128,384},{384,256},{256,0},{1,129},{129,385},{385,257},{2... | collective-permute-start | bytes 983048 | tf_op jit(solution)/shard_map/ppermute | solution.py:88
  82.6 12.9 %collective-permute-start.6 = (f32[80,1024]{1,0:T(8,128)S(1)}, f32[80,1024]{1,0:T(8,128)S(1)}, u32[]{:S(2)}, u32[]{:S(2)}) collective-permute-start(f32[80,1024]{1,0:T(8,128)S(1)} %collective-permute-done.5.refs_1_), channel_id=1, source_target_pairs={{0,128},{128,384},{384,256},{256,0},{1,129},{129,385},{385,257},{2... | collective-permute-start | bytes 983048 | tf_op jit(solution)/shard_map/ppermute | solution.py:88
  89.0 16.3 %collective-permute-start.8 = (f32[160,1024]{1,0:T(8,128)S(1)}, f32[160,1024]{1,0:T(8,128)S(1)}, u32[]{:S(2)}, u32[]{:S(2)}) collective-permute-start(f32[160,1024]{1,0:T(8,128)S(1)} %pad_maximum_fusion.3), channel_id=1, source_target_pairs={{0,32},{32,64},{64,96},{96,0},{1,33},{33,65},{65,97},{97,1},{2,34}... | collective-permute-start | bytes 1966088 | tf_op jit(solution)/shard_map/ppermute | solution.py:24
  92.1 14.8 %collective-permute-start.9 = (f32[160,1024]{1,0:T(8,128)S(1)}, f32[160,1024]{1,0:T(8,128)S(1)}, u32[]{:S(2)}, u32[]{:S(2)}) collective-permute-start(f32[160,1024]{1,0:T(8,128)S(1)} %pad_maximum_fusion.3), channel_id=1, source_target_pairs={{0,96},{32,0},{64,32},{96,64},{1,97},{33,1},{65,33},{97,65},{2,98}... | collective-permute-start | bytes 1966088 | tf_op jit(solution)/shard_map/ppermute | solution.py:24
  95.5 11.4 %collective-permute-start.7 = (f32[80,1024]{1,0:T(8,128)S(1)}, f32[80,1024]{1,0:T(8,128)S(1)}, u32[]{:S(2)}, u32[]{:S(2)}) collective-permute-start(f32[80,1024]{1,0:T(8,128)S(1)} %collective-permute-done.6.refs_2_), channel_id=1, source_target_pairs={{0,128},{128,384},{384,256},{256,0},{1,129},{129,385},{385,257},{2... | collective-permute-start | bytes 983048 | tf_op jit(solution)/shard_map/ppermute | solution.py:88
  108.5 27.2 %collective-permute-start.10 = (f32[240,1024]{1,0:T(8,128)}, f32[240,1024]{1,0:T(8,128)}, u32[]{:S(2)}, u32[]{:S(2)}) collective-permute-start(f32[240,1024]{1,0:T(8,128)} %get-tuple-element.18), channel_id=1, source_target_pairs={{0,32},{32,64},{64,96},{96,0},{1,33},{33,65},{65,97},{97,1},{2,34}... | collective-permute-start | bytes 2949128 | tf_op jit(solution)/shard_map/ppermute | solution.py:24
  111.6 28.2 %collective-permute-start.11 = (f32[240,1024]{1,0:T(8,128)}, f32[240,1024]{1,0:T(8,128)}, u32[]{:S(2)}, u32[]{:S(2)}) collective-permute-start(f32[240,1024]{1,0:T(8,128)} %get-tuple-element.17), channel_id=1, source_target_pairs={{0,96},{32,0},{64,32},{96,64},{1,97},{33,1},{65,33},{97,65},{2,98}... | collective-permute-start | bytes 2949128 | tf_op jit(solution)/shard_map/ppermute | solution.py:24
  133.1 11.1 %collective-permute-start.4 = (f32[152,1280]{1,0:T(8,128)S(1)}, f32[152,1280]{1,0:T(8,128)S(1)}, u32[]{:S(2)}, u32[]{:S(2)}) collective-permute-start(f32[152,1280]{1,0:T(8,128)S(1)} %get-tuple-element.10), channel_id=1, source_target_pairs={{0,16},{16,0},{1,17},{17,1},{2,18},{18,2},{3,19},{19,3},{4,20},{20... | collective-permute-start | bytes 2334728 | tf_op jit(solution)/shard_map/ppermute | solution.py:128
  136.7 12.0 %collective-permute-start.12 = (f32[80,1024]{1,0:T(8,128)S(1)}, f32[80,1024]{1,0:T(8,128)S(1)}, u32[]{:S(2)}, u32[]{:S(2)}) collective-permute-start(f32[80,1024]{1,0:T(8,128)S(1)} %slice.58), channel_id=1, source_target_pairs={{0,32},{32,64},{64,96},{96,0},{1,33},{33,65},{65,97},{97,1},{2,34}... | collective-permute-start | bytes 983048 | tf_op jit(solution)/shard_map/ppermute | solution.py:24
  140.8 10.9 %collective-permute-start.13 = (f32[80,1024]{1,0:T(8,128)S(1)}, f32[80,1024]{1,0:T(8,128)S(1)}, u32[]{:S(2)}, u32[]{:S(2)}) collective-permute-start(f32[80,1024]{1,0:T(8,128)S(1)} %slice.59), channel_id=1, source_target_pairs={{0,96},{32,0},{64,32},{96,64},{1,97},{33,1},{65,33},{97,65},{2,98}... | collective-permute-start | bytes 983048 | tf_op jit(solution)/shard_map/ppermute | solution.py:24
  151.7 7.2 %copy-start.6 = (s32[152,2]{0,1:T(2,128)S(1)}, s32[152,2]{0,1:T(2,128)}, u32[]{:S(2)}) copy-start(s32[152,2]{0,1:T(2,128)} %param.10) | copy-start | bytes 3652
  155.8 4.7 %collective-permute-start.14 = (f32[152,1024]{1,0:T(8,128)S(1)}, f32[152,1024]{1,0:T(8,128)S(1)}, u32[]{:S(2)}, u32[]{:S(2)}) collective-permute-start(f32[152,1024]{1,0:T(8,128)S(1)} %get-tuple-element.12), channel_id=1, source_target_pairs={{0,16},{16,0},{1,17},{17,1},{2,18},{18,2},{3,19},{19,3},{4,20},{20... | collective-permute-start | bytes 1867784 | tf_op jit(solution)/shard_map/ppermute | solution.py:140
  (2 other events, 2.6 us)
Sparse Core Ops, SparseCore 0:
  72.9 48.5 all-gather.1

commit v3 on v2

--- a/solution.py
+++ b/solution.py
@@ -20,36 +20,67 @@
     return [(i, (i + by) % n) for i in range(n)]
 
 
-def around(up, down, axis):
-    return lax.ppermute(up, axis, shift(4, 1)), lax.ppermute(down, axis, shift(4, -1))
-
-
-def symmetrized(integrals):
-    rows = integrals.shape[0]
-    here = integrals.shape[1] // NA
-    ranks = NA // here
-    sent = integrals.reshape(rows, here, ranks, here).transpose(2, 1, 3, 0).reshape(ranks, here, here * rows)
-    got = lax.all_to_all(sent, VIR, split_axis=0, concat_axis=0, tiled=True)
-    swapped = got.reshape(NA, here * rows).T.reshape(here, rows, NA)
-    return integrals + swapped.transpose(1, 0, 2).reshape(integrals.shape)
-
-
-def antisym_kernel(block, base_ref, other_ref, tau_ref, mine_ref, theirs_ref, rows_ref):
+def pack_kernel(turned_ref, packed_ref):
+    rows, pairs = turned_ref.shape
+    tail = pairs - 128
+    step = packed_ref.shape[0] - rows
+    packed_ref[:rows, :] = turned_ref[:, :128]
+    parts = [turned_ref[j : j + step, 128:] for j in range(0, rows, step)]
+    parts.append(jnp.zeros((step, 128 - tail * len(parts)), jnp.float32))
+    packed_ref[rows:, :] = jnp.concatenate(parts, axis=1)
+
+
+def symmetrize_kernel(integrals_ref, got_ref, out_ref, turned_ref):
+    ranks, here = got_ref.shape[0], integrals_ref.shape[1] // NA
+    rows = integrals_ref.shape[0]
+    for t in range(here * rows // 128):
+        block = got_ref[:, t * here : (t + 1) * here, :].reshape(ranks * here, 128)
+        turned_ref[t * 128 : (t + 1) * 128, :] = block.T
+    for a in range(here):
+        columns = slice(a * NA, (a + 1) * NA)
+        out_ref[:, columns] = integrals_ref[:, columns] + turned_ref[a * rows : (a + 1) * rows, :]
+
+
+def copies_kernel(*refs):
+    copies_ref = refs[-1]
+    at = 0
+    for piece in refs[:-1]:
+        for i in range(copies_ref.shape[0]):
+            copies_ref[i, at : at + piece.shape[0], :] = piece[...]
+        at += piece.shape[0]
+
+
+def antisym_kernel(block, columns_k, base_ref, other_ref, tau_ref, mine_ref, theirs_ref, head_ref, tail_ref, rows_ref, ends_ref):
     total = rows_ref.shape[0]
+    pairs = mine_ref.shape[0]
+    ranks = total // columns_k
+    per = tau_ref.shape[0] // ranks
+    step = per - columns_k
+    for r in range(ranks):
+        head_ref[r * columns_k : (r + 1) * columns_k, :] = tau_ref[r * per : r * per + columns_k, :]
+        packed = tau_ref[r * per + columns_k : (r + 1) * per, :]
+        for j in range(columns_k // step):
+            turned = packed if j == 0 else pltpu.roll(packed, 128 - j * (pairs - 128), 1)
+            tail_ref[r * columns_k + j * step : r * columns_k + (j + 1) * step, :] = turned
 
     def one(b, _):
         at = pl.multiple_of(b * block, 8)
         for r in range(block):
-            rows_ref[pl.ds(at + r, 1), :] = tau_ref[pl.ds(other_ref[at + r], 1), :]
-        here = tau_ref[pl.ds(pl.multiple_of(base_ref[b], 8), block), :]
-        rows_ref[pl.ds(at, block), :] = here - rows_ref[pl.ds(at, block), :]
+            k = other_ref[at + r]
+            rows_ref[pl.ds(at + r, 1), :] = head_ref[pl.ds(k, 1), :]
+            ends_ref[pl.ds(at + r, 1), :] = tail_ref[pl.ds(k, 1), :]
+        here = pl.ds(pl.multiple_of(base_ref[b], 8), block)
+        rows_ref[pl.ds(at, block), :] = head_ref[here, :] - rows_ref[pl.ds(at, block), :]
+        ends_ref[pl.ds(at, block), :] = tail_ref[here, :] - ends_ref[pl.ds(at, block), :]
         return 0
 
     lax.fori_loop(0, total // block, one, 0)
     half = total // 2
     for j in range(0, half, 128):
-        mine_ref[:, j : j + 128] = rows_ref[j : j + 128, :].T
-        theirs_ref[:, j : j + 128] = rows_ref[half + j : half + j + 128, :].T
+        mine_ref[:128, j : j + 128] = rows_ref[j : j + 128, :].T
+        mine_ref[128:, j : j + 128] = ends_ref[j : j + 128, :].T[: pairs - 128]
+        theirs_ref[:128, j : j + 128] = rows_ref[half + j : half + j + 128, :].T
+        theirs_ref[128:, j : j + 128] = ends_ref[half + j : half + j + 128, :].T[: pairs - 128]
 
 
 def product_kernel(counts, mine_ref, theirs_ref, *refs):
@@ -75,33 +106,62 @@
         other_ref[:, n : n + 256] = total[pairs:]
 
 
+def around(up, down, axis):
+    return lax.ppermute(up, axis, shift(4, 1)), lax.ppermute(down, axis, shift(4, -1))
+
+
 def body(amplitudes, integrals, pair_list, partner):
     rows_k, columns = integrals.shape
     pairs, columns_k = amplitudes.shape
     slab = partner.shape[0]
-    x, core = lax.axis_index("x"), lax.axis_index("c")
-    zh = lax.axis_index("zh")
+    x, core, zh = lax.axis_index("x"), lax.axis_index("c"), lax.axis_index("zh")
     ring_place = jnp.array([0, 1, 3, 2], jnp.int32)[lax.axis_index("zl")]
 
-    s = [symmetrized(integrals)]
+    lanes = 128 // (pairs - 128)
+    packed_rows = columns_k + columns_k // lanes
+    packed = pl.pallas_call(
+        pack_kernel,
+        out_shape=jax.ShapeDtypeStruct((packed_rows, 128), jnp.float32),
+        in_specs=[VMEM],
+        out_specs=VMEM,
+        name="pack",
+    )(amplitudes.T)
+    left, right = around(packed, packed, "zh")
+    half = packed_rows // 2
+    far = around(left[:half], right[half:], "zh")
+    copies = pl.pallas_call(
+        copies_kernel,
+        out_shape=jax.ShapeDtypeStruct((4, 4 * packed_rows, 128), jnp.float32),
+        in_specs=[VMEM] * 5,
+        out_specs=VMEM,
+        name="copies",
+    )(packed, left, right, *far)
+    tau = lax.all_to_all(copies, "y", split_axis=0, concat_axis=0, tiled=True).reshape(-1, 128)
+
+    here = columns // NA
+    ranks = NA // here
+    tiles = here * rows_k // 128
+    blocks = integrals.reshape(rows_k, here, ranks, here).transpose(2, 1, 3, 0).reshape(ranks, here, tiles, 128)
+    sent = blocks.transpose(0, 2, 1, 3).reshape(ranks, tiles * here, 128)
+    got = lax.all_to_all(sent, VIR, split_axis=0, concat_axis=0, tiled=True)
+    start = pl.pallas_call(
+        symmetrize_kernel,
+        out_shape=jax.ShapeDtypeStruct((rows_k, columns), jnp.float32),
+        in_specs=[VMEM] * 2,
+        out_specs=VMEM,
+        scratch_shapes=[pltpu.VMEM((tiles * 128, 128), jnp.float32)],
+        name="symmetrize",
+    )(integrals, got)
+
+    s = [start]
     for _ in range(3):
         s.append(lax.ppermute(s[-1], "zl", [(RING[i], RING[(i + 1) % 4]) for i in range(4)]))
-    first = jnp.concatenate(s[:2], axis=0)
-    la, ra = around(first, first, "x")
-    lb, rb = around(
-        jnp.concatenate([s[2], s[3], la[:rows_k]], axis=0), jnp.concatenate([s[2], s[3], ra[rows_k:]], axis=0), "x"
-    )
-    lc, rc = around(lb[:rows_k], rb[rows_k : 2 * rows_k], "x")
-    pieces = s + [la, ra, lb, rb, lc, rc]
-    order = [(0, 0), (1, 0), (2, 0), (3, 0), (0, -1), (1, -1), (0, 1), (1, 1)]
-    order += [(2, -1), (3, -1), (0, 2), (2, 1), (3, 1), (1, 2), (2, 2), (3, 2)]
-
-    turned = amplitudes.T
-    half = columns_k // 2
-    left, right = around(turned, turned, "zh")
-    far_top, far_low = around(left[:half], right[half:], "zh")
-    by_zh = jnp.concatenate([turned, left, right, far_top, far_low], axis=0)
-    tau = lax.all_gather(by_zh, "y", axis=0, tiled=True)
+    pieces, order = [], []
+    for i in (0, 2):
+        part = jnp.concatenate(s[i : i + 2], axis=0)
+        left, right = around(part, part, "x")
+        pieces += [part, left, right, *around(left[:rows_k], right[rows_k:], "x")]
+        order += [(i, 0), (i + 1, 0), (i, -1), (i + 1, -1), (i, 1), (i + 1, 1), (i, 2), (i + 1, 2)]
 
     slot = jnp.array(SLOT, jnp.int32)
 
@@ -113,18 +173,17 @@
     zs = jnp.array(RING, jnp.int32)[(ring_place - steps[:, 0]) % 4]
     chunk = (zs * 4 + (x + steps[:, 1]) % 4) * 2
     chunk = jnp.concatenate([chunk + core, chunk + 1 - core])
-    base = place(chunk * rows_k)
     other = place(partner).reshape(-1, rows_k).at[chunk].get(mode="promise_in_bounds").reshape(-1)
     mine, theirs = pl.pallas_call(
-        functools.partial(antisym_kernel, rows_k),
+        functools.partial(antisym_kernel, rows_k, columns_k),
         out_shape=[jax.ShapeDtypeStruct((pairs, slab // 2), jnp.float32)] * 2,
         in_specs=[SMEM, SMEM, VMEM],
         out_specs=[VMEM] * 2,
-        scratch_shapes=[pltpu.VMEM((slab, pairs), jnp.float32)],
+        scratch_shapes=[pltpu.VMEM((slab, 128), jnp.float32)] * 4,
         compiler_params=pltpu.CompilerParams(vmem_limit_bytes=16 * 2**20),
         cost_estimate=pl.CostEstimate(flops=slab * pairs, bytes_accessed=3 * slab * pairs * 4, transcendentals=0),
         name="antisym",
-    )(base, other, tau)
+    )(place(chunk * rows_k), other, tau)
     theirs = lax.ppermute(theirs, "c", shift(2, 1))
 
     own, back = pl.pallas_call(

time: 171 us -> 148 us (0.87)
  waiting for transfers between devices: 54.8 us -> 24 us
  starting transfers between devices: 73 us -> 90.2 us
  between operations: 13.8 us -> 0.47 us
  local copies, waits for them, and re-layouts: 9.24 us -> 12.4 us
    ppermute x5 -> x6, waiting for transfers between devices: 23.1 us -> 8.98 us  [around(): lax.ppermute(down, axis, shift(4, -1))]
    ppermute x5 -> x6, waiting for transfers between devices: 17.4 us -> 6.27 us  [around(): lax.ppermute(up, axis, shift(4, 1))]
    ppermute x5 -> x6, starting transfers between devices: 14.2 us -> 21.8 us  [around(): lax.ppermute(down, axis, shift(4, -1))]
    all_gather x1 -> x0, waiting for transfers between devices: 6.38 us -> none  [body(): tau = lax.all_gather(by_zh, 'y', axis=0, tiled=True)]
    all_to_all x1 -> x2, starting transfers between devices: 18.5 us -> 23 us  [the longest x1 18.5 us: body(): got = lax.all_to_all(sent, VIR, split_axis=0, concat_axis=0, tiled=True)]
    ppermute x1, starting transfers between devices: 2.58 us -> 6.69 us  [body(): theirs = lax.ppermute(theirs, 'c', shift(2, 1))]
    unnamed x24 -> x31, local copies, waits for them, and re-layouts: 3.95 us -> 5.1 us
    pallas_call x1 -> x4, Pallas kernels: 9.8 us -> 10.8 us  [the longest x1 4.87 us: body(): pl.pallas_call(functools.partial(antisym_kernel, rows_k, columns_k), out_...]
  transfers between devices with their start and end apart: 17 -> 19, of which waited for: 11 -> 8; matrix products, arithmetic and copies ran while one was open for 4% -> 8% of each run, Pallas kernels for 6% -> 7%
where the time goes in v3:
time: 148 us; the launch traced here: 146 us
  starting transfers between devices  90.2 us (61%)
  waiting for transfers between devices  24 us (16%)
  Pallas kernels  14.9 us (10%)
  local copies, waits for them, and re-layouts  12.4 us (8%)
  other arithmetic  4.25 us (3%)
    ppermute x6, starting transfers between devices, around(): lax.ppermute(down, axis, shift(4, -1))  21.8 us
    ppermute x6, starting transfers between devices, around(): lax.ppermute(up, axis, shift(4, 1))  21.2 us
    all_to_all x1, starting transfers between devices, body(): got = lax.all_to_all(sent, VIR, split_axis=0, concat_axis=0, tiled=True)  18.5 us
    ppermute x3, starting transfers between devices, body(): lax.ppermute(s[-1], 'zl', [(RING[i], RING[(i + 1) % 4]) for i in range(4)])  13.7 us
    ppermute x6, waiting for transfers between devices, around(): lax.ppermute(down, axis, shift(4, -1))  8.98 us
    ppermute x3, waiting for transfers between devices, body(): lax.ppermute(s[-1], 'zl', [(RING[i], RING[(i + 1) % 4]) for i in range(4)])  7.07 us
    ppermute x1, starting transfers between devices, body(): theirs = lax.ppermute(theirs, 'c', shift(2, 1))  6.69 us
    ppermute x6, waiting for transfers between devices, around(): lax.ppermute(up, axis, shift(4, 1))  6.27 us
  transfers between devices with their start and end apart: 19, of which 8 were waited for; matrix products, arithmetic and copies ran while one was open for 8% of the time, Pallas kernels for 7%

profile of v3, /device:TPU:1, one launch (start us, length us, event | category | flops | bytes accessed | tf_op | source)
XLA Modules:
  0.0 146.2 jit_solution(7154038225411405807)
XLA Ops:
  2.4 18.5 %all-to-all-start.1 = ((f32[16,40,128]{2,1,0:T(8,128)}), f32[16,40,128]{2,1,0:T(8,128)S(1)}, u32[]{:S(2)}, u32[]{:S(2)}) async-start(f32[16,40,128]{2,1,0:T(8,128)} %bitcast.43), calls=%async_computation.1 | async-start | bytes 655360 | tf_op jit(solution)/shard_map/all_to_all | solution.py:146
  23.3 7.2 %collective-permute-start = (f32[192,128]{1,0:T(8,128)}, f32[192,128]{1,0:T(8,128)S(1)}, u32[]{:S(2)}, u32[]{:S(2)}) collective-permute-start(f32[192,128]{1,0:T(8,128)} %pack.1.refs_0_), channel_id=1, source_target_pairs={{0,1},{1,2},{2,3},{3,0},{4,5},{5,6},{6,7},{7,4},{8,9},{9,10},{10,1... | collective-permute-start | bytes 294920 | tf_op jit(solution)/shard_map/ppermute | solution.py:110
  30.5 2.0 %collective-permute-start.1 = (f32[192,128]{1,0:T(8,128)}, f32[192,128]{1,0:T(8,128)S(1)}, u32[]{:S(2)}, u32[]{:S(2)}) collective-permute-start(f32[192,128]{1,0:T(8,128)} %pack.1.refs_0_), channel_id=1, source_target_pairs={{0,3},{1,0},{2,1},{3,2},{4,7},{5,4},{6,5},{7,6},{8,11},{9,8},{10,9... | collective-permute-start | bytes 294920 | tf_op jit(solution)/shard_map/ppermute | solution.py:110
  34.4 2.0 %collective-permute-done.refs_1_ = f32[192,128]{1,0:T(8,128)S(1)} collective-permute-done((f32[192,128]{1,0:T(8,128)}, f32[192,128]{1,0:T(8,128)S(1)}, u32[]{:S(2)}, u32[]{:S(2)}) %collective-permute-start) | collective-permute-done | bytes 98336 | tf_op jit(solution)/shard_map/ppermute | solution.py:110
  36.4 5.2 %collective-permute-start.2 = (f32[96,128]{1,0:T(8,128)S(1)}, f32[96,128]{1,0:T(8,128)S(1)}, u32[]{:S(2)}, u32[]{:S(2)}) collective-permute-start(f32[96,128]{1,0:T(8,128)S(1)} %slice.54), channel_id=1, source_target_pairs={{0,1},{1,2},{2,3},{3,0},{4,5},{5,6},{6,7},{7,4},{8,9},{9,10},{10,1... | collective-permute-start | bytes 147464 | tf_op jit(solution)/shard_map/ppermute | solution.py:110
  41.6 6.2 %collective-permute-done.1.refs_2_ = f32[192,128]{1,0:T(8,128)S(1)} collective-permute-done((f32[192,128]{1,0:T(8,128)}, f32[192,128]{1,0:T(8,128)S(1)}, u32[]{:S(2)}, u32[]{:S(2)}) %collective-permute-start.1) | collective-permute-done | bytes 98336 | tf_op jit(solution)/shard_map/ppermute | solution.py:110
  47.8 2.7 %collective-permute-start.3 = (f32[96,128]{1,0:T(8,128)S(1)}, f32[96,128]{1,0:T(8,128)S(1)}, u32[]{:S(2)}, u32[]{:S(2)}) collective-permute-start(f32[96,128]{1,0:T(8,128)S(1)} %slice.55), channel_id=1, source_target_pairs={{0,3},{1,0},{2,1},{3,2},{4,7},{5,4},{6,5},{7,6},{8,11},{9,8},{10,9... | collective-permute-start | bytes 147464 | tf_op jit(solution)/shard_map/ppermute | solution.py:110
  53.3 2.4 %collective-permute-start.5 = (f32[80,1024]{1,0:T(8,128)}, f32[80,1024]{1,0:T(8,128)S(1)}, u32[]{:S(2)}, u32[]{:S(2)}) collective-permute-start(f32[80,1024]{1,0:T(8,128)} %symmetrize.1), channel_id=1, source_target_pairs={{0,128},{128,384},{384,256},{256,0},{1,129},{129,385},{385,257},{2... | collective-permute-start | bytes 983048 | tf_op jit(solution)/shard_map/ppermute | solution.py:158
  57.3 2.3 %copies.1 = f32[4,768,128]{2,1,0:T(8,128)} custom-call(f32[192,128]{1,0:T(8,128)} %pack.1.refs_0_, f32[192,128]{1,0:T(8,128)} %copy-done.3, f32[192,128]{1,0:T(8,128)} %copy-done.4, f32[96,128]{1,0:T(8,128)} %copy-done.6, f32[96,128]{1,0:T(8,128)} %copy-done.7), custom_call_target="tpu_custom_call" | custom-call | tf_op jit(solution)/shard_map/copies/pallas_call | solution.py:132
  59.6 4.5 %all-to-all-start = ((f32[4,768,128]{2,1,0:T(8,128)}), f32[4,768,128]{2,1,0:T(8,128)S(1)}, u32[]{:S(2)}, u32[]{:S(2)}) async-start(f32[4,768,128]{2,1,0:T(8,128)} %copies.1), calls=%async_computation | async-start | bytes 3145728 | tf_op jit(solution)/shard_map/all_to_all | solution.py:139
  64.7 3.2 %collective-permute-done.5 = f32[80,1024]{1,0:T(8,128)S(1)} collective-permute-done((f32[80,1024]{1,0:T(8,128)}, f32[80,1024]{1,0:T(8,128)S(1)}, u32[]{:S(2)}, u32[]{:S(2)}) %collective-permute-start.5) | collective-permute-done | bytes 327712 | tf_op jit(solution)/shard_map/ppermute | solution.py:158
  67.9 7.1 %collective-permute-start.10 = (f32[80,1024]{1,0:T(8,128)S(1)}, f32[80,1024]{1,0:T(8,128)}, u32[]{:S(2)}, u32[]{:S(2)}) collective-permute-start(f32[80,1024]{1,0:T(8,128)S(1)} %collective-permute-done.5), channel_id=1, source_target_pairs={{0,128},{128,384},{384,256},{256,0},{1,129},{129,385},{385,257},{2... | collective-permute-start | bytes 983048 | tf_op jit(solution)/shard_map/ppermute | solution.py:158
  75.8 3.8 %collective-permute-done.10 = f32[80,1024]{1,0:T(8,128)} collective-permute-done((f32[80,1024]{1,0:T(8,128)S(1)}, f32[80,1024]{1,0:T(8,128)}, u32[]{:S(2)}, u32[]{:S(2)}) %collective-permute-start.10) | collective-permute-done | bytes 327712 | tf_op jit(solution)/shard_map/ppermute | solution.py:158
  79.6 4.2 %collective-permute-start.11 = (f32[80,1024]{1,0:T(8,128)}, f32[80,1024]{1,0:T(8,128)S(1)}, u32[]{:S(2)}, u32[]{:S(2)}) collective-permute-start(f32[80,1024]{1,0:T(8,128)} %collective-permute-done.10), channel_id=1, source_target_pairs={{0,128},{128,384},{384,256},{256,0},{1,129},{129,385},{385,257},{2... | collective-permute-start | bytes 983048 | tf_op jit(solution)/shard_map/ppermute | solution.py:158
  84.0 3.1 %collective-permute-start.6 = (f32[160,1024]{1,0:T(8,128)S(1)}, f32[160,1024]{1,0:T(8,128)S(1)}, u32[]{:S(2)}, u32[]{:S(2)}) collective-permute-start(f32[160,1024]{1,0:T(8,128)S(1)} %pad_maximum_fusion.refs_0_), channel_id=1, source_target_pairs={{0,32},{32,64},{64,96},{96,0},{1,33},{33,65},{65,97},{97,1},{2,34}... | collective-permute-start | bytes 1966088 | tf_op jit(solution)/shard_map/ppermute | solution.py:110
  87.1 3.4 %collective-permute-start.7 = (f32[160,1024]{1,0:T(8,128)S(1)}, f32[160,1024]{1,0:T(8,128)S(1)}, u32[]{:S(2)}, u32[]{:S(2)}) collective-permute-start(f32[160,1024]{1,0:T(8,128)S(1)} %pad_maximum_fusion.refs_0_), channel_id=1, source_target_pairs={{0,96},{32,0},{64,32},{96,64},{1,97},{33,1},{65,33},{97,65},{2,98}... | collective-permute-start | bytes 1966088 | tf_op jit(solution)/shard_map/ppermute | solution.py:110
  94.9 4.6 %collective-permute-start.13 = (f32[160,1024]{1,0:T(8,128)}, f32[160,1024]{1,0:T(8,128)}, u32[]{:S(2)}, u32[]{:S(2)}) collective-permute-start(f32[160,1024]{1,0:T(8,128)} %constant_dynamic-update-slice_fusion.refs_5_), channel_id=1, source_target_pairs={{0,96},{32,0},{64,32},{96,64},{1,97},{33,1},{65,33},{97,65},{2,98}... | collective-permute-start | bytes 1966088 | tf_op jit(solution)/shard_map/ppermute | solution.py:110
  103.0 4.9 %antisym.1 = (f32[152,1280]{1,0:T(8,128)S(1)}, f32[152,1280]{1,0:T(8,128)S(1)}) custom-call(s32[32]{0:T(128)S(1)} %fusion.11.base_ref, s32[2560]{0:T(1024)S(1)} %reshape.219.other_ref, f32[3072,128]{1,0:T(8,128)S(1)} %bitcast.44), custom_call_target="tpu_custom_call" | custom-call | flops 389120 | bytes 4669440 | tf_op jit(solution)/shard_map/antisym/pallas_call | solution.py:177
  107.8 6.7 %collective-permute-start.4 = (f32[152,1280]{1,0:T(8,128)S(1)}, f32[152,1280]{1,0:T(8,128)S(1)}, u32[]{:S(2)}, u32[]{:S(2)}) collective-permute-start(f32[152,1280]{1,0:T(8,128)S(1)} %get-tuple-element.10), channel_id=1, source_target_pairs={{0,16},{16,0},{1,17},{17,1},{2,18},{18,2},{3,19},{19,3},{4,20},{20... | collective-permute-start | bytes 2334728 | tf_op jit(solution)/shard_map/ppermute | solution.py:187
  116.6 4.6 %collective-permute-start.9 = (f32[80,1024]{1,0:T(8,128)S(1)}, f32[80,1024]{1,0:T(8,128)S(1)}, u32[]{:S(2)}, u32[]{:S(2)}) collective-permute-start(f32[80,1024]{1,0:T(8,128)S(1)} %slice.57), channel_id=1, source_target_pairs={{0,96},{32,0},{64,32},{96,64},{1,97},{33,1},{65,33},{97,65},{2,98}... | collective-permute-start | bytes 983048 | tf_op jit(solution)/shard_map/ppermute | solution.py:110
  125.1 4.6 %collective-permute-start.15 = (f32[80,1024]{1,0:T(8,128)S(1)}, f32[80,1024]{1,0:T(8,128)S(1)}, u32[]{:S(2)}, u32[]{:S(2)}) collective-permute-start(f32[80,1024]{1,0:T(8,128)S(1)} %slice.59), channel_id=1, source_target_pairs={{0,96},{32,0},{64,32},{96,64},{1,97},{33,1},{65,33},{97,65},{2,98}... | collective-permute-start | bytes 983048 | tf_op jit(solution)/shard_map/ppermute | solution.py:110
  129.7 4.2 %collective-permute-done.14.refs_8_ = f32[80,1024]{1,0:T(8,128)S(1)} collective-permute-done((f32[80,1024]{1,0:T(8,128)S(1)}, f32[80,1024]{1,0:T(8,128)S(1)}, u32[]{:S(2)}, u32[]{:S(2)}) %collective-permute-start.14) | collective-permute-done | bytes 327712 | tf_op jit(solution)/shard_map/ppermute | solution.py:110
  135.8 4.1 %product.1 = (f32[152,1024]{1,0:T(8,128)S(1)}, f32[152,1024]{1,0:T(8,128)S(1)}) custom-call(f32[152,1280]{1,0:T(8,128)S(1)} %get-tuple-element.9.mine_ref, f32[152,1280]{1,0:T(8,128)S(1)} %collective-permute-done.4.theirs_ref, f32[160,1024]{1,0:T(8,128)S(1)} %pad_maximum_fusion.refs_0_, f32[160,1024]{1,0:T(8,128)S(1)} %collective-permute-done.6.refs_1_, ...), custom_call_target="tpu_custom_call" | custom-call | flops 2390753280 | bytes 8388608 | tf_op jit(solution)/shard_map/product/pallas_call | solution.py:189
  139.9 3.7 %collective-permute-start.16 = (f32[152,1024]{1,0:T(8,128)S(1)}, f32[152,1024]{1,0:T(8,128)S(1)}, u32[]{:S(2)}, u32[]{:S(2)}) collective-permute-start(f32[152,1024]{1,0:T(8,128)S(1)} %get-tuple-element.12), channel_id=1, source_target_pairs={{0,16},{16,0},{1,17},{17,1},{2,18},{18,2},{3,19},{19,3},{4,20},{20... | collective-permute-start | bytes 1867784 | tf_op jit(solution)/shard_map/ppermute | solution.py:199
  (77 shorter events, 30.5 us)
Async XLA Ops:
  1.2 31.3 %copy-start = (s32[4]{0:T(128)S(1)}, s32[4]{0:T(128)}, u32[]{:S(2)}) copy-start(s32[4]{0:T(128)} %constant.129.clone) | copy-start | bytes 52
  1.2 31.9 %copy-start.13 = (s32[16,1]{0,1:T(1,128)S(1)}, s32[16,1]{0,1:T(1,128)}, u32[]{:S(2)}) copy-start(s32[16,1]{0,1:T(1,128)} %constant.137) | copy-start | bytes 196
  1.2 32.5 %copy-start.8 = (s32[2560]{0:T(1024)S(1)}, s32[2560]{0:T(1024)}, u32[]{:S(2)}) copy-start(s32[2560]{0:T(1024)} %param.11) | copy-start | bytes 30724
  2.4 53.3 %copy-start.10 = (s32[16,1]{0,1:T(1,128)S(1)}, s32[16,1]{0,1:T(1,128)}, u32[]{:S(2)}) copy-start(s32[16,1]{0,1:T(1,128)} %constant.136) | copy-start | bytes 196
  2.4 48.2 %all-to-all-start.1 = ((f32[16,40,128]{2,1,0:T(8,128)}), f32[16,40,128]{2,1,0:T(8,128)S(1)}, u32[]{:S(2)}, u32[]{:S(2)}) async-start(f32[16,40,128]{2,1,0:T(8,128)} %bitcast.43), calls=%async_computation.1 | async-start | bytes 655360 | tf_op jit(solution)/shard_map/all_to_all | solution.py:146
  23.3 13.1 %collective-permute-start = (f32[192,128]{1,0:T(8,128)}, f32[192,128]{1,0:T(8,128)S(1)}, u32[]{:S(2)}, u32[]{:S(2)}) collective-permute-start(f32[192,128]{1,0:T(8,128)} %pack.1.refs_0_), channel_id=1, source_target_pairs={{0,1},{1,2},{2,3},{3,0},{4,5},{5,6},{6,7},{7,4},{8,9},{9,10},{10,1... | collective-permute-start | bytes 294920 | tf_op jit(solution)/shard_map/ppermute | solution.py:110
  30.5 17.3 %collective-permute-start.1 = (f32[192,128]{1,0:T(8,128)}, f32[192,128]{1,0:T(8,128)S(1)}, u32[]{:S(2)}, u32[]{:S(2)}) collective-permute-start(f32[192,128]{1,0:T(8,128)} %pack.1.refs_0_), channel_id=1, source_target_pairs={{0,3},{1,0},{2,1},{3,2},{4,7},{5,4},{6,5},{7,6},{8,11},{9,8},{10,9... | collective-permute-start | bytes 294920 | tf_op jit(solution)/shard_map/ppermute | solution.py:110
  36.4 19.2 %collective-permute-start.2 = (f32[96,128]{1,0:T(8,128)S(1)}, f32[96,128]{1,0:T(8,128)S(1)}, u32[]{:S(2)}, u32[]{:S(2)}) collective-permute-start(f32[96,128]{1,0:T(8,128)S(1)} %slice.54), channel_id=1, source_target_pairs={{0,1},{1,2},{2,3},{3,0},{4,5},{5,6},{6,7},{7,4},{8,9},{9,10},{10,1... | collective-permute-start | bytes 147464 | tf_op jit(solution)/shard_map/ppermute | solution.py:110
  47.8 8.8 %collective-permute-start.3 = (f32[96,128]{1,0:T(8,128)S(1)}, f32[96,128]{1,0:T(8,128)S(1)}, u32[]{:S(2)}, u32[]{:S(2)}) collective-permute-start(f32[96,128]{1,0:T(8,128)S(1)} %slice.55), channel_id=1, source_target_pairs={{0,3},{1,0},{2,1},{3,2},{4,7},{5,4},{6,5},{7,6},{8,11},{9,8},{10,9... | collective-permute-start | bytes 147464 | tf_op jit(solution)/shard_map/ppermute | solution.py:110
  53.3 14.7 %collective-permute-start.5 = (f32[80,1024]{1,0:T(8,128)}, f32[80,1024]{1,0:T(8,128)S(1)}, u32[]{:S(2)}, u32[]{:S(2)}) collective-permute-start(f32[80,1024]{1,0:T(8,128)} %symmetrize.1), channel_id=1, source_target_pairs={{0,128},{128,384},{384,256},{256,0},{1,129},{129,385},{385,257},{2... | collective-permute-start | bytes 983048 | tf_op jit(solution)/shard_map/ppermute | solution.py:158
  55.7 28.1 %copy-start.11 = (s32[16,1]{0,1:T(1,128)}, s32[16,1]{0,1:T(1,128)S(1)}, u32[]{:S(2)}) copy-start(s32[16,1]{0,1:T(1,128)S(1)} %get-tuple-element.13) | copy-start | bytes 196
  59.6 43.4 %all-to-all-start = ((f32[4,768,128]{2,1,0:T(8,128)}), f32[4,768,128]{2,1,0:T(8,128)S(1)}, u32[]{:S(2)}, u32[]{:S(2)}) async-start(f32[4,768,128]{2,1,0:T(8,128)} %copies.1), calls=%async_computation | async-start | bytes 3145728 | tf_op jit(solution)/shard_map/all_to_all | solution.py:139
  67.9 11.7 %collective-permute-start.10 = (f32[80,1024]{1,0:T(8,128)S(1)}, f32[80,1024]{1,0:T(8,128)}, u32[]{:S(2)}, u32[]{:S(2)}) collective-permute-start(f32[80,1024]{1,0:T(8,128)S(1)} %collective-permute-done.5), channel_id=1, source_target_pairs={{0,128},{128,384},{384,256},{256,0},{1,129},{129,385},{385,257},{2... | collective-permute-start | bytes 983048 | tf_op jit(solution)/shard_map/ppermute | solution.py:158
  79.6 12.6 %collective-permute-start.11 = (f32[80,1024]{1,0:T(8,128)}, f32[80,1024]{1,0:T(8,128)S(1)}, u32[]{:S(2)}, u32[]{:S(2)}) collective-permute-start(f32[80,1024]{1,0:T(8,128)} %collective-permute-done.10), channel_id=1, source_target_pairs={{0,128},{128,384},{384,256},{256,0},{1,129},{129,385},{385,257},{2... | collective-permute-start | bytes 983048 | tf_op jit(solution)/shard_map/ppermute | solution.py:158
  84.0 30.6 %collective-permute-start.6 = (f32[160,1024]{1,0:T(8,128)S(1)}, f32[160,1024]{1,0:T(8,128)S(1)}, u32[]{:S(2)}, u32[]{:S(2)}) collective-permute-start(f32[160,1024]{1,0:T(8,128)S(1)} %pad_maximum_fusion.refs_0_), channel_id=1, source_target_pairs={{0,32},{32,64},{64,96},{96,0},{1,33},{33,65},{65,97},{97,1},{2,34}... | collective-permute-start | bytes 1966088 | tf_op jit(solution)/shard_map/ppermute | solution.py:110
  87.1 29.4 %collective-permute-start.7 = (f32[160,1024]{1,0:T(8,128)S(1)}, f32[160,1024]{1,0:T(8,128)S(1)}, u32[]{:S(2)}, u32[]{:S(2)}) collective-permute-start(f32[160,1024]{1,0:T(8,128)S(1)} %pad_maximum_fusion.refs_0_), channel_id=1, source_target_pairs={{0,96},{32,0},{64,32},{96,64},{1,97},{33,1},{65,33},{97,65},{2,98}... | collective-permute-start | bytes 1966088 | tf_op jit(solution)/shard_map/ppermute | solution.py:110
  93.0 28.1 %collective-permute-start.12 = (f32[160,1024]{1,0:T(8,128)}, f32[160,1024]{1,0:T(8,128)}, u32[]{:S(2)}, u32[]{:S(2)}) collective-permute-start(f32[160,1024]{1,0:T(8,128)} %constant_dynamic-update-slice_fusion.refs_5_), channel_id=1, source_target_pairs={{0,32},{32,64},{64,96},{96,0},{1,33},{33,65},{65,97},{97,1},{2,34}... | collective-permute-start | bytes 1966088 | tf_op jit(solution)/shard_map/ppermute | solution.py:110
  94.9 29.2 %collective-permute-start.13 = (f32[160,1024]{1,0:T(8,128)}, f32[160,1024]{1,0:T(8,128)}, u32[]{:S(2)}, u32[]{:S(2)}) collective-permute-start(f32[160,1024]{1,0:T(8,128)} %constant_dynamic-update-slice_fusion.refs_5_), channel_id=1, source_target_pairs={{0,96},{32,0},{64,32},{96,64},{1,97},{33,1},{65,33},{97,65},{2,98}... | collective-permute-start | bytes 1966088 | tf_op jit(solution)/shard_map/ppermute | solution.py:110
  107.8 21.8 %collective-permute-start.4 = (f32[152,1280]{1,0:T(8,128)S(1)}, f32[152,1280]{1,0:T(8,128)S(1)}, u32[]{:S(2)}, u32[]{:S(2)}) collective-permute-start(f32[152,1280]{1,0:T(8,128)S(1)} %get-tuple-element.10), channel_id=1, source_target_pairs={{0,16},{16,0},{1,17},{17,1},{2,18},{18,2},{3,19},{19,3},{4,20},{20... | collective-permute-start | bytes 2334728 | tf_op jit(solution)/shard_map/ppermute | solution.py:187
  114.6 15.1 %collective-permute-start.8 = (f32[80,1024]{1,0:T(8,128)S(1)}, f32[80,1024]{1,0:T(8,128)S(1)}, u32[]{:S(2)}, u32[]{:S(2)}) collective-permute-start(f32[80,1024]{1,0:T(8,128)S(1)} %slice.56), channel_id=1, source_target_pairs={{0,32},{32,64},{64,96},{96,0},{1,33},{33,65},{65,97},{97,1},{2,34}... | collective-permute-start | bytes 983048 | tf_op jit(solution)/shard_map/ppermute | solution.py:110
  116.6 13.1 %collective-permute-start.9 = (f32[80,1024]{1,0:T(8,128)S(1)}, f32[80,1024]{1,0:T(8,128)S(1)}, u32[]{:S(2)}, u32[]{:S(2)}) collective-permute-start(f32[80,1024]{1,0:T(8,128)S(1)} %slice.57), channel_id=1, source_target_pairs={{0,96},{32,0},{64,32},{96,64},{1,97},{33,1},{65,33},{97,65},{2,98}... | collective-permute-start | bytes 983048 | tf_op jit(solution)/shard_map/ppermute | solution.py:110
  122.2 11.8 %collective-permute-start.14 = (f32[80,1024]{1,0:T(8,128)S(1)}, f32[80,1024]{1,0:T(8,128)S(1)}, u32[]{:S(2)}, u32[]{:S(2)}) collective-permute-start(f32[80,1024]{1,0:T(8,128)S(1)} %slice.58), channel_id=1, source_target_pairs={{0,32},{32,64},{64,96},{96,0},{1,33},{33,65},{65,97},{97,1},{2,34}... | collective-permute-start | bytes 983048 | tf_op jit(solution)/shard_map/ppermute | solution.py:110
  125.1 10.7 %collective-permute-start.15 = (f32[80,1024]{1,0:T(8,128)S(1)}, f32[80,1024]{1,0:T(8,128)S(1)}, u32[]{:S(2)}, u32[]{:S(2)}) collective-permute-start(f32[80,1024]{1,0:T(8,128)S(1)} %slice.59), channel_id=1, source_target_pairs={{0,96},{32,0},{64,32},{96,64},{1,97},{33,1},{65,33},{97,65},{2,98}... | collective-permute-start | bytes 983048 | tf_op jit(solution)/shard_map/ppermute | solution.py:110
  139.9 5.3 %collective-permute-start.16 = (f32[152,1024]{1,0:T(8,128)S(1)}, f32[152,1024]{1,0:T(8,128)S(1)}, u32[]{:S(2)}, u32[]{:S(2)}) collective-permute-start(f32[152,1024]{1,0:T(8,128)S(1)} %get-tuple-element.12), channel_id=1, source_target_pairs={{0,16},{16,0},{1,17},{17,1},{2,18},{18,2},{3,19},{19,3},{4,20},{20... | collective-permute-start | bytes 1867784 | tf_op jit(solution)/shard_map/ppermute | solution.py:199
  (9 other events, 93.1 us)

commit v4 on v3

--- a/solution.py
+++ b/solution.py
@@ -50,7 +50,7 @@
         at += piece.shape[0]
 
 
-def antisym_kernel(block, columns_k, base_ref, other_ref, tau_ref, mine_ref, theirs_ref, head_ref, tail_ref, rows_ref, ends_ref):
+def antisym_kernel(block, columns_k, chunk_ref, base_ref, other_ref, tau_ref, mine_ref, theirs_ref, head_ref, tail_ref, rows_ref, ends_ref):
     total = rows_ref.shape[0]
     pairs = mine_ref.shape[0]
     ranks = total // columns_k
@@ -65,8 +65,9 @@
 
     def one(b, _):
         at = pl.multiple_of(b * block, 8)
+        first = chunk_ref[b]
         for r in range(block):
-            k = other_ref[at + r]
+            k = other_ref[first + r]
             rows_ref[pl.ds(at + r, 1), :] = head_ref[pl.ds(k, 1), :]
             ends_ref[pl.ds(at + r, 1), :] = tail_ref[pl.ds(k, 1), :]
         here = pl.ds(pl.multiple_of(base_ref[b], 8), block)
@@ -124,6 +125,7 @@
         out_shape=jax.ShapeDtypeStruct((packed_rows, 128), jnp.float32),
         in_specs=[VMEM],
         out_specs=VMEM,
+        compiler_params=pltpu.CompilerParams(vmem_limit_bytes=8 * 2**20),
         name="pack",
     )(amplitudes.T)
     left, right = around(packed, packed, "zh")
@@ -134,6 +136,7 @@
         out_shape=jax.ShapeDtypeStruct((4, 4 * packed_rows, 128), jnp.float32),
         in_specs=[VMEM] * 5,
         out_specs=VMEM,
+        compiler_params=pltpu.CompilerParams(vmem_limit_bytes=8 * 2**20),
         name="copies",
     )(packed, left, right, *far)
     tau = lax.all_to_all(copies, "y", split_axis=0, concat_axis=0, tiled=True).reshape(-1, 128)
@@ -150,40 +153,45 @@
         in_specs=[VMEM] * 2,
         out_specs=VMEM,
         scratch_shapes=[pltpu.VMEM((tiles * 128, 128), jnp.float32)],
+        compiler_params=pltpu.CompilerParams(vmem_limit_bytes=8 * 2**20),
         name="symmetrize",
     )(integrals, got)
 
-    s = [start]
-    for _ in range(3):
-        s.append(lax.ppermute(s[-1], "zl", [(RING[i], RING[(i + 1) % 4]) for i in range(4)]))
+    def lower(block):
+        return lax.ppermute(block, "zl", [(RING[i], RING[(i + 1) % 4]) for i in range(4)])
+
+    one = lower(start)
+    two = lower(one)
+    first = jnp.concatenate([start, one], axis=0)
+    first = [first, *around(first, first, "x")]
+    three = lower(two)
+    last = jnp.concatenate([two, three], axis=0)
+    last = [last, *around(last, last, "x")]
     pieces, order = [], []
-    for i in (0, 2):
-        part = jnp.concatenate(s[i : i + 2], axis=0)
-        left, right = around(part, part, "x")
-        pieces += [part, left, right, *around(left[:rows_k], right[rows_k:], "x")]
+    for i, part in ((0, first), (2, last)):
+        pieces += part + list(around(part[1][:rows_k], part[2][rows_k:], "x"))
         order += [(i, 0), (i + 1, 0), (i, -1), (i + 1, -1), (i, 1), (i + 1, 1), (i, 2), (i + 1, 2)]
 
     slot = jnp.array(SLOT, jnp.int32)
 
     def place(k):
         rank = k // columns_k
-        return ((rank // 4) * 4 + slot[(rank % 4 - zh) % 4]) * columns_k + k % columns_k
+        return k + (slot[(rank % 4 - zh) % 4] - rank % 4) * columns_k
 
     steps = jnp.array(order, jnp.int32)
     zs = jnp.array(RING, jnp.int32)[(ring_place - steps[:, 0]) % 4]
     chunk = (zs * 4 + (x + steps[:, 1]) % 4) * 2
-    chunk = jnp.concatenate([chunk + core, chunk + 1 - core])
-    other = place(partner).reshape(-1, rows_k).at[chunk].get(mode="promise_in_bounds").reshape(-1)
+    chunk = jnp.concatenate([chunk + core, chunk + 1 - core]) * rows_k
     mine, theirs = pl.pallas_call(
         functools.partial(antisym_kernel, rows_k, columns_k),
         out_shape=[jax.ShapeDtypeStruct((pairs, slab // 2), jnp.float32)] * 2,
-        in_specs=[SMEM, SMEM, VMEM],
+        in_specs=[SMEM, SMEM, SMEM, VMEM],
         out_specs=[VMEM] * 2,
         scratch_shapes=[pltpu.VMEM((slab, 128), jnp.float32)] * 4,
-        compiler_params=pltpu.CompilerParams(vmem_limit_bytes=16 * 2**20),
+        compiler_params=pltpu.CompilerParams(vmem_limit_bytes=10 * 2**20),
         cost_estimate=pl.CostEstimate(flops=slab * pairs, bytes_accessed=3 * slab * pairs * 4, transcendentals=0),
         name="antisym",
-    )(place(chunk * rows_k), other, tau)
+    )(chunk, place(chunk), place(partner), tau)
     theirs = lax.ppermute(theirs, "c", shift(2, 1))
 
     own, back = pl.pallas_call(
@@ -192,7 +200,7 @@
         in_specs=[VMEM] * (2 + len(pieces)),
         out_specs=[VMEM] * 2,
         scratch_shapes=[pltpu.VMEM((slab // 2, columns), jnp.bfloat16)] * 2,
-        compiler_params=pltpu.CompilerParams(vmem_limit_bytes=32 * 2**20),
+        compiler_params=pltpu.CompilerParams(vmem_limit_bytes=16 * 2**20),
         cost_estimate=pl.CostEstimate(flops=6 * pairs * slab * columns, bytes_accessed=8 * 2**20, transcendentals=0),
         name="product",
     )(mine, theirs, *pieces)

time: 148 us -> 141 us (0.953)
  waiting for transfers between devices: 24 us -> 34.1 us
  starting transfers between devices: 90.2 us -> 83.1 us
  local copies, waits for them, and re-layouts: 12.4 us -> 8.29 us
  Pallas kernels: 14.9 us -> 10.8 us
  other arithmetic: 4.25 us -> 2.6 us
    ppermute x3, starting transfers between devices: 13.7 us -> 6.51 us  [lower(): lax.ppermute(block, 'zl', [(RING[i], RING[(i + 1) % 4]) for i in range(4)])]
    ppermute x6, waiting for transfers between devices: 8.98 us -> 16 us  [around(): lax.ppermute(down, axis, shift(4, -1))]
    unnamed x31 -> x15, local copies, waits for them, and re-layouts: 5.1 us -> 2.08 us
    ppermute x3, waiting for transfers between devices: 7.07 us -> 10.1 us  [lower(): lax.ppermute(block, 'zl', [(RING[i], RING[(i + 1) % 4]) for i in range(4)])]
    pallas_call x1, Pallas kernels: 1.97 us -> 0.17 us  [body(): pl.pallas_call(symmetrize_kernel, out_shape=jax.ShapeDtypeStruct((rows_k,...]
    pallas_call x1, Pallas kernels: 1.65 us -> 0.08 us  [body(): pl.pallas_call(pack_kernel, out_shape=jax.ShapeDtypeStruct((packed_rows,...]
  transfers between devices with their start and end apart: 19 -> 19, of which waited for: 8 -> 9; matrix products, arithmetic and copies ran while one was open for 8% -> 5% of each run, Pallas kernels for 7% -> 5%
where the time goes in v4:
time: 141 us; the launch traced here: 139 us
  starting transfers between devices  83.1 us (59%)
  waiting for transfers between devices  34.1 us (24%)
  Pallas kernels  10.8 us (8%)
  local copies, waits for them, and re-layouts  8.29 us (6%)
  other arithmetic  2.6 us (2%)
    ppermute x6, starting transfers between devices, around(): lax.ppermute(up, axis, shift(4, 1))  21.8 us
    ppermute x6, starting transfers between devices, around(): lax.ppermute(down, axis, shift(4, -1))  20.6 us
    all_to_all x1, starting transfers between devices, body(): got = lax.all_to_all(sent, VIR, split_axis=0, concat_axis=0, tiled=True)  18.5 us
    ppermute x6, waiting for transfers between devices, around(): lax.ppermute(down, axis, shift(4, -1))  16 us
    ppermute x3, waiting for transfers between devices, lower(): lax.ppermute(block, 'zl', [(RING[i], RING[(i + 1) % 4]) for i in range(4)])  10.1 us
    ppermute x1, starting transfers between devices, body(): theirs = lax.ppermute(theirs, 'c', shift(2, 1))  8.01 us
    ppermute x3, starting transfers between devices, lower(): lax.ppermute(block, 'zl', [(RING[i], RING[(i + 1) % 4]) for i in range(4)])  6.51 us
    ppermute x6, waiting for transfers between devices, around(): lax.ppermute(up, axis, shift(4, 1))  6.36 us
  transfers between devices with their start and end apart: 19, of which 9 were waited for; matrix products, arithmetic and copies ran while one was open for 5% of the time, Pallas kernels for 5%

profile of v4, /device:TPU:1, one launch (start us, length us, event | category | flops | bytes accessed | tf_op | source)
XLA Modules:
  0.0 139.2 jit_solution(2004352584607231691)
XLA Ops:
  2.4 18.5 %all-to-all-start.1 = ((f32[16,40,128]{2,1,0:T(8,128)}), f32[16,40,128]{2,1,0:T(8,128)S(1)}, u32[]{:S(2)}, u32[]{:S(2)}) async-start(f32[16,40,128]{2,1,0:T(8,128)} %bitcast.41), calls=%async_computation.1 | async-start | bytes 655360 | tf_op jit(solution)/shard_map/all_to_all | solution.py:149
  21.1 7.2 %collective-permute-start = (f32[192,128]{1,0:T(8,128)S(1)}, f32[192,128]{1,0:T(8,128)S(1)}, u32[]{:S(2)}, u32[]{:S(2)}) collective-permute-start(f32[192,128]{1,0:T(8,128)S(1)} %pack.1.refs_0_), channel_id=1, source_target_pairs={{0,1},{1,2},{2,3},{3,0},{4,5},{5,6},{6,7},{7,4},{8,9},{9,10},{10,1... | collective-permute-start | bytes 294920 | tf_op jit(solution)/shard_map/ppermute | solution.py:111
  28.3 2.0 %collective-permute-start.1 = (f32[192,128]{1,0:T(8,128)S(1)}, f32[192,128]{1,0:T(8,128)S(1)}, u32[]{:S(2)}, u32[]{:S(2)}) collective-permute-start(f32[192,128]{1,0:T(8,128)S(1)} %pack.1.refs_0_), channel_id=1, source_target_pairs={{0,3},{1,0},{2,1},{3,2},{4,7},{5,4},{6,5},{7,6},{8,11},{9,8},{10,9... | collective-permute-start | bytes 294920 | tf_op jit(solution)/shard_map/ppermute | solution.py:111
  32.4 2.0 %collective-permute-done.refs_1_ = f32[192,128]{1,0:T(8,128)S(1)} collective-permute-done((f32[192,128]{1,0:T(8,128)S(1)}, f32[192,128]{1,0:T(8,128)S(1)}, u32[]{:S(2)}, u32[]{:S(2)}) %collective-permute-start) | collective-permute-done | bytes 98336 | tf_op jit(solution)/shard_map/ppermute | solution.py:111
  34.3 5.2 %collective-permute-start.2 = (f32[96,128]{1,0:T(8,128)S(1)}, f32[96,128]{1,0:T(8,128)S(1)}, u32[]{:S(2)}, u32[]{:S(2)}) collective-permute-start(f32[96,128]{1,0:T(8,128)S(1)} %slice.52), channel_id=1, source_target_pairs={{0,1},{1,2},{2,3},{3,0},{4,5},{5,6},{6,7},{7,4},{8,9},{9,10},{10,1... | collective-permute-start | bytes 147464 | tf_op jit(solution)/shard_map/ppermute | solution.py:111
  39.6 9.7 %collective-permute-done.1.refs_2_ = f32[192,128]{1,0:T(8,128)S(1)} collective-permute-done((f32[192,128]{1,0:T(8,128)S(1)}, f32[192,128]{1,0:T(8,128)S(1)}, u32[]{:S(2)}, u32[]{:S(2)}) %collective-permute-start.1) | collective-permute-done | bytes 98336 | tf_op jit(solution)/shard_map/ppermute | solution.py:111
  49.3 2.0 %collective-permute-start.3 = (f32[96,128]{1,0:T(8,128)S(1)}, f32[96,128]{1,0:T(8,128)S(1)}, u32[]{:S(2)}, u32[]{:S(2)}) collective-permute-start(f32[96,128]{1,0:T(8,128)S(1)} %slice.53), channel_id=1, source_target_pairs={{0,3},{1,0},{2,1},{3,2},{4,7},{5,4},{6,5},{7,6},{8,11},{9,8},{10,9... | collective-permute-start | bytes 147464 | tf_op jit(solution)/shard_map/ppermute | solution.py:111
  51.5 1.9 %collective-permute-start.5 = (f32[80,1024]{1,0:T(8,128)S(1)}, f32[80,1024]{1,0:T(8,128)S(1)}, u32[]{:S(2)}, u32[]{:S(2)}) collective-permute-start(f32[80,1024]{1,0:T(8,128)S(1)} %symmetrize.1), channel_id=1, source_target_pairs={{0,128},{128,384},{384,256},{256,0},{1,129},{129,385},{385,257},{2... | collective-permute-start | bytes 983048 | tf_op jit(solution)/shard_map/ppermute | solution.py:161
  53.6 4.4 %collective-permute-done.3.refs_4_ = f32[96,128]{1,0:T(8,128)S(1)} collective-permute-done((f32[96,128]{1,0:T(8,128)S(1)}, f32[96,128]{1,0:T(8,128)S(1)}, u32[]{:S(2)}, u32[]{:S(2)}) %collective-permute-start.3) | collective-permute-done | bytes 49184 | tf_op jit(solution)/shard_map/ppermute | solution.py:111
  59.3 4.0 %all-to-all-start = ((f32[4,768,128]{2,1,0:T(8,128)}), f32[4,768,128]{2,1,0:T(8,128)S(1)}, u32[]{:S(2)}, u32[]{:S(2)}) async-start(f32[4,768,128]{2,1,0:T(8,128)} %copies.1), calls=%async_computation | async-start | bytes 3145728 | tf_op jit(solution)/shard_map/all_to_all | solution.py:142
  63.3 3.8 %collective-permute-done.5 = f32[80,1024]{1,0:T(8,128)S(1)} collective-permute-done((f32[80,1024]{1,0:T(8,128)S(1)}, f32[80,1024]{1,0:T(8,128)S(1)}, u32[]{:S(2)}, u32[]{:S(2)}) %collective-permute-start.5) | collective-permute-done | bytes 327712 | tf_op jit(solution)/shard_map/ppermute | solution.py:161
  67.1 2.7 %collective-permute-start.10 = (f32[80,1024]{1,0:T(8,128)S(1)}, f32[80,1024]{1,0:T(8,128)S(1)}, u32[]{:S(2)}, u32[]{:S(2)}) collective-permute-start(f32[80,1024]{1,0:T(8,128)S(1)} %collective-permute-done.5), channel_id=1, source_target_pairs={{0,128},{128,384},{384,256},{256,0},{1,129},{129,385},{385,257},{2... | collective-permute-start | bytes 983048 | tf_op jit(solution)/shard_map/ppermute | solution.py:161
  69.8 6.3 %collective-permute-done.10 = f32[80,1024]{1,0:T(8,128)S(1)} collective-permute-done((f32[80,1024]{1,0:T(8,128)S(1)}, f32[80,1024]{1,0:T(8,128)S(1)}, u32[]{:S(2)}, u32[]{:S(2)}) %collective-permute-start.10) | collective-permute-done | bytes 327712 | tf_op jit(solution)/shard_map/ppermute | solution.py:161
  78.2 3.1 %collective-permute-start.6 = (f32[160,1024]{1,0:T(8,128)S(1)}, f32[160,1024]{1,0:T(8,128)S(1)}, u32[]{:S(2)}, u32[]{:S(2)}) collective-permute-start(f32[160,1024]{1,0:T(8,128)S(1)} %pad_maximum_fusion.refs_0_), channel_id=1, source_target_pairs={{0,32},{32,64},{64,96},{96,0},{1,33},{33,65},{65,97},{97,1},{2,34}... | collective-permute-start | bytes 1966088 | tf_op jit(solution)/shard_map/ppermute | solution.py:111
  81.3 3.4 %collective-permute-start.7 = (f32[160,1024]{1,0:T(8,128)S(1)}, f32[160,1024]{1,0:T(8,128)}, u32[]{:S(2)}, u32[]{:S(2)}) collective-permute-start(f32[160,1024]{1,0:T(8,128)S(1)} %pad_maximum_fusion.refs_0_), channel_id=1, source_target_pairs={{0,96},{32,0},{64,32},{96,64},{1,97},{33,1},{65,33},{97,65},{2,98}... | collective-permute-start | bytes 1966088 | tf_op jit(solution)/shard_map/ppermute | solution.py:111
  86.2 2.5 %collective-permute-start.12 = (f32[160,1024]{1,0:T(8,128)}, f32[160,1024]{1,0:T(8,128)}, u32[]{:S(2)}, u32[]{:S(2)}) collective-permute-start(f32[160,1024]{1,0:T(8,128)} %constant_dynamic-update-slice_fusion.refs_5_), channel_id=1, source_target_pairs={{0,32},{32,64},{64,96},{96,0},{1,33},{33,65},{65,97},{97,1},{2,34}... | collective-permute-start | bytes 1966088 | tf_op jit(solution)/shard_map/ppermute | solution.py:111
  88.7 4.0 %collective-permute-start.13 = (f32[160,1024]{1,0:T(8,128)}, f32[160,1024]{1,0:T(8,128)}, u32[]{:S(2)}, u32[]{:S(2)}) collective-permute-start(f32[160,1024]{1,0:T(8,128)} %constant_dynamic-update-slice_fusion.refs_5_), channel_id=1, source_target_pairs={{0,96},{32,0},{64,32},{96,64},{1,97},{33,1},{65,33},{97,65},{2,98}... | collective-permute-start | bytes 1966088 | tf_op jit(solution)/shard_map/ppermute | solution.py:111
  93.5 4.9 %antisym.1 = (f32[152,1280]{1,0:T(8,128)S(1)}, f32[152,1280]{1,0:T(8,128)S(1)}) custom-call(s32[32]{0:T(128)S(1)} %get-tuple-element.14.chunk_ref, s32[32]{0:T(128)S(1)} %get-tuple-element.13.base_ref, s32[2560]{0:T(1024)S(1)} %fusion.3.other_ref, f32[3072,128]{1,0:T(8,128)S(1)} %bitcast.42), custom_call_target="tpu_custom_call" | custom-call | flops 389120 | bytes 4669440 | tf_op jit(solution)/shard_map/antisym/pallas_call | solution.py:185
  98.4 8.0 %collective-permute-start.4 = (f32[152,1280]{1,0:T(8,128)S(1)}, f32[152,1280]{1,0:T(8,128)S(1)}, u32[]{:S(2)}, u32[]{:S(2)}) collective-permute-start(f32[152,1280]{1,0:T(8,128)S(1)} %get-tuple-element.10), channel_id=1, source_target_pairs={{0,16},{16,0},{1,17},{17,1},{2,18},{18,2},{3,19},{19,3},{4,20},{20... | collective-permute-start | bytes 2334728 | tf_op jit(solution)/shard_map/ppermute | solution.py:195
  109.4 4.6 %collective-permute-start.9 = (f32[80,1024]{1,0:T(8,128)S(1)}, f32[80,1024]{1,0:T(8,128)S(1)}, u32[]{:S(2)}, u32[]{:S(2)}) collective-permute-start(f32[80,1024]{1,0:T(8,128)S(1)} %slice.55), channel_id=1, source_target_pairs={{0,96},{32,0},{64,32},{96,64},{1,97},{33,1},{65,33},{97,65},{2,98}... | collective-permute-start | bytes 983048 | tf_op jit(solution)/shard_map/ppermute | solution.py:111
  117.9 4.6 %collective-permute-start.15 = (f32[80,1024]{1,0:T(8,128)S(1)}, f32[80,1024]{1,0:T(8,128)S(1)}, u32[]{:S(2)}, u32[]{:S(2)}) collective-permute-start(f32[80,1024]{1,0:T(8,128)S(1)} %slice.57), channel_id=1, source_target_pairs={{0,96},{32,0},{64,32},{96,64},{1,97},{33,1},{65,33},{97,65},{2,98}... | collective-permute-start | bytes 983048 | tf_op jit(solution)/shard_map/ppermute | solution.py:111
  122.5 4.2 %collective-permute-done.14.refs_8_ = f32[80,1024]{1,0:T(8,128)S(1)} collective-permute-done((f32[80,1024]{1,0:T(8,128)S(1)}, f32[80,1024]{1,0:T(8,128)S(1)}, u32[]{:S(2)}, u32[]{:S(2)}) %collective-permute-start.14) | collective-permute-done | bytes 327712 | tf_op jit(solution)/shard_map/ppermute | solution.py:111
  128.7 4.3 %product.1 = (f32[152,1024]{1,0:T(8,128)S(1)}, f32[152,1024]{1,0:T(8,128)S(1)}) custom-call(f32[152,1280]{1,0:T(8,128)S(1)} %get-tuple-element.9.mine_ref, f32[152,1280]{1,0:T(8,128)S(1)} %collective-permute-done.4.theirs_ref, f32[160,1024]{1,0:T(8,128)S(1)} %pad_maximum_fusion.refs_0_, f32[160,1024]{1,0:T(8,128)S(1)} %collective-permute-done.6.refs_1_, ...), custom_call_target="tpu_custom_call" | custom-call | flops 2390753280 | bytes 8388608 | tf_op jit(solution)/shard_map/product/pallas_call | solution.py:197
  133.0 3.7 %collective-permute-start.16 = (f32[152,1024]{1,0:T(8,128)S(1)}, f32[152,1024]{1,0:T(8,128)S(1)}, u32[]{:S(2)}, u32[]{:S(2)}) collective-permute-start(f32[152,1024]{1,0:T(8,128)S(1)} %get-tuple-element.12), channel_id=1, source_target_pairs={{0,16},{16,0},{1,17},{17,1},{2,18},{18,2},{3,19},{19,3},{4,20},{20... | collective-permute-start | bytes 1867784 | tf_op jit(solution)/shard_map/ppermute | solution.py:207
  (56 shorter events, 21.9 us)
Async XLA Ops:
  0.0 20.9 %copy-start.2 = (f32[152,160]{1,0:T(8,128)S(1)}, f32[152,160]{1,0:T(8,128)}, u32[]{:S(2)}) copy-start(f32[152,160]{1,0:T(8,128)} %param.8) | copy-start | bytes 291844
  1.2 29.1 %copy-start.1 = (s32[4]{0:T(128)S(1)}, s32[4]{0:T(128)}, u32[]{:S(2)}) copy-start(s32[4]{0:T(128)} %constant.111.clone) | copy-start | bytes 52
  1.2 29.8 %copy-start.5 = (s32[16,1]{0,1:T(1,128)S(1)}, s32[16,1]{0,1:T(1,128)}, u32[]{:S(2)}) copy-start(s32[16,1]{0,1:T(1,128)} %constant.119) | copy-start | bytes 196
  1.4 49.8 %copy-start = (f32[80,1024]{1,0:T(8,128)S(1)}, f32[80,1024]{1,0:T(8,128)}, u32[]{:S(2)}) copy-start(f32[80,1024]{1,0:T(8,128)} %integrals_ref.1) | copy-start | bytes 983044
  2.4 51.0 %copy-start.4 = (s32[16,1]{0,1:T(1,128)S(1)}, s32[16,1]{0,1:T(1,128)}, u32[]{:S(2)}) copy-start(s32[16,1]{0,1:T(1,128)} %constant.118) | copy-start | bytes 196
  2.4 48.9 %all-to-all-start.1 = ((f32[16,40,128]{2,1,0:T(8,128)}), f32[16,40,128]{2,1,0:T(8,128)S(1)}, u32[]{:S(2)}, u32[]{:S(2)}) async-start(f32[16,40,128]{2,1,0:T(8,128)} %bitcast.41), calls=%async_computation.1 | async-start | bytes 655360 | tf_op jit(solution)/shard_map/all_to_all | solution.py:149
  21.1 13.2 %collective-permute-start = (f32[192,128]{1,0:T(8,128)S(1)}, f32[192,128]{1,0:T(8,128)S(1)}, u32[]{:S(2)}, u32[]{:S(2)}) collective-permute-start(f32[192,128]{1,0:T(8,128)S(1)} %pack.1.refs_0_), channel_id=1, source_target_pairs={{0,1},{1,2},{2,3},{3,0},{4,5},{5,6},{6,7},{7,4},{8,9},{9,10},{10,1... | collective-permute-start | bytes 294920 | tf_op jit(solution)/shard_map/ppermute | solution.py:111
  28.3 21.0 %collective-permute-start.1 = (f32[192,128]{1,0:T(8,128)S(1)}, f32[192,128]{1,0:T(8,128)S(1)}, u32[]{:S(2)}, u32[]{:S(2)}) collective-permute-start(f32[192,128]{1,0:T(8,128)S(1)} %pack.1.refs_0_), channel_id=1, source_target_pairs={{0,3},{1,0},{2,1},{3,2},{4,7},{5,4},{6,5},{7,6},{8,11},{9,8},{10,9... | collective-permute-start | bytes 294920 | tf_op jit(solution)/shard_map/ppermute | solution.py:111
  34.3 19.2 %collective-permute-start.2 = (f32[96,128]{1,0:T(8,128)S(1)}, f32[96,128]{1,0:T(8,128)S(1)}, u32[]{:S(2)}, u32[]{:S(2)}) collective-permute-start(f32[96,128]{1,0:T(8,128)S(1)} %slice.52), channel_id=1, source_target_pairs={{0,1},{1,2},{2,3},{3,0},{4,5},{5,6},{6,7},{7,4},{8,9},{9,10},{10,1... | collective-permute-start | bytes 147464 | tf_op jit(solution)/shard_map/ppermute | solution.py:111
  49.3 8.7 %collective-permute-start.3 = (f32[96,128]{1,0:T(8,128)S(1)}, f32[96,128]{1,0:T(8,128)S(1)}, u32[]{:S(2)}, u32[]{:S(2)}) collective-permute-start(f32[96,128]{1,0:T(8,128)S(1)} %slice.53), channel_id=1, source_target_pairs={{0,3},{1,0},{2,1},{3,2},{4,7},{5,4},{6,5},{7,6},{8,11},{9,8},{10,9... | collective-permute-start | bytes 147464 | tf_op jit(solution)/shard_map/ppermute | solution.py:111
  51.5 15.6 %collective-permute-start.5 = (f32[80,1024]{1,0:T(8,128)S(1)}, f32[80,1024]{1,0:T(8,128)S(1)}, u32[]{:S(2)}, u32[]{:S(2)}) collective-permute-start(f32[80,1024]{1,0:T(8,128)S(1)} %symmetrize.1), channel_id=1, source_target_pairs={{0,128},{128,384},{384,256},{256,0},{1,129},{129,385},{385,257},{2... | collective-permute-start | bytes 983048 | tf_op jit(solution)/shard_map/ppermute | solution.py:161
  59.3 34.2 %all-to-all-start = ((f32[4,768,128]{2,1,0:T(8,128)}), f32[4,768,128]{2,1,0:T(8,128)S(1)}, u32[]{:S(2)}, u32[]{:S(2)}) async-start(f32[4,768,128]{2,1,0:T(8,128)} %copies.1), calls=%async_computation | async-start | bytes 3145728 | tf_op jit(solution)/shard_map/all_to_all | solution.py:142
  67.1 9.0 %collective-permute-start.10 = (f32[80,1024]{1,0:T(8,128)S(1)}, f32[80,1024]{1,0:T(8,128)S(1)}, u32[]{:S(2)}, u32[]{:S(2)}) collective-permute-start(f32[80,1024]{1,0:T(8,128)S(1)} %collective-permute-done.5), channel_id=1, source_target_pairs={{0,128},{128,384},{384,256},{256,0},{1,129},{129,385},{385,257},{2... | collective-permute-start | bytes 983048 | tf_op jit(solution)/shard_map/ppermute | solution.py:161
  76.1 9.3 %collective-permute-start.11 = (f32[80,1024]{1,0:T(8,128)S(1)}, f32[80,1024]{1,0:T(8,128)S(1)}, u32[]{:S(2)}, u32[]{:S(2)}) collective-permute-start(f32[80,1024]{1,0:T(8,128)S(1)} %collective-permute-done.10), channel_id=1, source_target_pairs={{0,128},{128,384},{384,256},{256,0},{1,129},{129,385},{385,257},{2... | collective-permute-start | bytes 983048 | tf_op jit(solution)/shard_map/ppermute | solution.py:161
  78.2 28.2 %collective-permute-start.6 = (f32[160,1024]{1,0:T(8,128)S(1)}, f32[160,1024]{1,0:T(8,128)S(1)}, u32[]{:S(2)}, u32[]{:S(2)}) collective-permute-start(f32[160,1024]{1,0:T(8,128)S(1)} %pad_maximum_fusion.refs_0_), channel_id=1, source_target_pairs={{0,32},{32,64},{64,96},{96,0},{1,33},{33,65},{65,97},{97,1},{2,34}... | collective-permute-start | bytes 1966088 | tf_op jit(solution)/shard_map/ppermute | solution.py:111
  81.3 27.1 %collective-permute-start.7 = (f32[160,1024]{1,0:T(8,128)S(1)}, f32[160,1024]{1,0:T(8,128)}, u32[]{:S(2)}, u32[]{:S(2)}) collective-permute-start(f32[160,1024]{1,0:T(8,128)S(1)} %pad_maximum_fusion.refs_0_), channel_id=1, source_target_pairs={{0,96},{32,0},{64,32},{96,64},{1,97},{33,1},{65,33},{97,65},{2,98}... | collective-permute-start | bytes 1966088 | tf_op jit(solution)/shard_map/ppermute | solution.py:111
  86.2 27.8 %collective-permute-start.12 = (f32[160,1024]{1,0:T(8,128)}, f32[160,1024]{1,0:T(8,128)}, u32[]{:S(2)}, u32[]{:S(2)}) collective-permute-start(f32[160,1024]{1,0:T(8,128)} %constant_dynamic-update-slice_fusion.refs_5_), channel_id=1, source_target_pairs={{0,32},{32,64},{64,96},{96,0},{1,33},{33,65},{65,97},{97,1},{2,34}... | collective-permute-start | bytes 1966088 | tf_op jit(solution)/shard_map/ppermute | solution.py:111
  88.7 28.3 %collective-permute-start.13 = (f32[160,1024]{1,0:T(8,128)}, f32[160,1024]{1,0:T(8,128)}, u32[]{:S(2)}, u32[]{:S(2)}) collective-permute-start(f32[160,1024]{1,0:T(8,128)} %constant_dynamic-update-slice_fusion.refs_5_), channel_id=1, source_target_pairs={{0,96},{32,0},{64,32},{96,64},{1,97},{33,1},{65,33},{97,65},{2,98}... | collective-permute-start | bytes 1966088 | tf_op jit(solution)/shard_map/ppermute | solution.py:111
  98.4 24.1 %collective-permute-start.4 = (f32[152,1280]{1,0:T(8,128)S(1)}, f32[152,1280]{1,0:T(8,128)S(1)}, u32[]{:S(2)}, u32[]{:S(2)}) collective-permute-start(f32[152,1280]{1,0:T(8,128)S(1)} %get-tuple-element.10), channel_id=1, source_target_pairs={{0,16},{16,0},{1,17},{17,1},{2,18},{18,2},{3,19},{19,3},{4,20},{20... | collective-permute-start | bytes 2334728 | tf_op jit(solution)/shard_map/ppermute | solution.py:195
  106.5 16.1 %collective-permute-start.8 = (f32[80,1024]{1,0:T(8,128)S(1)}, f32[80,1024]{1,0:T(8,128)S(1)}, u32[]{:S(2)}, u32[]{:S(2)}) collective-permute-start(f32[80,1024]{1,0:T(8,128)S(1)} %slice.54), channel_id=1, source_target_pairs={{0,32},{32,64},{64,96},{96,0},{1,33},{33,65},{65,97},{97,1},{2,34}... | collective-permute-start | bytes 983048 | tf_op jit(solution)/shard_map/ppermute | solution.py:111
  109.4 13.1 %collective-permute-start.9 = (f32[80,1024]{1,0:T(8,128)S(1)}, f32[80,1024]{1,0:T(8,128)S(1)}, u32[]{:S(2)}, u32[]{:S(2)}) collective-permute-start(f32[80,1024]{1,0:T(8,128)S(1)} %slice.55), channel_id=1, source_target_pairs={{0,96},{32,0},{64,32},{96,64},{1,97},{33,1},{65,33},{97,65},{2,98}... | collective-permute-start | bytes 983048 | tf_op jit(solution)/shard_map/ppermute | solution.py:111
  115.0 11.8 %collective-permute-start.14 = (f32[80,1024]{1,0:T(8,128)S(1)}, f32[80,1024]{1,0:T(8,128)S(1)}, u32[]{:S(2)}, u32[]{:S(2)}) collective-permute-start(f32[80,1024]{1,0:T(8,128)S(1)} %slice.56), channel_id=1, source_target_pairs={{0,32},{32,64},{64,96},{96,0},{1,33},{33,65},{65,97},{97,1},{2,34}... | collective-permute-start | bytes 983048 | tf_op jit(solution)/shard_map/ppermute | solution.py:111
  117.9 10.7 %collective-permute-start.15 = (f32[80,1024]{1,0:T(8,128)S(1)}, f32[80,1024]{1,0:T(8,128)S(1)}, u32[]{:S(2)}, u32[]{:S(2)}) collective-permute-start(f32[80,1024]{1,0:T(8,128)S(1)} %slice.57), channel_id=1, source_target_pairs={{0,96},{32,0},{64,32},{96,64},{1,97},{33,1},{65,33},{97,65},{2,98}... | collective-permute-start | bytes 983048 | tf_op jit(solution)/shard_map/ppermute | solution.py:111
  133.0 5.3 %collective-permute-start.16 = (f32[152,1024]{1,0:T(8,128)S(1)}, f32[152,1024]{1,0:T(8,128)S(1)}, u32[]{:S(2)}, u32[]{:S(2)}) collective-permute-start(f32[152,1024]{1,0:T(8,128)S(1)} %get-tuple-element.12), channel_id=1, source_target_pairs={{0,16},{16,0},{1,17},{17,1},{2,18},{18,2},{3,19},{19,3},{4,20},{20... | collective-permute-start | bytes 1867784 | tf_op jit(solution)/shard_map/ppermute | solution.py:207
  (1 other events, 8.0 us)

commit v5 on v4

--- a/solution.py
+++ b/solution.py
@@ -84,9 +84,9 @@
         theirs_ref[128:, j : j + 128] = ends_ref[half + j : half + j + 128, :].T[: pairs - 128]
 
 
-def product_kernel(counts, mine_ref, theirs_ref, *refs):
-    pieces = refs[: len(counts)]
-    own_ref, other_ref, high_ref, low_ref = refs[len(counts) :]
+def product_kernel(first, counts, mine_ref, theirs_ref, *refs):
+    pieces, sums = refs[: len(counts)], refs[len(counts) : -4]
+    own_ref, other_ref, high_ref, low_ref = refs[-4:]
     at = 0
     for piece, count in zip(pieces, counts):
         for r in range(0, count, 80):
@@ -95,7 +95,7 @@
             high_ref[at : at + 80, :] = high
             low_ref[at : at + 80, :] = (value - high.astype(jnp.float32)).astype(jnp.bfloat16)
             at += 80
-    lhs = jnp.concatenate([mine_ref[...], theirs_ref[...]], axis=0)
+    lhs = jnp.concatenate([mine_ref[:, first : first + at], theirs_ref[:, first : first + at]], axis=0)
     lhs_high = lhs.astype(jnp.bfloat16)
     lhs_low = (lhs - lhs_high.astype(jnp.float32)).astype(jnp.bfloat16)
     dot = functools.partial(jnp.dot, preferred_element_type=jnp.float32)
@@ -103,6 +103,8 @@
     for n in range(0, own_ref.shape[1], 256):
         high, low = high_ref[:, n : n + 256], low_ref[:, n : n + 256]
         total = dot(lhs_high, high) + (dot(lhs_high, low) + dot(lhs_low, high))
+        if sums:
+            total = total + jnp.concatenate([ref[:, n : n + 256] for ref in sums], axis=0)
         own_ref[:, n : n + 256] = total[:pairs]
         other_ref[:, n : n + 256] = total[pairs:]
 
@@ -169,8 +171,10 @@
     last = [last, *around(last, last, "x")]
     pieces, order = [], []
     for i, part in ((0, first), (2, last)):
-        pieces += part + list(around(part[1][:rows_k], part[2][rows_k:], "x"))
+        pieces += part + [lax.ppermute(part[1 + i // 2], "x", shift(4, 1 - i))]
         order += [(i, 0), (i + 1, 0), (i, -1), (i + 1, -1), (i, 1), (i + 1, 1), (i, 2), (i + 1, 2)]
+
+    pieces[1:4], tau = lax.optimization_barrier((pieces[1:4], tau))
 
     slot = jnp.array(SLOT, jnp.int32)
 
@@ -194,16 +198,19 @@
     )(chunk, place(chunk), place(partner), tau)
     theirs = lax.ppermute(theirs, "c", shift(2, 1))
 
-    own, back = pl.pallas_call(
-        functools.partial(product_kernel, [p.shape[0] for p in pieces]),
-        out_shape=[jax.ShapeDtypeStruct((pairs, columns), jnp.float32)] * 2,
-        in_specs=[VMEM] * (2 + len(pieces)),
-        out_specs=[VMEM] * 2,
-        scratch_shapes=[pltpu.VMEM((slab // 2, columns), jnp.bfloat16)] * 2,
-        compiler_params=pltpu.CompilerParams(vmem_limit_bytes=16 * 2**20),
-        cost_estimate=pl.CostEstimate(flops=6 * pairs * slab * columns, bytes_accessed=8 * 2**20, transcendentals=0),
-        name="product",
-    )(mine, theirs, *pieces)
+    def product(first, pieces, sums):
+        return pl.pallas_call(
+            functools.partial(product_kernel, first, [p.shape[0] for p in pieces]),
+            out_shape=[jax.ShapeDtypeStruct((pairs, columns), jnp.float32)] * 2,
+            in_specs=[VMEM] * (2 + len(pieces) + len(sums)),
+            out_specs=[VMEM] * 2,
+            scratch_shapes=[pltpu.VMEM((slab // 4, columns), jnp.bfloat16)] * 2,
+            compiler_params=pltpu.CompilerParams(vmem_limit_bytes=16 * 2**20),
+            cost_estimate=pl.CostEstimate(flops=3 * pairs * slab * columns, bytes_accessed=4 * 2**20, transcendentals=0),
+            name="product",
+        )(mine, theirs, *pieces, *sums)
+
+    own, back = product(slab // 4, pieces[4:], product(0, pieces[:4], ()))
     back = lax.ppermute(back, "c", shift(2, 1))
     weight = jnp.where(pair_list[:, 0] == pair_list[:, 1], 0.5, 1.0).astype(jnp.float32)
     return weight[:, None] * (own + back)

time: 141 us -> 140 us (level)
  starting transfers between devices: 83.1 us -> 87.1 us
  local copies, waits for them, and re-layouts: 8.29 us -> 4.5 us
  waiting for transfers between devices: 34.1 us -> 31.2 us
  other arithmetic: 2.6 us -> 4.29 us
    ppermute x6 -> x4, waiting for transfers between devices: 16 us -> 1.15 us  [around(): lax.ppermute(down, axis, shift(4, -1))]
    ppermute x3, starting transfers between devices: 6.51 us -> 16.9 us  [lower(): lax.ppermute(block, 'zl', [(RING[i], RING[(i + 1) % 4]) for i in range(4)])]
    all_to_all x1, waiting for transfers between devices: 0.01 us -> 9.49 us  [body(): got = lax.all_to_all(sent, VIR, split_axis=0, concat_axis=0, tiled=True)]
    ppermute x3, waiting for transfers between devices: 10.1 us -> 2.8 us  [lower(): lax.ppermute(block, 'zl', [(RING[i], RING[(i + 1) % 4]) for i in range(4)])]
    ppermute x6 -> x4, starting transfers between devices: 20.6 us -> 13.9 us  [around(): lax.ppermute(down, axis, shift(4, -1))]
    ppermute x0 -> x2, waiting for transfers between devices: none -> 6.3 us  [body(): pieces += part + [lax.ppermute(part[1 + i // 2], 'x', shift(4, 1 - i))]]
    ppermute x0 -> x2, starting transfers between devices: none -> 5.16 us  [body(): pieces += part + [lax.ppermute(part[1 + i // 2], 'x', shift(4, 1 - i))]]
    ppermute x6 -> x4, starting transfers between devices: 21.8 us -> 18.3 us  [around(): lax.ppermute(up, axis, shift(4, 1))]
  transfers between devices with their start and end apart: 19 -> 17, of which waited for: 9 -> 8; matrix products, arithmetic and copies ran while one was open for 5% -> 3% of each run, Pallas kernels for 5% -> 7%
where the time goes in v5:
time: 140 us; the launch traced here: 139 us
  starting transfers between devices  87.1 us (62%)
  waiting for transfers between devices  31.2 us (22%)
  Pallas kernels  11.2 us (8%)
  local copies, waits for them, and re-layouts  4.5 us (3%)
  other arithmetic  4.29 us (3%)
    all_to_all x1, starting transfers between devices, body(): got = lax.all_to_all(sent, VIR, split_axis=0, concat_axis=0, tiled=True)  18.4 us
    ppermute x4, starting transfers between devices, around(): lax.ppermute(up, axis, shift(4, 1))  18.3 us
    ppermute x3, starting transfers between devices, lower(): lax.ppermute(block, 'zl', [(RING[i], RING[(i + 1) % 4]) for i in range(4)])  16.9 us
    ppermute x4, starting transfers between devices, around(): lax.ppermute(down, axis, shift(4, -1))  13.9 us
    ppermute x4, waiting for transfers between devices, around(): lax.ppermute(up, axis, shift(4, 1))  9.83 us
    all_to_all x1, waiting for transfers between devices, body(): got = lax.all_to_all(sent, VIR, split_axis=0, concat_axis=0, tiled=True)  9.49 us
    ppermute x1, starting transfers between devices, body(): theirs = lax.ppermute(theirs, 'c', shift(2, 1))  7.85 us
    ppermute x2, waiting for transfers between devices, body(): pieces += part + [lax.ppermute(part[1 + i // 2], 'x', shift(4, 1 - i))]  6.3 us
  transfers between devices with their start and end apart: 17, of which 8 were waited for; matrix products, arithmetic and copies ran while one was open for 3% of the time, Pallas kernels for 7%

profile of v5, /device:TPU:1, one launch (start us, length us, event | category | flops | bytes accessed | tf_op | source)
XLA Modules:
  0.0 138.7 jit_solution(8686314535968610840)
XLA Ops:
  2.4 18.4 %all-to-all-start = ((f32[16,40,128]{2,1,0:T(8,128)}), f32[16,40,128]{2,1,0:T(8,128)S(1)}, u32[]{:S(2)}, u32[]{:S(2)}) async-start(f32[16,40,128]{2,1,0:T(8,128)} %bitcast.41), calls=%async_computation | async-start | bytes 655360 | tf_op jit(solution)/shard_map/all_to_all | solution.py:151
  21.0 7.2 %collective-permute-start.4 = (f32[192,128]{1,0:T(8,128)S(1)}, f32[192,128]{1,0:T(8,128)S(1)}, u32[]{:S(2)}, u32[]{:S(2)}) collective-permute-start(f32[192,128]{1,0:T(8,128)S(1)} %pack.1.refs_0_), channel_id=1, source_target_pairs={{0,1},{1,2},{2,3},{3,0},{4,5},{5,6},{6,7},{7,4},{8,9},{9,10},{10,1... | collective-permute-start | bytes 294920 | tf_op jit(solution)/shard_map/ppermute | solution.py:113
  28.2 2.0 %collective-permute-start.5 = (f32[192,128]{1,0:T(8,128)S(1)}, f32[192,128]{1,0:T(8,128)S(1)}, u32[]{:S(2)}, u32[]{:S(2)}) collective-permute-start(f32[192,128]{1,0:T(8,128)S(1)} %pack.1.refs_0_), channel_id=1, source_target_pairs={{0,3},{1,0},{2,1},{3,2},{4,7},{5,4},{6,5},{7,6},{8,11},{9,8},{10,9... | collective-permute-start | bytes 294920 | tf_op jit(solution)/shard_map/ppermute | solution.py:113
  30.9 9.5 %all-to-all-done.got_ref = f32[16,40,128]{2,1,0:T(8,128)S(1)} async-done(((f32[16,40,128]{2,1,0:T(8,128)}), f32[16,40,128]{2,1,0:T(8,128)S(1)}, u32[]{:S(2)}, u32[]{:S(2)}) %all-to-all-start) | async-done | bytes 327712 | tf_op jit(solution)/shard_map/all_to_all | solution.py:151
  40.5 11.9 %collective-permute-start = (f32[80,1024]{1,0:T(8,128)S(1)}, f32[80,1024]{1,0:T(8,128)S(1)}, u32[]{:S(2)}, u32[]{:S(2)}) collective-permute-start(f32[80,1024]{1,0:T(8,128)S(1)} %symmetrize.1), channel_id=1, source_target_pairs={{0,128},{128,384},{384,256},{256,0},{1,129},{129,385},{385,257},{2... | collective-permute-start | bytes 983048 | tf_op jit(solution)/shard_map/ppermute | solution.py:163
  53.9 4.7 %collective-permute-start.6 = (f32[96,128]{1,0:T(8,128)S(1)}, f32[96,128]{1,0:T(8,128)S(1)}, u32[]{:S(2)}, u32[]{:S(2)}) collective-permute-start(f32[96,128]{1,0:T(8,128)S(1)} %slice.36), channel_id=1, source_target_pairs={{0,1},{1,2},{2,3},{3,0},{4,5},{5,6},{6,7},{7,4},{8,9},{9,10},{10,1... | collective-permute-start | bytes 147464 | tf_op jit(solution)/shard_map/ppermute | solution.py:113
  58.6 4.5 %collective-permute-start.7 = (f32[96,128]{1,0:T(8,128)S(1)}, f32[96,128]{1,0:T(8,128)S(1)}, u32[]{:S(2)}, u32[]{:S(2)}) collective-permute-start(f32[96,128]{1,0:T(8,128)S(1)} %slice.37), channel_id=1, source_target_pairs={{0,3},{1,0},{2,1},{3,2},{4,7},{5,4},{6,5},{7,6},{8,11},{9,8},{10,9... | collective-permute-start | bytes 147464 | tf_op jit(solution)/shard_map/ppermute | solution.py:113
  63.2 3.1 %collective-permute-start.1 = (f32[160,1024]{1,0:T(8,128)S(1)}, f32[160,1024]{1,0:T(8,128)}, u32[]{:S(2)}, u32[]{:S(2)}) collective-permute-start(f32[160,1024]{1,0:T(8,128)S(1)} %pad_maximum_fusion.refs_0_), channel_id=1, source_target_pairs={{0,32},{32,64},{64,96},{96,0},{1,33},{33,65},{65,97},{97,1},{2,34}... | collective-permute-start | bytes 1966088 | tf_op jit(solution)/shard_map/ppermute | solution.py:113
  66.3 1.9 %collective-permute-start.9 = (f32[80,1024]{1,0:T(8,128)S(1)}, f32[80,1024]{1,0:T(8,128)S(1)}, u32[]{:S(2)}, u32[]{:S(2)}) collective-permute-start(f32[80,1024]{1,0:T(8,128)S(1)} %collective-permute-done), channel_id=1, source_target_pairs={{0,128},{128,384},{384,256},{256,0},{1,129},{129,385},{385,257},{2... | collective-permute-start | bytes 983048 | tf_op jit(solution)/shard_map/ppermute | solution.py:163
  69.6 3.6 %all-to-all-start.1 = ((f32[4,768,128]{2,1,0:T(8,128)}), f32[4,768,128]{2,1,0:T(8,128)S(1)}, u32[]{:S(2)}, u32[]{:S(2)}) async-start(f32[4,768,128]{2,1,0:T(8,128)} %copies.1), calls=%async_computation.1 | async-start | bytes 3145728 | tf_op jit(solution)/shard_map/all_to_all | solution.py:144
  73.2 2.3 %collective-permute-done.9 = f32[80,1024]{1,0:T(8,128)S(1)} collective-permute-done((f32[80,1024]{1,0:T(8,128)S(1)}, f32[80,1024]{1,0:T(8,128)S(1)}, u32[]{:S(2)}, u32[]{:S(2)}) %collective-permute-start.9) | collective-permute-done | bytes 327712 | tf_op jit(solution)/shard_map/ppermute | solution.py:163
  75.4 3.1 %collective-permute-start.10 = (f32[80,1024]{1,0:T(8,128)S(1)}, f32[80,1024]{1,0:T(8,128)S(1)}, u32[]{:S(2)}, u32[]{:S(2)}) collective-permute-start(f32[80,1024]{1,0:T(8,128)S(1)} %collective-permute-done.9), channel_id=1, source_target_pairs={{0,128},{128,384},{384,256},{256,0},{1,129},{129,385},{385,257},{2... | collective-permute-start | bytes 983048 | tf_op jit(solution)/shard_map/ppermute | solution.py:163
  78.5 3.4 %collective-permute-start.2 = (f32[160,1024]{1,0:T(8,128)S(1)}, f32[160,1024]{1,0:T(8,128)}, u32[]{:S(2)}, u32[]{:S(2)}) collective-permute-start(f32[160,1024]{1,0:T(8,128)S(1)} %pad_maximum_fusion.refs_0_), channel_id=1, source_target_pairs={{0,96},{32,0},{64,32},{96,64},{1,97},{33,1},{65,33},{97,65},{2,98}... | collective-permute-start | bytes 1966088 | tf_op jit(solution)/shard_map/ppermute | solution.py:113
  81.9 1.9 %collective-permute-start.3 = (f32[160,1024]{1,0:T(8,128)}, f32[160,1024]{1,0:T(8,128)}, u32[]{:S(2)}, u32[]{:S(2)}) collective-permute-start(f32[160,1024]{1,0:T(8,128)} %collective-permute-done.1.refs_1_), channel_id=1, source_target_pairs={{0,32},{32,64},{64,96},{96,0},{1,33},{33,65},{65,97},{97,1},{2,34}... | collective-permute-start | bytes 1966088 | tf_op jit(solution)/shard_map/ppermute | solution.py:174
  84.4 4.0 %collective-permute-start.12 = (f32[160,1024]{1,0:T(8,128)S(1)}, f32[160,1024]{1,0:T(8,128)S(1)}, u32[]{:S(2)}, u32[]{:S(2)}) collective-permute-start(f32[160,1024]{1,0:T(8,128)S(1)} %constant_dynamic-update-slice_fusion.refs_0_), channel_id=1, source_target_pairs={{0,96},{32,0},{64,32},{96,64},{1,97},{33,1},{65,33},{97,65},{2,98}... | collective-permute-start | bytes 1966088 | tf_op jit(solution)/shard_map/ppermute | solution.py:113
  92.2 4.6 %collective-permute-done.3.refs_3_ = f32[160,1024]{1,0:T(8,128)} collective-permute-done((f32[160,1024]{1,0:T(8,128)}, f32[160,1024]{1,0:T(8,128)}, u32[]{:S(2)}, u32[]{:S(2)}) %collective-permute-start.3) | collective-permute-done | bytes 655392 | tf_op jit(solution)/shard_map/ppermute | solution.py:174
  97.4 4.9 %antisym.1 = (f32[152,1280]{1,0:T(8,128)S(1)}, f32[152,1280]{1,0:T(8,128)S(1)}) custom-call(s32[32]{0:T(128)S(1)} %copy-done.1, s32[32]{0:T(128)S(1)} %get-tuple-element.25.base_ref, s32[2560]{0:T(1024)S(1)} %fusion.3.other_ref, f32[3072,128]{1,0:T(8,128)S(1)} %bitcast.42), custom_call_target="tpu_custom_call" | custom-call | flops 389120 | bytes 4669440 | tf_op jit(solution)/shard_map/antisym/pallas_call | solution.py:189
  102.4 7.9 %collective-permute-start.8 = (f32[152,1280]{1,0:T(8,128)S(1)}, f32[152,1280]{1,0:T(8,128)S(1)}, u32[]{:S(2)}, u32[]{:S(2)}) collective-permute-start(f32[152,1280]{1,0:T(8,128)S(1)} %get-tuple-element.17), channel_id=1, source_target_pairs={{0,16},{16,0},{1,17},{17,1},{2,18},{18,2},{3,19},{19,3},{4,20},{20... | collective-permute-start | bytes 2334728 | tf_op jit(solution)/shard_map/ppermute | solution.py:199
  110.2 3.3 %collective-permute-start.11 = (f32[160,1024]{1,0:T(8,128)S(1)}, f32[160,1024]{1,0:T(8,128)S(1)}, u32[]{:S(2)}, u32[]{:S(2)}) collective-permute-start(f32[160,1024]{1,0:T(8,128)S(1)} %constant_dynamic-update-slice_fusion.refs_0_), channel_id=1, source_target_pairs={{0,32},{32,64},{64,96},{96,0},{1,33},{33,65},{65,97},{97,1},{2,34}... | collective-permute-start | bytes 1966088 | tf_op jit(solution)/shard_map/ppermute | solution.py:113
  113.5 3.2 %collective-permute-start.13 = (f32[160,1024]{1,0:T(8,128)S(1)}, f32[160,1024]{1,0:T(8,128)S(1)}, u32[]{:S(2)}, u32[]{:S(2)}) collective-permute-start(f32[160,1024]{1,0:T(8,128)S(1)} %collective-permute-done.12.refs_2_), channel_id=1, source_target_pairs={{0,96},{32,0},{64,32},{96,64},{1,97},{33,1},{65,33},{97,65},{2,98}... | collective-permute-start | bytes 1966088 | tf_op jit(solution)/shard_map/ppermute | solution.py:174
  116.8 3.1 %product.2 = (f32[152,1024]{1,0:T(8,128)S(1)}, f32[152,1024]{1,0:T(8,128)S(1)}) custom-call(f32[152,1280]{1,0:T(8,128)S(1)} %get-tuple-element.16.mine_ref, f32[152,1280]{1,0:T(8,128)S(1)} %collective-permute-done.8.theirs_ref, f32[160,1024]{1,0:T(8,128)S(1)} %pad_maximum_fusion.refs_0_, f32[160,1024]{1,0:T(8,128)} %collective-permute-done.1.refs_1_, ...), custom_call_target="tpu_custom_call" | custom-call | flops 1195376640 | bytes 4194304 | tf_op jit(solution)/shard_map/product/pallas_call | solution.py:202
  119.9 9.8 %collective-permute-done.11.refs_1_ = f32[160,1024]{1,0:T(8,128)S(1)} collective-permute-done((f32[160,1024]{1,0:T(8,128)S(1)}, f32[160,1024]{1,0:T(8,128)S(1)}, u32[]{:S(2)}, u32[]{:S(2)}) %collective-permute-start.11) | collective-permute-done | bytes 655392 | tf_op jit(solution)/shard_map/ppermute | solution.py:113
  129.7 1.7 %collective-permute-done.13.refs_3_ = f32[160,1024]{1,0:T(8,128)S(1)} collective-permute-done((f32[160,1024]{1,0:T(8,128)S(1)}, f32[160,1024]{1,0:T(8,128)S(1)}, u32[]{:S(2)}, u32[]{:S(2)}) %collective-permute-start.13) | collective-permute-done | bytes 655392 | tf_op jit(solution)/shard_map/ppermute | solution.py:174
  133.1 3.0 %collective-permute-start.14 = (f32[152,1024]{1,0:T(8,128)S(1)}, f32[152,1024]{1,0:T(8,128)S(1)}, u32[]{:S(2)}, u32[]{:S(2)}) collective-permute-start(f32[152,1024]{1,0:T(8,128)S(1)} %get-tuple-element.24), channel_id=1, source_target_pairs={{0,16},{16,0},{1,17},{17,1},{2,18},{18,2},{3,19},{19,3},{4,20},{20... | collective-permute-start | bytes 1867784 | tf_op jit(solution)/shard_map/ppermute | solution.py:214
  (51 shorter events, 15.3 us)
Async XLA Ops:
  0.0 20.8 %copy-start.3 = (f32[152,160]{1,0:T(8,128)S(1)}, f32[152,160]{1,0:T(8,128)}, u32[]{:S(2)}) copy-start(f32[152,160]{1,0:T(8,128)} %param.8) | copy-start | bytes 291844
  1.2 29.0 %copy-start.2 = (s32[4]{0:T(128)S(1)}, s32[4]{0:T(128)}, u32[]{:S(2)}) copy-start(s32[4]{0:T(128)} %constant.111.clone) | copy-start | bytes 52
  1.2 39.1 %copy-start = (f32[80,1024]{1,0:T(8,128)S(1)}, f32[80,1024]{1,0:T(8,128)}, u32[]{:S(2)}) copy-start(f32[80,1024]{1,0:T(8,128)} %integrals_ref.1) | copy-start | bytes 983044
  1.4 51.0 %copy-start.6 = (s32[16,1]{0,1:T(1,128)S(1)}, s32[16,1]{0,1:T(1,128)}, u32[]{:S(2)}) copy-start(s32[16,1]{0,1:T(1,128)} %constant.119) | copy-start | bytes 196
  2.4 38.0 %all-to-all-start = ((f32[16,40,128]{2,1,0:T(8,128)}), f32[16,40,128]{2,1,0:T(8,128)S(1)}, u32[]{:S(2)}, u32[]{:S(2)}) async-start(f32[16,40,128]{2,1,0:T(8,128)} %bitcast.41), calls=%async_computation | async-start | bytes 655360 | tf_op jit(solution)/shard_map/all_to_all | solution.py:151
  21.0 47.3 %copy-start.5 = (s32[16,1]{0,1:T(1,128)S(1)}, s32[16,1]{0,1:T(1,128)}, u32[]{:S(2)}) copy-start(s32[16,1]{0,1:T(1,128)} %constant.118) | copy-start | bytes 196
  21.0 32.9 %collective-permute-start.4 = (f32[192,128]{1,0:T(8,128)S(1)}, f32[192,128]{1,0:T(8,128)S(1)}, u32[]{:S(2)}, u32[]{:S(2)}) collective-permute-start(f32[192,128]{1,0:T(8,128)S(1)} %pack.1.refs_0_), channel_id=1, source_target_pairs={{0,1},{1,2},{2,3},{3,0},{4,5},{5,6},{6,7},{7,4},{8,9},{9,10},{10,1... | collective-permute-start | bytes 294920 | tf_op jit(solution)/shard_map/ppermute | solution.py:113
  28.2 30.4 %collective-permute-start.5 = (f32[192,128]{1,0:T(8,128)S(1)}, f32[192,128]{1,0:T(8,128)S(1)}, u32[]{:S(2)}, u32[]{:S(2)}) collective-permute-start(f32[192,128]{1,0:T(8,128)S(1)} %pack.1.refs_0_), channel_id=1, source_target_pairs={{0,3},{1,0},{2,1},{3,2},{4,7},{5,4},{6,5},{7,6},{8,11},{9,8},{10,9... | collective-permute-start | bytes 294920 | tf_op jit(solution)/shard_map/ppermute | solution.py:113
  40.5 22.6 %collective-permute-start = (f32[80,1024]{1,0:T(8,128)S(1)}, f32[80,1024]{1,0:T(8,128)S(1)}, u32[]{:S(2)}, u32[]{:S(2)}) collective-permute-start(f32[80,1024]{1,0:T(8,128)S(1)} %symmetrize.1), channel_id=1, source_target_pairs={{0,128},{128,384},{384,256},{256,0},{1,129},{129,385},{385,257},{2... | collective-permute-start | bytes 983048 | tf_op jit(solution)/shard_map/ppermute | solution.py:163
  53.9 14.4 %collective-permute-start.6 = (f32[96,128]{1,0:T(8,128)S(1)}, f32[96,128]{1,0:T(8,128)S(1)}, u32[]{:S(2)}, u32[]{:S(2)}) collective-permute-start(f32[96,128]{1,0:T(8,128)S(1)} %slice.36), channel_id=1, source_target_pairs={{0,1},{1,2},{2,3},{3,0},{4,5},{5,6},{6,7},{7,4},{8,9},{9,10},{10,1... | collective-permute-start | bytes 147464 | tf_op jit(solution)/shard_map/ppermute | solution.py:113
  58.6 9.7 %collective-permute-start.7 = (f32[96,128]{1,0:T(8,128)S(1)}, f32[96,128]{1,0:T(8,128)S(1)}, u32[]{:S(2)}, u32[]{:S(2)}) collective-permute-start(f32[96,128]{1,0:T(8,128)S(1)} %slice.37), channel_id=1, source_target_pairs={{0,3},{1,0},{2,1},{3,2},{4,7},{5,4},{6,5},{7,6},{8,11},{9,8},{10,9... | collective-permute-start | bytes 147464 | tf_op jit(solution)/shard_map/ppermute | solution.py:113
  63.2 18.8 %collective-permute-start.1 = (f32[160,1024]{1,0:T(8,128)S(1)}, f32[160,1024]{1,0:T(8,128)}, u32[]{:S(2)}, u32[]{:S(2)}) collective-permute-start(f32[160,1024]{1,0:T(8,128)S(1)} %pad_maximum_fusion.refs_0_), channel_id=1, source_target_pairs={{0,32},{32,64},{64,96},{96,0},{1,33},{33,65},{65,97},{97,1},{2,34}... | collective-permute-start | bytes 1966088 | tf_op jit(solution)/shard_map/ppermute | solution.py:113
  66.3 9.1 %collective-permute-start.9 = (f32[80,1024]{1,0:T(8,128)S(1)}, f32[80,1024]{1,0:T(8,128)S(1)}, u32[]{:S(2)}, u32[]{:S(2)}) collective-permute-start(f32[80,1024]{1,0:T(8,128)S(1)} %collective-permute-done), channel_id=1, source_target_pairs={{0,128},{128,384},{384,256},{256,0},{1,129},{129,385},{385,257},{2... | collective-permute-start | bytes 983048 | tf_op jit(solution)/shard_map/ppermute | solution.py:163
  69.6 21.5 %all-to-all-start.1 = ((f32[4,768,128]{2,1,0:T(8,128)}), f32[4,768,128]{2,1,0:T(8,128)S(1)}, u32[]{:S(2)}, u32[]{:S(2)}) async-start(f32[4,768,128]{2,1,0:T(8,128)} %copies.1), calls=%async_computation.1 | async-start | bytes 3145728 | tf_op jit(solution)/shard_map/all_to_all | solution.py:144
  75.4 9.0 %collective-permute-start.10 = (f32[80,1024]{1,0:T(8,128)S(1)}, f32[80,1024]{1,0:T(8,128)S(1)}, u32[]{:S(2)}, u32[]{:S(2)}) collective-permute-start(f32[80,1024]{1,0:T(8,128)S(1)} %collective-permute-done.9), channel_id=1, source_target_pairs={{0,128},{128,384},{384,256},{256,0},{1,129},{129,385},{385,257},{2... | collective-permute-start | bytes 983048 | tf_op jit(solution)/shard_map/ppermute | solution.py:163
  78.5 13.7 %collective-permute-start.2 = (f32[160,1024]{1,0:T(8,128)S(1)}, f32[160,1024]{1,0:T(8,128)}, u32[]{:S(2)}, u32[]{:S(2)}) collective-permute-start(f32[160,1024]{1,0:T(8,128)S(1)} %pad_maximum_fusion.refs_0_), channel_id=1, source_target_pairs={{0,96},{32,0},{64,32},{96,64},{1,97},{33,1},{65,33},{97,65},{2,98}... | collective-permute-start | bytes 1966088 | tf_op jit(solution)/shard_map/ppermute | solution.py:113
  81.9 14.8 %collective-permute-start.3 = (f32[160,1024]{1,0:T(8,128)}, f32[160,1024]{1,0:T(8,128)}, u32[]{:S(2)}, u32[]{:S(2)}) collective-permute-start(f32[160,1024]{1,0:T(8,128)} %collective-permute-done.1.refs_1_), channel_id=1, source_target_pairs={{0,32},{32,64},{64,96},{96,0},{1,33},{33,65},{65,97},{97,1},{2,34}... | collective-permute-start | bytes 1966088 | tf_op jit(solution)/shard_map/ppermute | solution.py:174
  84.4 29.1 %collective-permute-start.12 = (f32[160,1024]{1,0:T(8,128)S(1)}, f32[160,1024]{1,0:T(8,128)S(1)}, u32[]{:S(2)}, u32[]{:S(2)}) collective-permute-start(f32[160,1024]{1,0:T(8,128)S(1)} %constant_dynamic-update-slice_fusion.refs_0_), channel_id=1, source_target_pairs={{0,96},{32,0},{64,32},{96,64},{1,97},{33,1},{65,33},{97,65},{2,98}... | collective-permute-start | bytes 1966088 | tf_op jit(solution)/shard_map/ppermute | solution.py:113
  96.8 0.7 copy-start.1
  102.4 14.4 %collective-permute-start.8 = (f32[152,1280]{1,0:T(8,128)S(1)}, f32[152,1280]{1,0:T(8,128)S(1)}, u32[]{:S(2)}, u32[]{:S(2)}) collective-permute-start(f32[152,1280]{1,0:T(8,128)S(1)} %get-tuple-element.17), channel_id=1, source_target_pairs={{0,16},{16,0},{1,17},{17,1},{2,18},{18,2},{3,19},{19,3},{4,20},{20... | collective-permute-start | bytes 2334728 | tf_op jit(solution)/shard_map/ppermute | solution.py:199
  110.2 19.5 %collective-permute-start.11 = (f32[160,1024]{1,0:T(8,128)S(1)}, f32[160,1024]{1,0:T(8,128)S(1)}, u32[]{:S(2)}, u32[]{:S(2)}) collective-permute-start(f32[160,1024]{1,0:T(8,128)S(1)} %constant_dynamic-update-slice_fusion.refs_0_), channel_id=1, source_target_pairs={{0,32},{32,64},{64,96},{96,0},{1,33},{33,65},{65,97},{97,1},{2,34}... | collective-permute-start | bytes 1966088 | tf_op jit(solution)/shard_map/ppermute | solution.py:113
  113.5 17.9 %collective-permute-start.13 = (f32[160,1024]{1,0:T(8,128)S(1)}, f32[160,1024]{1,0:T(8,128)S(1)}, u32[]{:S(2)}, u32[]{:S(2)}) collective-permute-start(f32[160,1024]{1,0:T(8,128)S(1)} %collective-permute-done.12.refs_2_), channel_id=1, source_target_pairs={{0,96},{32,0},{64,32},{96,64},{1,97},{33,1},{65,33},{97,65},{2,98}... | collective-permute-start | bytes 1966088 | tf_op jit(solution)/shard_map/ppermute | solution.py:174
  131.5 4.7 %copy-start.4 = (s32[152,2]{0,1:T(2,128)S(1)}, s32[152,2]{0,1:T(2,128)}, u32[]{:S(2)}) copy-start(s32[152,2]{0,1:T(2,128)} %param.10) | copy-start | bytes 3652
  133.1 4.7 %collective-permute-start.14 = (f32[152,1024]{1,0:T(8,128)S(1)}, f32[152,1024]{1,0:T(8,128)S(1)}, u32[]{:S(2)}, u32[]{:S(2)}) collective-permute-start(f32[152,1024]{1,0:T(8,128)S(1)} %get-tuple-element.24), channel_id=1, source_target_pairs={{0,16},{16,0},{1,17},{17,1},{2,18},{18,2},{3,19},{19,3},{4,20},{20... | collective-permute-start | bytes 1867784 | tf_op jit(solution)/shard_map/ppermute | solution.py:214

commit v6 on v5

--- a/solution.py
+++ b/solution.py
@@ -193,7 +193,7 @@
         out_specs=[VMEM] * 2,
         scratch_shapes=[pltpu.VMEM((slab, 128), jnp.float32)] * 4,
         compiler_params=pltpu.CompilerParams(vmem_limit_bytes=10 * 2**20),
-        cost_estimate=pl.CostEstimate(flops=slab * pairs, bytes_accessed=3 * slab * pairs * 4, transcendentals=0),
+        cost_estimate=pl.CostEstimate(flops=slab * pairs, bytes_accessed=slab * pairs * 64, transcendentals=0),
         name="antisym",
     )(chunk, place(chunk), place(partner), tau)
     theirs = lax.ppermute(theirs, "c", shift(2, 1))
@@ -206,7 +206,7 @@
             out_specs=[VMEM] * 2,
             scratch_shapes=[pltpu.VMEM((slab // 4, columns), jnp.bfloat16)] * 2,
             compiler_params=pltpu.CompilerParams(vmem_limit_bytes=16 * 2**20),
-            cost_estimate=pl.CostEstimate(flops=3 * pairs * slab * columns, bytes_accessed=4 * 2**20, transcendentals=0),
+            cost_estimate=pl.CostEstimate(flops=pairs * slab * columns, bytes_accessed=2**20, transcendentals=0),
             name="product",
         )(mine, theirs, *pieces, *sums)
 

time: 140 us -> 141 us (level)
  transfers between devices with their start and end apart: 17 -> 17, of which waited for: 8 -> 7; matrix products, arithmetic and copies ran while one was open for 3% -> 3% of each run, Pallas kernels for 7% -> 7%
where the time goes in v6:
time: 141 us; the launch traced here: 140 us
  starting transfers between devices  87.6 us (62%)
  waiting for transfers between devices  31.3 us (22%)
  Pallas kernels  12.1 us (9%)
  local copies, waits for them, and re-layouts  5.46 us (4%)
  other arithmetic  3.07 us (2%)
    all_to_all x1, starting transfers between devices, body(): got = lax.all_to_all(sent, VIR, split_axis=0, concat_axis=0, tiled=True)  18.4 us
    ppermute x4, starting transfers between devices, around(): lax.ppermute(up, axis, shift(4, 1))  17.7 us
    ppermute x3, starting transfers between devices, lower(): lax.ppermute(block, 'zl', [(RING[i], RING[(i + 1) % 4]) for i in range(4)])  17 us
    ppermute x4, starting transfers between devices, around(): lax.ppermute(down, axis, shift(4, -1))  14.5 us
    ppermute x4, waiting for transfers between devices, around(): lax.ppermute(up, axis, shift(4, 1))  10 us
    all_to_all x1, waiting for transfers between devices, body(): got = lax.all_to_all(sent, VIR, split_axis=0, concat_axis=0, tiled=True)  9.49 us
    ppermute x1, starting transfers between devices, body(): theirs = lax.ppermute(theirs, 'c', shift(2, 1))  7.75 us
    ppermute x2, waiting for transfers between devices, body(): pieces += part + [lax.ppermute(part[1 + i // 2], 'x', shift(4, 1 - i))]  6.69 us
  transfers between devices with their start and end apart: 17, of which 7 were waited for; matrix products, arithmetic and copies ran while one was open for 3% of the time, Pallas kernels for 7%

profile of v6, /device:TPU:1, one launch (start us, length us, event | category | flops | bytes accessed | tf_op | source)
XLA Modules:
  0.0 140.0 jit_solution(8706413524153295432)
XLA Ops:
  2.4 18.4 %all-to-all-start = ((f32[16,40,128]{2,1,0:T(8,128)}), f32[16,40,128]{2,1,0:T(8,128)S(1)}, u32[]{:S(2)}, u32[]{:S(2)}) async-start(f32[16,40,128]{2,1,0:T(8,128)} %bitcast.41), calls=%async_computation | async-start | bytes 655360 | tf_op jit(solution)/shard_map/all_to_all | solution.py:151
  21.0 7.2 %collective-permute-start.4 = (f32[192,128]{1,0:T(8,128)S(1)}, f32[192,128]{1,0:T(8,128)S(1)}, u32[]{:S(2)}, u32[]{:S(2)}) collective-permute-start(f32[192,128]{1,0:T(8,128)S(1)} %pack.1.refs_0_), channel_id=1, source_target_pairs={{0,1},{1,2},{2,3},{3,0},{4,5},{5,6},{6,7},{7,4},{8,9},{9,10},{10,1... | collective-permute-start | bytes 294920 | tf_op jit(solution)/shard_map/ppermute | solution.py:113
  28.2 2.0 %collective-permute-start.5 = (f32[192,128]{1,0:T(8,128)S(1)}, f32[192,128]{1,0:T(8,128)S(1)}, u32[]{:S(2)}, u32[]{:S(2)}) collective-permute-start(f32[192,128]{1,0:T(8,128)S(1)} %pack.1.refs_0_), channel_id=1, source_target_pairs={{0,3},{1,0},{2,1},{3,2},{4,7},{5,4},{6,5},{7,6},{8,11},{9,8},{10,9... | collective-permute-start | bytes 294920 | tf_op jit(solution)/shard_map/ppermute | solution.py:113
  30.9 9.5 %all-to-all-done.got_ref = f32[16,40,128]{2,1,0:T(8,128)S(1)} async-done(((f32[16,40,128]{2,1,0:T(8,128)}), f32[16,40,128]{2,1,0:T(8,128)S(1)}, u32[]{:S(2)}, u32[]{:S(2)}) %all-to-all-start) | async-done | bytes 327712 | tf_op jit(solution)/shard_map/all_to_all | solution.py:151
  40.5 11.9 %collective-permute-start = (f32[80,1024]{1,0:T(8,128)S(1)}, f32[80,1024]{1,0:T(8,128)S(1)}, u32[]{:S(2)}, u32[]{:S(2)}) collective-permute-start(f32[80,1024]{1,0:T(8,128)S(1)} %symmetrize.1), channel_id=1, source_target_pairs={{0,128},{128,384},{384,256},{256,0},{1,129},{129,385},{385,257},{2... | collective-permute-start | bytes 983048 | tf_op jit(solution)/shard_map/ppermute | solution.py:163
  53.9 4.7 %collective-permute-start.6 = (f32[96,128]{1,0:T(8,128)S(1)}, f32[96,128]{1,0:T(8,128)S(1)}, u32[]{:S(2)}, u32[]{:S(2)}) collective-permute-start(f32[96,128]{1,0:T(8,128)S(1)} %slice.36), channel_id=1, source_target_pairs={{0,1},{1,2},{2,3},{3,0},{4,5},{5,6},{6,7},{7,4},{8,9},{9,10},{10,1... | collective-permute-start | bytes 147464 | tf_op jit(solution)/shard_map/ppermute | solution.py:113
  58.6 4.5 %collective-permute-start.7 = (f32[96,128]{1,0:T(8,128)S(1)}, f32[96,128]{1,0:T(8,128)S(1)}, u32[]{:S(2)}, u32[]{:S(2)}) collective-permute-start(f32[96,128]{1,0:T(8,128)S(1)} %slice.37), channel_id=1, source_target_pairs={{0,3},{1,0},{2,1},{3,2},{4,7},{5,4},{6,5},{7,6},{8,11},{9,8},{10,9... | collective-permute-start | bytes 147464 | tf_op jit(solution)/shard_map/ppermute | solution.py:113
  63.2 3.1 %collective-permute-start.1 = (f32[160,1024]{1,0:T(8,128)S(1)}, f32[160,1024]{1,0:T(8,128)S(1)}, u32[]{:S(2)}, u32[]{:S(2)}) collective-permute-start(f32[160,1024]{1,0:T(8,128)S(1)} %pad_maximum_fusion.refs_0_), channel_id=1, source_target_pairs={{0,32},{32,64},{64,96},{96,0},{1,33},{33,65},{65,97},{97,1},{2,34}... | collective-permute-start | bytes 1966088 | tf_op jit(solution)/shard_map/ppermute | solution.py:113
  66.3 1.9 %collective-permute-start.9 = (f32[80,1024]{1,0:T(8,128)S(1)}, f32[80,1024]{1,0:T(8,128)}, u32[]{:S(2)}, u32[]{:S(2)}) collective-permute-start(f32[80,1024]{1,0:T(8,128)S(1)} %collective-permute-done), channel_id=1, source_target_pairs={{0,128},{128,384},{384,256},{256,0},{1,129},{129,385},{385,257},{2... | collective-permute-start | bytes 983048 | tf_op jit(solution)/shard_map/ppermute | solution.py:163
  69.6 3.6 %all-to-all-start.1 = ((f32[4,768,128]{2,1,0:T(8,128)}), f32[4,768,128]{2,1,0:T(8,128)S(1)}, u32[]{:S(2)}, u32[]{:S(2)}) async-start(f32[4,768,128]{2,1,0:T(8,128)} %copies.1), calls=%async_computation.1 | async-start | bytes 3145728 | tf_op jit(solution)/shard_map/all_to_all | solution.py:144
  73.2 2.1 %collective-permute-done.9 = f32[80,1024]{1,0:T(8,128)} collective-permute-done((f32[80,1024]{1,0:T(8,128)S(1)}, f32[80,1024]{1,0:T(8,128)}, u32[]{:S(2)}, u32[]{:S(2)}) %collective-permute-start.9) | collective-permute-done | bytes 327712 | tf_op jit(solution)/shard_map/ppermute | solution.py:163
  75.3 3.2 %collective-permute-start.10 = (f32[80,1024]{1,0:T(8,128)}, f32[80,1024]{1,0:T(8,128)S(1)}, u32[]{:S(2)}, u32[]{:S(2)}) collective-permute-start(f32[80,1024]{1,0:T(8,128)} %collective-permute-done.9), channel_id=1, source_target_pairs={{0,128},{128,384},{384,256},{256,0},{1,129},{129,385},{385,257},{2... | collective-permute-start | bytes 983048 | tf_op jit(solution)/shard_map/ppermute | solution.py:163
  78.5 3.4 %collective-permute-start.2 = (f32[160,1024]{1,0:T(8,128)S(1)}, f32[160,1024]{1,0:T(8,128)}, u32[]{:S(2)}, u32[]{:S(2)}) collective-permute-start(f32[160,1024]{1,0:T(8,128)S(1)} %pad_maximum_fusion.refs_0_), channel_id=1, source_target_pairs={{0,96},{32,0},{64,32},{96,64},{1,97},{33,1},{65,33},{97,65},{2,98}... | collective-permute-start | bytes 1966088 | tf_op jit(solution)/shard_map/ppermute | solution.py:113
  82.9 1.9 %collective-permute-start.3 = (f32[160,1024]{1,0:T(8,128)S(1)}, f32[160,1024]{1,0:T(8,128)}, u32[]{:S(2)}, u32[]{:S(2)}) collective-permute-start(f32[160,1024]{1,0:T(8,128)S(1)} %collective-permute-done.1.refs_1_), channel_id=1, source_target_pairs={{0,32},{32,64},{64,96},{96,0},{1,33},{33,65},{65,97},{97,1},{2,34}... | collective-permute-start | bytes 1966088 | tf_op jit(solution)/shard_map/ppermute | solution.py:174
  84.9 4.6 %collective-permute-start.12 = (f32[160,1024]{1,0:T(8,128)S(1)}, f32[160,1024]{1,0:T(8,128)}, u32[]{:S(2)}, u32[]{:S(2)}) collective-permute-start(f32[160,1024]{1,0:T(8,128)S(1)} %constant_dynamic-update-slice_fusion.refs_0_), channel_id=1, source_target_pairs={{0,96},{32,0},{64,32},{96,64},{1,97},{33,1},{65,33},{97,65},{2,98}... | collective-permute-start | bytes 1966088 | tf_op jit(solution)/shard_map/ppermute | solution.py:113
  92.1 5.3 %collective-permute-done.3.refs_3_ = f32[160,1024]{1,0:T(8,128)} collective-permute-done((f32[160,1024]{1,0:T(8,128)S(1)}, f32[160,1024]{1,0:T(8,128)}, u32[]{:S(2)}, u32[]{:S(2)}) %collective-permute-start.3) | collective-permute-done | bytes 655392 | tf_op jit(solution)/shard_map/ppermute | solution.py:174
  98.1 4.9 %antisym.1 = (f32[152,1280]{1,0:T(8,128)S(1)}, f32[152,1280]{1,0:T(8,128)S(1)}) custom-call(s32[32]{0:T(128)S(1)} %copy-done.1, s32[32]{0:T(128)S(1)} %get-tuple-element.25.base_ref, s32[2560]{0:T(1024)S(1)} %fusion.3.other_ref, f32[3072,128]{1,0:T(8,128)S(1)} %bitcast.42), custom_call_target="tpu_custom_call" | custom-call | flops 389120 | bytes 24903680 | tf_op jit(solution)/shard_map/antisym/pallas_call | solution.py:189
  103.0 7.8 %collective-permute-start.8 = (f32[152,1280]{1,0:T(8,128)S(1)}, f32[152,1280]{1,0:T(8,128)S(1)}, u32[]{:S(2)}, u32[]{:S(2)}) collective-permute-start(f32[152,1280]{1,0:T(8,128)S(1)} %get-tuple-element.17), channel_id=1, source_target_pairs={{0,16},{16,0},{1,17},{17,1},{2,18},{18,2},{3,19},{19,3},{4,20},{20... | collective-permute-start | bytes 2334728 | tf_op jit(solution)/shard_map/ppermute | solution.py:199
  110.8 2.7 %collective-permute-start.11 = (f32[160,1024]{1,0:T(8,128)S(1)}, f32[160,1024]{1,0:T(8,128)S(1)}, u32[]{:S(2)}, u32[]{:S(2)}) collective-permute-start(f32[160,1024]{1,0:T(8,128)S(1)} %constant_dynamic-update-slice_fusion.refs_0_), channel_id=1, source_target_pairs={{0,32},{32,64},{64,96},{96,0},{1,33},{33,65},{65,97},{97,1},{2,34}... | collective-permute-start | bytes 1966088 | tf_op jit(solution)/shard_map/ppermute | solution.py:113
  113.5 3.8 %collective-permute-start.13 = (f32[160,1024]{1,0:T(8,128)}, f32[160,1024]{1,0:T(8,128)S(1)}, u32[]{:S(2)}, u32[]{:S(2)}) collective-permute-start(f32[160,1024]{1,0:T(8,128)} %collective-permute-done.12.refs_2_), channel_id=1, source_target_pairs={{0,96},{32,0},{64,32},{96,64},{1,97},{33,1},{65,33},{97,65},{2,98}... | collective-permute-start | bytes 1966088 | tf_op jit(solution)/shard_map/ppermute | solution.py:174
  117.3 2.9 %product.2 = (f32[152,1024]{1,0:T(8,128)S(1)}, f32[152,1024]{1,0:T(8,128)S(1)}) custom-call(f32[152,1280]{1,0:T(8,128)S(1)} %get-tuple-element.16.mine_ref, f32[152,1280]{1,0:T(8,128)S(1)} %collective-permute-done.8.theirs_ref, f32[160,1024]{1,0:T(8,128)S(1)} %pad_maximum_fusion.refs_0_, f32[160,1024]{1,0:T(8,128)S(1)} %collective-permute-done.1.refs_1_, ...), custom_call_target="tpu_custom_call" | custom-call | flops 398458880 | bytes 1048576 | tf_op jit(solution)/shard_map/product/pallas_call | solution.py:202
  120.2 10.0 %collective-permute-done.11.refs_1_ = f32[160,1024]{1,0:T(8,128)S(1)} collective-permute-done((f32[160,1024]{1,0:T(8,128)S(1)}, f32[160,1024]{1,0:T(8,128)S(1)}, u32[]{:S(2)}, u32[]{:S(2)}) %collective-permute-start.11) | collective-permute-done | bytes 655392 | tf_op jit(solution)/shard_map/ppermute | solution.py:113
  131.6 2.7 %product.3 = (f32[152,1024]{1,0:T(8,128)S(1)}, f32[152,1024]{1,0:T(8,128)S(1)}) custom-call(f32[152,1280]{1,0:T(8,128)S(1)} %get-tuple-element.16.mine_ref, f32[152,1280]{1,0:T(8,128)S(1)} %collective-permute-done.8.theirs_ref, f32[160,1024]{1,0:T(8,128)S(1)} %constant_dynamic-update-slice_fusion.refs_0_, f32[160,1024]{1,0:T(8,128)S(1)} %collective-permute-done.11.refs_1_, ...), custom_call_target="tpu_custom_call" | custom-call | flops 398458880 | bytes 1048576 | tf_op jit(solution)/shard_map/product/pallas_call | solution.py:202
  134.4 3.0 %collective-permute-start.14 = (f32[152,1024]{1,0:T(8,128)S(1)}, f32[152,1024]{1,0:T(8,128)S(1)}, u32[]{:S(2)}, u32[]{:S(2)}) collective-permute-start(f32[152,1024]{1,0:T(8,128)S(1)} %get-tuple-element.24), channel_id=1, source_target_pairs={{0,16},{16,0},{1,17},{17,1},{2,18},{18,2},{3,19},{19,3},{4,20},{20... | collective-permute-start | bytes 1867784 | tf_op jit(solution)/shard_map/ppermute | solution.py:214
  (51 shorter events, 14.4 us)
Async XLA Ops:
  0.0 20.8 %copy-start.3 = (f32[152,160]{1,0:T(8,128)S(1)}, f32[152,160]{1,0:T(8,128)}, u32[]{:S(2)}) copy-start(f32[152,160]{1,0:T(8,128)} %param.8) | copy-start | bytes 291844
  1.2 29.0 %copy-start.2 = (s32[4]{0:T(128)S(1)}, s32[4]{0:T(128)}, u32[]{:S(2)}) copy-start(s32[4]{0:T(128)} %constant.111.clone) | copy-start | bytes 52
  1.2 39.1 %copy-start = (f32[80,1024]{1,0:T(8,128)S(1)}, f32[80,1024]{1,0:T(8,128)}, u32[]{:S(2)}) copy-start(f32[80,1024]{1,0:T(8,128)} %integrals_ref.1) | copy-start | bytes 983044
  1.4 51.0 %copy-start.6 = (s32[16,1]{0,1:T(1,128)S(1)}, s32[16,1]{0,1:T(1,128)}, u32[]{:S(2)}) copy-start(s32[16,1]{0,1:T(1,128)} %constant.119) | copy-start | bytes 196
  2.4 38.0 %all-to-all-start = ((f32[16,40,128]{2,1,0:T(8,128)}), f32[16,40,128]{2,1,0:T(8,128)S(1)}, u32[]{:S(2)}, u32[]{:S(2)}) async-start(f32[16,40,128]{2,1,0:T(8,128)} %bitcast.41), calls=%async_computation | async-start | bytes 655360 | tf_op jit(solution)/shard_map/all_to_all | solution.py:151
  21.0 47.3 %copy-start.5 = (s32[16,1]{0,1:T(1,128)S(1)}, s32[16,1]{0,1:T(1,128)}, u32[]{:S(2)}) copy-start(s32[16,1]{0,1:T(1,128)} %constant.118) | copy-start | bytes 196
  21.0 32.9 %collective-permute-start.4 = (f32[192,128]{1,0:T(8,128)S(1)}, f32[192,128]{1,0:T(8,128)S(1)}, u32[]{:S(2)}, u32[]{:S(2)}) collective-permute-start(f32[192,128]{1,0:T(8,128)S(1)} %pack.1.refs_0_), channel_id=1, source_target_pairs={{0,1},{1,2},{2,3},{3,0},{4,5},{5,6},{6,7},{7,4},{8,9},{9,10},{10,1... | collective-permute-start | bytes 294920 | tf_op jit(solution)/shard_map/ppermute | solution.py:113
  28.2 30.4 %collective-permute-start.5 = (f32[192,128]{1,0:T(8,128)S(1)}, f32[192,128]{1,0:T(8,128)S(1)}, u32[]{:S(2)}, u32[]{:S(2)}) collective-permute-start(f32[192,128]{1,0:T(8,128)S(1)} %pack.1.refs_0_), channel_id=1, source_target_pairs={{0,3},{1,0},{2,1},{3,2},{4,7},{5,4},{6,5},{7,6},{8,11},{9,8},{10,9... | collective-permute-start | bytes 294920 | tf_op jit(solution)/shard_map/ppermute | solution.py:113
  40.5 22.6 %collective-permute-start = (f32[80,1024]{1,0:T(8,128)S(1)}, f32[80,1024]{1,0:T(8,128)S(1)}, u32[]{:S(2)}, u32[]{:S(2)}) collective-permute-start(f32[80,1024]{1,0:T(8,128)S(1)} %symmetrize.1), channel_id=1, source_target_pairs={{0,128},{128,384},{384,256},{256,0},{1,129},{129,385},{385,257},{2... | collective-permute-start | bytes 983048 | tf_op jit(solution)/shard_map/ppermute | solution.py:163
  53.9 14.4 %collective-permute-start.6 = (f32[96,128]{1,0:T(8,128)S(1)}, f32[96,128]{1,0:T(8,128)S(1)}, u32[]{:S(2)}, u32[]{:S(2)}) collective-permute-start(f32[96,128]{1,0:T(8,128)S(1)} %slice.36), channel_id=1, source_target_pairs={{0,1},{1,2},{2,3},{3,0},{4,5},{5,6},{6,7},{7,4},{8,9},{9,10},{10,1... | collective-permute-start | bytes 147464 | tf_op jit(solution)/shard_map/ppermute | solution.py:113
  58.6 9.7 %collective-permute-start.7 = (f32[96,128]{1,0:T(8,128)S(1)}, f32[96,128]{1,0:T(8,128)S(1)}, u32[]{:S(2)}, u32[]{:S(2)}) collective-permute-start(f32[96,128]{1,0:T(8,128)S(1)} %slice.37), channel_id=1, source_target_pairs={{0,3},{1,0},{2,1},{3,2},{4,7},{5,4},{6,5},{7,6},{8,11},{9,8},{10,9... | collective-permute-start | bytes 147464 | tf_op jit(solution)/shard_map/ppermute | solution.py:113
  63.2 19.7 %collective-permute-start.1 = (f32[160,1024]{1,0:T(8,128)S(1)}, f32[160,1024]{1,0:T(8,128)S(1)}, u32[]{:S(2)}, u32[]{:S(2)}) collective-permute-start(f32[160,1024]{1,0:T(8,128)S(1)} %pad_maximum_fusion.refs_0_), channel_id=1, source_target_pairs={{0,32},{32,64},{64,96},{96,0},{1,33},{33,65},{65,97},{97,1},{2,34}... | collective-permute-start | bytes 1966088 | tf_op jit(solution)/shard_map/ppermute | solution.py:113
  66.3 9.0 %collective-permute-start.9 = (f32[80,1024]{1,0:T(8,128)S(1)}, f32[80,1024]{1,0:T(8,128)}, u32[]{:S(2)}, u32[]{:S(2)}) collective-permute-start(f32[80,1024]{1,0:T(8,128)S(1)} %collective-permute-done), channel_id=1, source_target_pairs={{0,128},{128,384},{384,256},{256,0},{1,129},{129,385},{385,257},{2... | collective-permute-start | bytes 983048 | tf_op jit(solution)/shard_map/ppermute | solution.py:163
  69.6 21.2 %all-to-all-start.1 = ((f32[4,768,128]{2,1,0:T(8,128)}), f32[4,768,128]{2,1,0:T(8,128)S(1)}, u32[]{:S(2)}, u32[]{:S(2)}) async-start(f32[4,768,128]{2,1,0:T(8,128)} %copies.1), calls=%async_computation.1 | async-start | bytes 3145728 | tf_op jit(solution)/shard_map/all_to_all | solution.py:144
  75.3 9.5 %collective-permute-start.10 = (f32[80,1024]{1,0:T(8,128)}, f32[80,1024]{1,0:T(8,128)S(1)}, u32[]{:S(2)}, u32[]{:S(2)}) collective-permute-start(f32[80,1024]{1,0:T(8,128)} %collective-permute-done.9), channel_id=1, source_target_pairs={{0,128},{128,384},{384,256},{256,0},{1,129},{129,385},{385,257},{2... | collective-permute-start | bytes 983048 | tf_op jit(solution)/shard_map/ppermute | solution.py:163
  78.5 13.6 %collective-permute-start.2 = (f32[160,1024]{1,0:T(8,128)S(1)}, f32[160,1024]{1,0:T(8,128)}, u32[]{:S(2)}, u32[]{:S(2)}) collective-permute-start(f32[160,1024]{1,0:T(8,128)S(1)} %pad_maximum_fusion.refs_0_), channel_id=1, source_target_pairs={{0,96},{32,0},{64,32},{96,64},{1,97},{33,1},{65,33},{97,65},{2,98}... | collective-permute-start | bytes 1966088 | tf_op jit(solution)/shard_map/ppermute | solution.py:113
  82.9 14.5 %collective-permute-start.3 = (f32[160,1024]{1,0:T(8,128)S(1)}, f32[160,1024]{1,0:T(8,128)}, u32[]{:S(2)}, u32[]{:S(2)}) collective-permute-start(f32[160,1024]{1,0:T(8,128)S(1)} %collective-permute-done.1.refs_1_), channel_id=1, source_target_pairs={{0,32},{32,64},{64,96},{96,0},{1,33},{33,65},{65,97},{97,1},{2,34}... | collective-permute-start | bytes 1966088 | tf_op jit(solution)/shard_map/ppermute | solution.py:174
  84.9 28.6 %collective-permute-start.12 = (f32[160,1024]{1,0:T(8,128)S(1)}, f32[160,1024]{1,0:T(8,128)}, u32[]{:S(2)}, u32[]{:S(2)}) collective-permute-start(f32[160,1024]{1,0:T(8,128)S(1)} %constant_dynamic-update-slice_fusion.refs_0_), channel_id=1, source_target_pairs={{0,96},{32,0},{64,32},{96,64},{1,97},{33,1},{65,33},{97,65},{2,98}... | collective-permute-start | bytes 1966088 | tf_op jit(solution)/shard_map/ppermute | solution.py:113
  97.4 0.7 copy-start.1
  103.0 14.3 %collective-permute-start.8 = (f32[152,1280]{1,0:T(8,128)S(1)}, f32[152,1280]{1,0:T(8,128)S(1)}, u32[]{:S(2)}, u32[]{:S(2)}) collective-permute-start(f32[152,1280]{1,0:T(8,128)S(1)} %get-tuple-element.17), channel_id=1, source_target_pairs={{0,16},{16,0},{1,17},{17,1},{2,18},{18,2},{3,19},{19,3},{4,20},{20... | collective-permute-start | bytes 2334728 | tf_op jit(solution)/shard_map/ppermute | solution.py:199
  110.8 19.5 %collective-permute-start.11 = (f32[160,1024]{1,0:T(8,128)S(1)}, f32[160,1024]{1,0:T(8,128)S(1)}, u32[]{:S(2)}, u32[]{:S(2)}) collective-permute-start(f32[160,1024]{1,0:T(8,128)S(1)} %constant_dynamic-update-slice_fusion.refs_0_), channel_id=1, source_target_pairs={{0,32},{32,64},{64,96},{96,0},{1,33},{33,65},{65,97},{97,1},{2,34}... | collective-permute-start | bytes 1966088 | tf_op jit(solution)/shard_map/ppermute | solution.py:113
  113.5 18.1 %collective-permute-start.13 = (f32[160,1024]{1,0:T(8,128)}, f32[160,1024]{1,0:T(8,128)S(1)}, u32[]{:S(2)}, u32[]{:S(2)}) collective-permute-start(f32[160,1024]{1,0:T(8,128)} %collective-permute-done.12.refs_2_), channel_id=1, source_target_pairs={{0,96},{32,0},{64,32},{96,64},{1,97},{33,1},{65,33},{97,65},{2,98}... | collective-permute-start | bytes 1966088 | tf_op jit(solution)/shard_map/ppermute | solution.py:174
  131.6 5.8 %copy-start.4 = (s32[152,2]{0,1:T(2,128)S(1)}, s32[152,2]{0,1:T(2,128)}, u32[]{:S(2)}) copy-start(s32[152,2]{0,1:T(2,128)} %param.10) | copy-start | bytes 3652
  134.4 4.7 %collective-permute-start.14 = (f32[152,1024]{1,0:T(8,128)S(1)}, f32[152,1024]{1,0:T(8,128)S(1)}, u32[]{:S(2)}, u32[]{:S(2)}) collective-permute-start(f32[152,1024]{1,0:T(8,128)S(1)} %get-tuple-element.24), channel_id=1, source_target_pairs={{0,16},{16,0},{1,17},{17,1},{2,18},{18,2},{3,19},{19,3},{4,20},{20... | collective-permute-start | bytes 1867784 | tf_op jit(solution)/shard_map/ppermute | solution.py:214

commit v7 on v5

--- a/solution.py
+++ b/solution.py
@@ -205,7 +205,7 @@
             in_specs=[VMEM] * (2 + len(pieces) + len(sums)),
             out_specs=[VMEM] * 2,
             scratch_shapes=[pltpu.VMEM((slab // 4, columns), jnp.bfloat16)] * 2,
-            compiler_params=pltpu.CompilerParams(vmem_limit_bytes=16 * 2**20),
+            compiler_params=pltpu.CompilerParams(vmem_limit_bytes=12 * 2**20),
             cost_estimate=pl.CostEstimate(flops=3 * pairs * slab * columns, bytes_accessed=4 * 2**20, transcendentals=0),
             name="product",
         )(mine, theirs, *pieces, *sums)

time: 140 us -> 140 us (level)
  no operation moved by 1% of the time
where the time goes in v7:
time: 140 us; the launch traced here: 139 us
  starting transfers between devices  87.1 us (62%)
  waiting for transfers between devices  31.2 us (22%)
  Pallas kernels  11.2 us (8%)
  local copies, waits for them, and re-layouts  4.5 us (3%)
  other arithmetic  4.29 us (3%)
    all_to_all x1, starting transfers between devices, body(): got = lax.all_to_all(sent, VIR, split_axis=0, concat_axis=0, tiled=True)  18.4 us
    ppermute x4, starting transfers between devices, around(): lax.ppermute(up, axis, shift(4, 1))  18.3 us
    ppermute x3, starting transfers between devices, lower(): lax.ppermute(block, 'zl', [(RING[i], RING[(i + 1) % 4]) for i in range(4)])  16.9 us
    ppermute x4, starting transfers between devices, around(): lax.ppermute(down, axis, shift(4, -1))  13.9 us
    ppermute x4, waiting for transfers between devices, around(): lax.ppermute(up, axis, shift(4, 1))  9.83 us
    all_to_all x1, waiting for transfers between devices, body(): got = lax.all_to_all(sent, VIR, split_axis=0, concat_axis=0, tiled=True)  9.49 us
    ppermute x1, starting transfers between devices, body(): theirs = lax.ppermute(theirs, 'c', shift(2, 1))  7.85 us
    ppermute x2, waiting for transfers between devices, body(): pieces += part + [lax.ppermute(part[1 + i // 2], 'x', shift(4, 1 - i))]  6.3 us
  transfers between devices with their start and end apart: 17, of which 8 were waited for; matrix products, arithmetic and copies ran while one was open for 3% of the time, Pallas kernels for 7%

profile of v7, /device:TPU:1, one launch (start us, length us, event | category | flops | bytes accessed | tf_op | source)
XLA Modules:
  0.0 138.7 jit_solution(15259555383136112165)
XLA Ops:
  2.4 18.4 %all-to-all-start = ((f32[16,40,128]{2,1,0:T(8,128)}), f32[16,40,128]{2,1,0:T(8,128)S(1)}, u32[]{:S(2)}, u32[]{:S(2)}) async-start(f32[16,40,128]{2,1,0:T(8,128)} %bitcast.41), calls=%async_computation | async-start | bytes 655360 | tf_op jit(solution)/shard_map/all_to_all | solution.py:151
  21.0 7.2 %collective-permute-start.4 = (f32[192,128]{1,0:T(8,128)S(1)}, f32[192,128]{1,0:T(8,128)S(1)}, u32[]{:S(2)}, u32[]{:S(2)}) collective-permute-start(f32[192,128]{1,0:T(8,128)S(1)} %pack.1.refs_0_), channel_id=1, source_target_pairs={{0,1},{1,2},{2,3},{3,0},{4,5},{5,6},{6,7},{7,4},{8,9},{9,10},{10,1... | collective-permute-start | bytes 294920 | tf_op jit(solution)/shard_map/ppermute | solution.py:113
  28.2 2.0 %collective-permute-start.5 = (f32[192,128]{1,0:T(8,128)S(1)}, f32[192,128]{1,0:T(8,128)S(1)}, u32[]{:S(2)}, u32[]{:S(2)}) collective-permute-start(f32[192,128]{1,0:T(8,128)S(1)} %pack.1.refs_0_), channel_id=1, source_target_pairs={{0,3},{1,0},{2,1},{3,2},{4,7},{5,4},{6,5},{7,6},{8,11},{9,8},{10,9... | collective-permute-start | bytes 294920 | tf_op jit(solution)/shard_map/ppermute | solution.py:113
  30.9 9.5 %all-to-all-done.got_ref = f32[16,40,128]{2,1,0:T(8,128)S(1)} async-done(((f32[16,40,128]{2,1,0:T(8,128)}), f32[16,40,128]{2,1,0:T(8,128)S(1)}, u32[]{:S(2)}, u32[]{:S(2)}) %all-to-all-start) | async-done | bytes 327712 | tf_op jit(solution)/shard_map/all_to_all | solution.py:151
  40.5 11.9 %collective-permute-start = (f32[80,1024]{1,0:T(8,128)S(1)}, f32[80,1024]{1,0:T(8,128)S(1)}, u32[]{:S(2)}, u32[]{:S(2)}) collective-permute-start(f32[80,1024]{1,0:T(8,128)S(1)} %symmetrize.1), channel_id=1, source_target_pairs={{0,128},{128,384},{384,256},{256,0},{1,129},{129,385},{385,257},{2... | collective-permute-start | bytes 983048 | tf_op jit(solution)/shard_map/ppermute | solution.py:163
  53.9 4.7 %collective-permute-start.6 = (f32[96,128]{1,0:T(8,128)S(1)}, f32[96,128]{1,0:T(8,128)S(1)}, u32[]{:S(2)}, u32[]{:S(2)}) collective-permute-start(f32[96,128]{1,0:T(8,128)S(1)} %slice.36), channel_id=1, source_target_pairs={{0,1},{1,2},{2,3},{3,0},{4,5},{5,6},{6,7},{7,4},{8,9},{9,10},{10,1... | collective-permute-start | bytes 147464 | tf_op jit(solution)/shard_map/ppermute | solution.py:113
  58.6 4.5 %collective-permute-start.7 = (f32[96,128]{1,0:T(8,128)S(1)}, f32[96,128]{1,0:T(8,128)S(1)}, u32[]{:S(2)}, u32[]{:S(2)}) collective-permute-start(f32[96,128]{1,0:T(8,128)S(1)} %slice.37), channel_id=1, source_target_pairs={{0,3},{1,0},{2,1},{3,2},{4,7},{5,4},{6,5},{7,6},{8,11},{9,8},{10,9... | collective-permute-start | bytes 147464 | tf_op jit(solution)/shard_map/ppermute | solution.py:113
  63.2 3.1 %collective-permute-start.1 = (f32[160,1024]{1,0:T(8,128)S(1)}, f32[160,1024]{1,0:T(8,128)}, u32[]{:S(2)}, u32[]{:S(2)}) collective-permute-start(f32[160,1024]{1,0:T(8,128)S(1)} %pad_maximum_fusion.refs_0_), channel_id=1, source_target_pairs={{0,32},{32,64},{64,96},{96,0},{1,33},{33,65},{65,97},{97,1},{2,34}... | collective-permute-start | bytes 1966088 | tf_op jit(solution)/shard_map/ppermute | solution.py:113
  66.3 1.9 %collective-permute-start.9 = (f32[80,1024]{1,0:T(8,128)S(1)}, f32[80,1024]{1,0:T(8,128)S(1)}, u32[]{:S(2)}, u32[]{:S(2)}) collective-permute-start(f32[80,1024]{1,0:T(8,128)S(1)} %collective-permute-done), channel_id=1, source_target_pairs={{0,128},{128,384},{384,256},{256,0},{1,129},{129,385},{385,257},{2... | collective-permute-start | bytes 983048 | tf_op jit(solution)/shard_map/ppermute | solution.py:163
  69.6 3.6 %all-to-all-start.1 = ((f32[4,768,128]{2,1,0:T(8,128)}), f32[4,768,128]{2,1,0:T(8,128)S(1)}, u32[]{:S(2)}, u32[]{:S(2)}) async-start(f32[4,768,128]{2,1,0:T(8,128)} %copies.1), calls=%async_computation.1 | async-start | bytes 3145728 | tf_op jit(solution)/shard_map/all_to_all | solution.py:144
  73.2 2.3 %collective-permute-done.9 = f32[80,1024]{1,0:T(8,128)S(1)} collective-permute-done((f32[80,1024]{1,0:T(8,128)S(1)}, f32[80,1024]{1,0:T(8,128)S(1)}, u32[]{:S(2)}, u32[]{:S(2)}) %collective-permute-start.9) | collective-permute-done | bytes 327712 | tf_op jit(solution)/shard_map/ppermute | solution.py:163
  75.4 3.1 %collective-permute-start.10 = (f32[80,1024]{1,0:T(8,128)S(1)}, f32[80,1024]{1,0:T(8,128)S(1)}, u32[]{:S(2)}, u32[]{:S(2)}) collective-permute-start(f32[80,1024]{1,0:T(8,128)S(1)} %collective-permute-done.9), channel_id=1, source_target_pairs={{0,128},{128,384},{384,256},{256,0},{1,129},{129,385},{385,257},{2... | collective-permute-start | bytes 983048 | tf_op jit(solution)/shard_map/ppermute | solution.py:163
  78.5 3.4 %collective-permute-start.2 = (f32[160,1024]{1,0:T(8,128)S(1)}, f32[160,1024]{1,0:T(8,128)}, u32[]{:S(2)}, u32[]{:S(2)}) collective-permute-start(f32[160,1024]{1,0:T(8,128)S(1)} %pad_maximum_fusion.refs_0_), channel_id=1, source_target_pairs={{0,96},{32,0},{64,32},{96,64},{1,97},{33,1},{65,33},{97,65},{2,98}... | collective-permute-start | bytes 1966088 | tf_op jit(solution)/shard_map/ppermute | solution.py:113
  81.9 1.9 %collective-permute-start.3 = (f32[160,1024]{1,0:T(8,128)}, f32[160,1024]{1,0:T(8,128)}, u32[]{:S(2)}, u32[]{:S(2)}) collective-permute-start(f32[160,1024]{1,0:T(8,128)} %collective-permute-done.1.refs_1_), channel_id=1, source_target_pairs={{0,32},{32,64},{64,96},{96,0},{1,33},{33,65},{65,97},{97,1},{2,34}... | collective-permute-start | bytes 1966088 | tf_op jit(solution)/shard_map/ppermute | solution.py:174
  84.4 4.0 %collective-permute-start.12 = (f32[160,1024]{1,0:T(8,128)S(1)}, f32[160,1024]{1,0:T(8,128)S(1)}, u32[]{:S(2)}, u32[]{:S(2)}) collective-permute-start(f32[160,1024]{1,0:T(8,128)S(1)} %constant_dynamic-update-slice_fusion.refs_0_), channel_id=1, source_target_pairs={{0,96},{32,0},{64,32},{96,64},{1,97},{33,1},{65,33},{97,65},{2,98}... | collective-permute-start | bytes 1966088 | tf_op jit(solution)/shard_map/ppermute | solution.py:113
  92.2 4.6 %collective-permute-done.3.refs_3_ = f32[160,1024]{1,0:T(8,128)} collective-permute-done((f32[160,1024]{1,0:T(8,128)}, f32[160,1024]{1,0:T(8,128)}, u32[]{:S(2)}, u32[]{:S(2)}) %collective-permute-start.3) | collective-permute-done | bytes 655392 | tf_op jit(solution)/shard_map/ppermute | solution.py:174
  97.4 4.9 %antisym.1 = (f32[152,1280]{1,0:T(8,128)S(1)}, f32[152,1280]{1,0:T(8,128)S(1)}) custom-call(s32[32]{0:T(128)S(1)} %copy-done.1, s32[32]{0:T(128)S(1)} %get-tuple-element.25.base_ref, s32[2560]{0:T(1024)S(1)} %fusion.3.other_ref, f32[3072,128]{1,0:T(8,128)S(1)} %bitcast.42), custom_call_target="tpu_custom_call" | custom-call | flops 389120 | bytes 4669440 | tf_op jit(solution)/shard_map/antisym/pallas_call | solution.py:189
  102.4 7.9 %collective-permute-start.8 = (f32[152,1280]{1,0:T(8,128)S(1)}, f32[152,1280]{1,0:T(8,128)S(1)}, u32[]{:S(2)}, u32[]{:S(2)}) collective-permute-start(f32[152,1280]{1,0:T(8,128)S(1)} %get-tuple-element.17), channel_id=1, source_target_pairs={{0,16},{16,0},{1,17},{17,1},{2,18},{18,2},{3,19},{19,3},{4,20},{20... | collective-permute-start | bytes 2334728 | tf_op jit(solution)/shard_map/ppermute | solution.py:199
  110.2 3.3 %collective-permute-start.11 = (f32[160,1024]{1,0:T(8,128)S(1)}, f32[160,1024]{1,0:T(8,128)S(1)}, u32[]{:S(2)}, u32[]{:S(2)}) collective-permute-start(f32[160,1024]{1,0:T(8,128)S(1)} %constant_dynamic-update-slice_fusion.refs_0_), channel_id=1, source_target_pairs={{0,32},{32,64},{64,96},{96,0},{1,33},{33,65},{65,97},{97,1},{2,34}... | collective-permute-start | bytes 1966088 | tf_op jit(solution)/shard_map/ppermute | solution.py:113
  113.5 3.2 %collective-permute-start.13 = (f32[160,1024]{1,0:T(8,128)S(1)}, f32[160,1024]{1,0:T(8,128)S(1)}, u32[]{:S(2)}, u32[]{:S(2)}) collective-permute-start(f32[160,1024]{1,0:T(8,128)S(1)} %collective-permute-done.12.refs_2_), channel_id=1, source_target_pairs={{0,96},{32,0},{64,32},{96,64},{1,97},{33,1},{65,33},{97,65},{2,98}... | collective-permute-start | bytes 1966088 | tf_op jit(solution)/shard_map/ppermute | solution.py:174
  116.8 3.1 %product.2 = (f32[152,1024]{1,0:T(8,128)S(1)}, f32[152,1024]{1,0:T(8,128)S(1)}) custom-call(f32[152,1280]{1,0:T(8,128)S(1)} %get-tuple-element.16.mine_ref, f32[152,1280]{1,0:T(8,128)S(1)} %collective-permute-done.8.theirs_ref, f32[160,1024]{1,0:T(8,128)S(1)} %pad_maximum_fusion.refs_0_, f32[160,1024]{1,0:T(8,128)} %collective-permute-done.1.refs_1_, ...), custom_call_target="tpu_custom_call" | custom-call | flops 1195376640 | bytes 4194304 | tf_op jit(solution)/shard_map/product/pallas_call | solution.py:202
  119.9 9.8 %collective-permute-done.11.refs_1_ = f32[160,1024]{1,0:T(8,128)S(1)} collective-permute-done((f32[160,1024]{1,0:T(8,128)S(1)}, f32[160,1024]{1,0:T(8,128)S(1)}, u32[]{:S(2)}, u32[]{:S(2)}) %collective-permute-start.11) | collective-permute-done | bytes 655392 | tf_op jit(solution)/shard_map/ppermute | solution.py:113
  129.7 1.7 %collective-permute-done.13.refs_3_ = f32[160,1024]{1,0:T(8,128)S(1)} collective-permute-done((f32[160,1024]{1,0:T(8,128)S(1)}, f32[160,1024]{1,0:T(8,128)S(1)}, u32[]{:S(2)}, u32[]{:S(2)}) %collective-permute-start.13) | collective-permute-done | bytes 655392 | tf_op jit(solution)/shard_map/ppermute | solution.py:174
  133.1 3.0 %collective-permute-start.14 = (f32[152,1024]{1,0:T(8,128)S(1)}, f32[152,1024]{1,0:T(8,128)S(1)}, u32[]{:S(2)}, u32[]{:S(2)}) collective-permute-start(f32[152,1024]{1,0:T(8,128)S(1)} %get-tuple-element.24), channel_id=1, source_target_pairs={{0,16},{16,0},{1,17},{17,1},{2,18},{18,2},{3,19},{19,3},{4,20},{20... | collective-permute-start | bytes 1867784 | tf_op jit(solution)/shard_map/ppermute | solution.py:214
  (51 shorter events, 15.3 us)
Async XLA Ops:
  0.0 20.8 %copy-start.3 = (f32[152,160]{1,0:T(8,128)S(1)}, f32[152,160]{1,0:T(8,128)}, u32[]{:S(2)}) copy-start(f32[152,160]{1,0:T(8,128)} %param.8) | copy-start | bytes 291844
  1.2 29.0 %copy-start.2 = (s32[4]{0:T(128)S(1)}, s32[4]{0:T(128)}, u32[]{:S(2)}) copy-start(s32[4]{0:T(128)} %constant.111.clone) | copy-start | bytes 52
  1.2 39.1 %copy-start = (f32[80,1024]{1,0:T(8,128)S(1)}, f32[80,1024]{1,0:T(8,128)}, u32[]{:S(2)}) copy-start(f32[80,1024]{1,0:T(8,128)} %integrals_ref.1) | copy-start | bytes 983044
  1.4 51.0 %copy-start.6 = (s32[16,1]{0,1:T(1,128)S(1)}, s32[16,1]{0,1:T(1,128)}, u32[]{:S(2)}) copy-start(s32[16,1]{0,1:T(1,128)} %constant.119) | copy-start | bytes 196
  2.4 38.0 %all-to-all-start = ((f32[16,40,128]{2,1,0:T(8,128)}), f32[16,40,128]{2,1,0:T(8,128)S(1)}, u32[]{:S(2)}, u32[]{:S(2)}) async-start(f32[16,40,128]{2,1,0:T(8,128)} %bitcast.41), calls=%async_computation | async-start | bytes 655360 | tf_op jit(solution)/shard_map/all_to_all | solution.py:151
  21.0 47.3 %copy-start.5 = (s32[16,1]{0,1:T(1,128)S(1)}, s32[16,1]{0,1:T(1,128)}, u32[]{:S(2)}) copy-start(s32[16,1]{0,1:T(1,128)} %constant.118) | copy-start | bytes 196
  21.0 32.9 %collective-permute-start.4 = (f32[192,128]{1,0:T(8,128)S(1)}, f32[192,128]{1,0:T(8,128)S(1)}, u32[]{:S(2)}, u32[]{:S(2)}) collective-permute-start(f32[192,128]{1,0:T(8,128)S(1)} %pack.1.refs_0_), channel_id=1, source_target_pairs={{0,1},{1,2},{2,3},{3,0},{4,5},{5,6},{6,7},{7,4},{8,9},{9,10},{10,1... | collective-permute-start | bytes 294920 | tf_op jit(solution)/shard_map/ppermute | solution.py:113
  28.2 30.4 %collective-permute-start.5 = (f32[192,128]{1,0:T(8,128)S(1)}, f32[192,128]{1,0:T(8,128)S(1)}, u32[]{:S(2)}, u32[]{:S(2)}) collective-permute-start(f32[192,128]{1,0:T(8,128)S(1)} %pack.1.refs_0_), channel_id=1, source_target_pairs={{0,3},{1,0},{2,1},{3,2},{4,7},{5,4},{6,5},{7,6},{8,11},{9,8},{10,9... | collective-permute-start | bytes 294920 | tf_op jit(solution)/shard_map/ppermute | solution.py:113
  40.5 22.6 %collective-permute-start = (f32[80,1024]{1,0:T(8,128)S(1)}, f32[80,1024]{1,0:T(8,128)S(1)}, u32[]{:S(2)}, u32[]{:S(2)}) collective-permute-start(f32[80,1024]{1,0:T(8,128)S(1)} %symmetrize.1), channel_id=1, source_target_pairs={{0,128},{128,384},{384,256},{256,0},{1,129},{129,385},{385,257},{2... | collective-permute-start | bytes 983048 | tf_op jit(solution)/shard_map/ppermute | solution.py:163
  53.9 14.4 %collective-permute-start.6 = (f32[96,128]{1,0:T(8,128)S(1)}, f32[96,128]{1,0:T(8,128)S(1)}, u32[]{:S(2)}, u32[]{:S(2)}) collective-permute-start(f32[96,128]{1,0:T(8,128)S(1)} %slice.36), channel_id=1, source_target_pairs={{0,1},{1,2},{2,3},{3,0},{4,5},{5,6},{6,7},{7,4},{8,9},{9,10},{10,1... | collective-permute-start | bytes 147464 | tf_op jit(solution)/shard_map/ppermute | solution.py:113
  58.6 9.7 %collective-permute-start.7 = (f32[96,128]{1,0:T(8,128)S(1)}, f32[96,128]{1,0:T(8,128)S(1)}, u32[]{:S(2)}, u32[]{:S(2)}) collective-permute-start(f32[96,128]{1,0:T(8,128)S(1)} %slice.37), channel_id=1, source_target_pairs={{0,3},{1,0},{2,1},{3,2},{4,7},{5,4},{6,5},{7,6},{8,11},{9,8},{10,9... | collective-permute-start | bytes 147464 | tf_op jit(solution)/shard_map/ppermute | solution.py:113
  63.2 18.8 %collective-permute-start.1 = (f32[160,1024]{1,0:T(8,128)S(1)}, f32[160,1024]{1,0:T(8,128)}, u32[]{:S(2)}, u32[]{:S(2)}) collective-permute-start(f32[160,1024]{1,0:T(8,128)S(1)} %pad_maximum_fusion.refs_0_), channel_id=1, source_target_pairs={{0,32},{32,64},{64,96},{96,0},{1,33},{33,65},{65,97},{97,1},{2,34}... | collective-permute-start | bytes 1966088 | tf_op jit(solution)/shard_map/ppermute | solution.py:113
  66.3 9.1 %collective-permute-start.9 = (f32[80,1024]{1,0:T(8,128)S(1)}, f32[80,1024]{1,0:T(8,128)S(1)}, u32[]{:S(2)}, u32[]{:S(2)}) collective-permute-start(f32[80,1024]{1,0:T(8,128)S(1)} %collective-permute-done), channel_id=1, source_target_pairs={{0,128},{128,384},{384,256},{256,0},{1,129},{129,385},{385,257},{2... | collective-permute-start | bytes 983048 | tf_op jit(solution)/shard_map/ppermute | solution.py:163
  69.6 21.5 %all-to-all-start.1 = ((f32[4,768,128]{2,1,0:T(8,128)}), f32[4,768,128]{2,1,0:T(8,128)S(1)}, u32[]{:S(2)}, u32[]{:S(2)}) async-start(f32[4,768,128]{2,1,0:T(8,128)} %copies.1), calls=%async_computation.1 | async-start | bytes 3145728 | tf_op jit(solution)/shard_map/all_to_all | solution.py:144
  75.4 9.0 %collective-permute-start.10 = (f32[80,1024]{1,0:T(8,128)S(1)}, f32[80,1024]{1,0:T(8,128)S(1)}, u32[]{:S(2)}, u32[]{:S(2)}) collective-permute-start(f32[80,1024]{1,0:T(8,128)S(1)} %collective-permute-done.9), channel_id=1, source_target_pairs={{0,128},{128,384},{384,256},{256,0},{1,129},{129,385},{385,257},{2... | collective-permute-start | bytes 983048 | tf_op jit(solution)/shard_map/ppermute | solution.py:163
  78.5 13.7 %collective-permute-start.2 = (f32[160,1024]{1,0:T(8,128)S(1)}, f32[160,1024]{1,0:T(8,128)}, u32[]{:S(2)}, u32[]{:S(2)}) collective-permute-start(f32[160,1024]{1,0:T(8,128)S(1)} %pad_maximum_fusion.refs_0_), channel_id=1, source_target_pairs={{0,96},{32,0},{64,32},{96,64},{1,97},{33,1},{65,33},{97,65},{2,98}... | collective-permute-start | bytes 1966088 | tf_op jit(solution)/shard_map/ppermute | solution.py:113
  81.9 14.8 %collective-permute-start.3 = (f32[160,1024]{1,0:T(8,128)}, f32[160,1024]{1,0:T(8,128)}, u32[]{:S(2)}, u32[]{:S(2)}) collective-permute-start(f32[160,1024]{1,0:T(8,128)} %collective-permute-done.1.refs_1_), channel_id=1, source_target_pairs={{0,32},{32,64},{64,96},{96,0},{1,33},{33,65},{65,97},{97,1},{2,34}... | collective-permute-start | bytes 1966088 | tf_op jit(solution)/shard_map/ppermute | solution.py:174
  84.4 29.1 %collective-permute-start.12 = (f32[160,1024]{1,0:T(8,128)S(1)}, f32[160,1024]{1,0:T(8,128)S(1)}, u32[]{:S(2)}, u32[]{:S(2)}) collective-permute-start(f32[160,1024]{1,0:T(8,128)S(1)} %constant_dynamic-update-slice_fusion.refs_0_), channel_id=1, source_target_pairs={{0,96},{32,0},{64,32},{96,64},{1,97},{33,1},{65,33},{97,65},{2,98}... | collective-permute-start | bytes 1966088 | tf_op jit(solution)/shard_map/ppermute | solution.py:113
  96.8 0.7 copy-start.1
  102.4 14.4 %collective-permute-start.8 = (f32[152,1280]{1,0:T(8,128)S(1)}, f32[152,1280]{1,0:T(8,128)S(1)}, u32[]{:S(2)}, u32[]{:S(2)}) collective-permute-start(f32[152,1280]{1,0:T(8,128)S(1)} %get-tuple-element.17), channel_id=1, source_target_pairs={{0,16},{16,0},{1,17},{17,1},{2,18},{18,2},{3,19},{19,3},{4,20},{20... | collective-permute-start | bytes 2334728 | tf_op jit(solution)/shard_map/ppermute | solution.py:199
  110.2 19.5 %collective-permute-start.11 = (f32[160,1024]{1,0:T(8,128)S(1)}, f32[160,1024]{1,0:T(8,128)S(1)}, u32[]{:S(2)}, u32[]{:S(2)}) collective-permute-start(f32[160,1024]{1,0:T(8,128)S(1)} %constant_dynamic-update-slice_fusion.refs_0_), channel_id=1, source_target_pairs={{0,32},{32,64},{64,96},{96,0},{1,33},{33,65},{65,97},{97,1},{2,34}... | collective-permute-start | bytes 1966088 | tf_op jit(solution)/shard_map/ppermute | solution.py:113
  113.5 17.9 %collective-permute-start.13 = (f32[160,1024]{1,0:T(8,128)S(1)}, f32[160,1024]{1,0:T(8,128)S(1)}, u32[]{:S(2)}, u32[]{:S(2)}) collective-permute-start(f32[160,1024]{1,0:T(8,128)S(1)} %collective-permute-done.12.refs_2_), channel_id=1, source_target_pairs={{0,96},{32,0},{64,32},{96,64},{1,97},{33,1},{65,33},{97,65},{2,98}... | collective-permute-start | bytes 1966088 | tf_op jit(solution)/shard_map/ppermute | solution.py:174
  131.5 4.7 %copy-start.4 = (s32[152,2]{0,1:T(2,128)S(1)}, s32[152,2]{0,1:T(2,128)}, u32[]{:S(2)}) copy-start(s32[152,2]{0,1:T(2,128)} %param.10) | copy-start | bytes 3652
  133.1 4.7 %collective-permute-start.14 = (f32[152,1024]{1,0:T(8,128)S(1)}, f32[152,1024]{1,0:T(8,128)S(1)}, u32[]{:S(2)}, u32[]{:S(2)}) collective-permute-start(f32[152,1024]{1,0:T(8,128)S(1)} %get-tuple-element.24), channel_id=1, source_target_pairs={{0,16},{16,0},{1,17},{17,1},{2,18},{18,2},{3,19},{19,3},{4,20},{20... | collective-permute-start | bytes 1867784 | tf_op jit(solution)/shard_map/ppermute | solution.py:214
